TPU v7x, 256 devices: a whole 4x4x8 slice. The times are simulated.
256 devices in a mesh: wave: 8 (over x_lo, y), slab: 32 (over x_hi, z, core).
Axes of the slice: x: 4 (x_hi: 2, x_lo: 2; x = x_hi * 2 + x_lo), y: 4, z: 8, core: 2. Of those that a mesh axis runs over, the one named last changes fastest.
Arguments:
- levels: int32 [2048, 2048], P('slab', 'wave'), may hold values from 0 to 15
- offsets: float32 [2048, 2048], P('slab', 'wave'), may hold values from -0.3 to 0.3
- targets: int32 [8, 64, 2], replicated, may hold values from 0 to 2047
- w_in: float32 [256], replicated, may hold values from -96 to 96
- b_in: float32 [256], replicated, may hold values from -87 to 87
- w_out: bfloat16 [256, 16], replicated, may hold values from -0.046875 to 0.046875
- b_out: float32 [16], replicated, may hold values from -2 to 2
Outputs:
- width_gradient: float32 [2048, 2048], P('slab', 'wave')
All inputs are finite; a program needn't handle non-finite values.
Results may differ from a plain program's by a relative error of at most 0.0039.
Values may be sent and summed in bfloat16 or wider, within the bound.
No kernel may reach another device: no remote copies, remote signals or barrier semaphores. Data moves between devices by JAX's collectives and lax.ppermute only.
A program may use at most 64 MiB of HBM per device.

v0:
```python
import math

import jax
import jax.numpy as jnp
from jax import lax
from jax.sharding import PartitionSpec as P

LEVELS = 16


def level_widths(levels, offsets):
    return 0.3 + levels.astype(jnp.float32) * (0.4 / (LEVELS - 1)) + offsets


def block_size(rows_count, cols_count):
    size_block = rows_count
    while size_block * cols_count > 32768 and size_block % 2 == 0:
        size_block = size_block // 2
    return size_block


def surrogate_rows(widths, w_in, b_in, w_out, b_out):
    rows_count, cols_count = widths.shape
    size_block = block_size(rows_count, cols_count)
    collected = jnp.zeros((w_out.shape[1], rows_count, cols_count), jnp.bfloat16)

    def surrogate_step_block(turn_index, gathered):
        pre_act = widths[..., None] * w_in + b_in
        hidden = (pre_act * jax.nn.sigmoid(pre_act)).astype(jnp.bfloat16)
        mixed_out = (
            jnp.einsum("rch,hj->jrc", hidden, w_out, preferred_element_type=jnp.float32)
            + b_out[:, None, None]
        )
        return mixed_out.astype(jnp.bfloat16)

    return lax.fori_loop(0, rows_count // size_block, surrogate_step_block, collected)


def slope_rows(widths, w_in, b_in, w_out, cotangent):
    rows_count, cols_count = widths.shape
    size_block = block_size(rows_count, cols_count)
    collected = jnp.zeros((rows_count, cols_count), jnp.float32)

    def slope_step_block(turn_index, gathered):
        pre_act = widths[..., None] * w_in + b_in
        sigmoid_value = jax.nn.sigmoid(pre_act)
        back_hidden = jnp.einsum(
            "jrc,hj->rch", cotangent, w_out, preferred_element_type=jnp.float32
        )
        act_slope = sigmoid_value * (1.0 + pre_act * (1.0 - sigmoid_value))
        rows_out = jnp.sum(back_hidden * act_slope * w_in, axis=-1)
        return rows_out

    return lax.fori_loop(0, rows_count // size_block, slope_step_block, collected)


def frequencies(length, first_index, total_len):
    index_all = first_index + jnp.arange(length, dtype=jnp.int32)
    signed_index = jnp.where(index_all < total_len // 2, index_all, index_all - total_len)
    return signed_index.astype(jnp.float32) * (2.0 * math.pi / total_len)


def transfer(wavelength, kx_rows, ky_cols, focal_length):
    wave_number = 2.0 * math.pi / wavelength
    kz_square = wave_number * wave_number - kx_rows[:, None] ** 2 - ky_cols[None, :] ** 2
    kz_root = jnp.sqrt(jnp.abs(kz_square))
    is_open = kz_square > 0.0
    phase_angle = jnp.where(is_open, focal_length * kz_root, 0.0)
    amplitude = jnp.where(is_open, 1.0, jnp.exp(-focal_length * kz_root))
    return (amplitude * jnp.cos(phase_angle), amplitude * jnp.sin(phase_angle))


def split_factor(length):
    factor = int(math.isqrt(length))
    while length % factor:
        factor = factor - 1
    return factor


def unit_table(rows_count, cols_count, modulus, direction):
    prod_index = (
        jnp.arange(rows_count, dtype=jnp.int32)[:, None]
        * jnp.arange(cols_count, dtype=jnp.int32)[None, :]
        % modulus
    )
    angle_value = prod_index.astype(jnp.float32) * (direction * 2.0 * math.pi / modulus)
    return (jnp.cos(angle_value), jnp.sin(angle_value))


def complex_einsum(spec, left_pair, right_pair):

    def real_dot(first_op, second_op):
        return jnp.einsum(
            spec,
            first_op,
            second_op,
            precision=lax.Precision.HIGHEST,
            preferred_element_type=jnp.float32,
        )

    return (
        real_dot(left_pair[0], right_pair[0]) - real_dot(left_pair[1], right_pair[1]),
        real_dot(left_pair[0], right_pair[1]) + real_dot(left_pair[1], right_pair[0]),
    )


def complex_mul(left_pair, right_pair):
    return (
        left_pair[0] * right_pair[0] - left_pair[1] * right_pair[1],
        left_pair[0] * right_pair[1] + left_pair[1] * right_pair[0],
    )


def transform_last(pair, direction):
    rows_count, length = pair[0].shape
    first_len = split_factor(length)
    second_len = length // first_len
    shaped = (
        pair[0].reshape(rows_count, first_len, second_len),
        pair[1].reshape(rows_count, first_len, second_len),
    )
    section_one = complex_einsum(
        "mab,ak->mkb", shaped, unit_table(first_len, first_len, first_len, direction)
    )
    twiddle = unit_table(first_len, second_len, length, direction)
    turned = complex_mul(section_one, (twiddle[0][None], twiddle[1][None]))
    section_two = complex_einsum(
        "mkb,bl->mlk", turned, unit_table(second_len, second_len, second_len, direction)
    )
    result = (
        section_two[0].reshape(rows_count, length),
        section_two[1].reshape(rows_count, length),
    )
    if direction > 0:
        result = (result[0] / length, result[1] / length)
    return result


def transform_first(pair, direction):
    length, cols_count = pair[0].shape
    first_len = split_factor(length)
    second_len = length // first_len
    shaped = (
        pair[0].reshape(first_len, second_len, cols_count),
        pair[1].reshape(first_len, second_len, cols_count),
    )
    section_one = complex_einsum(
        "abc,ak->kbc", shaped, unit_table(first_len, first_len, first_len, direction)
    )
    twiddle = unit_table(first_len, second_len, length, direction)
    turned = complex_mul(section_one, (twiddle[0][:, :, None], twiddle[1][:, :, None]))
    section_two = complex_einsum(
        "kbc,bl->lkc", turned, unit_table(second_len, second_len, second_len, direction)
    )
    result = (
        section_two[0].reshape(length, cols_count),
        section_two[1].reshape(length, cols_count),
    )
    if direction > 0:
        result = (result[0] / length, result[1] / length)
    return result


def propagate(spectrum_rows, wavelength, focal_length, conjugate):
    column_view = lax.all_to_all(spectrum_rows, "slab", split_axis=2, concat_axis=1, tiled=True)
    length = column_view.shape[1]
    block_cols = column_view.shape[2]
    freq_pair = transform_first((column_view[0], column_view[1]), -1.0)
    kx_all = frequencies(length, 0, length)
    ky_block = frequencies(block_cols, lax.axis_index("slab") * block_cols, length)
    kern_re, kern_im = transfer(wavelength, kx_all, ky_block, focal_length)
    if conjugate:
        kern_im = -kern_im
    filtered = complex_mul(freq_pair, (kern_re, kern_im))
    spatial = transform_first(filtered, 1.0)
    row_view = lax.all_to_all(jnp.stack(spatial), "slab", split_axis=1, concat_axis=2, tiled=True)
    return transform_last((row_view[0], row_view[1]), 1.0)


def local(levels, offsets, targets, w_in, b_in, w_out, b_out):
    rows_here = levels.shape[0]
    wave_count = lax.axis_size("wave")
    length = rows_here * lax.axis_size("slab")
    wave_index = lax.axis_index("wave")
    wavelength = 1.5 + wave_index.astype(jnp.float32) / (wave_count - 1)
    focal_length = float(length // 16)
    widths = level_widths(levels, offsets)
    all_trans = surrogate_rows(widths, w_in, b_in, w_out, b_out).reshape(
        2, wave_count, rows_here, widths.shape[1]
    )
    exchanged = lax.all_to_all(all_trans, "wave", split_axis=1, concat_axis=3, tiled=True)
    spectrum = jnp.stack(
        transform_last(
            (exchanged[0, 0].astype(jnp.float32), exchanged[1, 0].astype(jnp.float32)), -1.0
        )
    )
    field_re, field_im = propagate(spectrum, wavelength, focal_length, False)
    intensity = field_re * field_re + field_im * field_im
    own_targets = lax.dynamic_index_in_dim(targets, wave_index, 0, keepdims=False)
    local_rows = own_targets[:, 0] - lax.axis_index("slab") * rows_here
    inside = (local_rows >= 0) & (local_rows < rows_here)
    spot_map = (
        jnp.zeros((rows_here, length), jnp.float32)
        .at[jnp.clip(local_rows, 0, rows_here - 1), own_targets[:, 1]]
        .add(jnp.where(inside, float(length // 8), 0.0))
    )
    weight = (intensity - spot_map) / wave_count
    adj_spec = jnp.stack(transform_last((weight * field_re, weight * field_im), -1.0))
    back_re, back_im = propagate(adj_spec, wavelength, focal_length, True)
    cotangent = jnp.stack([back_re, back_im]).astype(jnp.bfloat16)
    returned = lax.all_to_all(
        cotangent.reshape(2, 1, rows_here, length), "wave", split_axis=3, concat_axis=1, tiled=True
    )
    return slope_rows(
        widths, w_in, b_in, w_out, returned.reshape(2 * wave_count, rows_here, widths.shape[1])
    )


def solution(mesh):
    placed = (P("slab", "wave"), P("slab", "wave"), P(), P(), P(), P(), P())
    return jax.shard_map(
        local, mesh=mesh, in_specs=placed, out_specs=P("slab", "wave"), check_vma=False
    )
```

profile of v0, /device:TPU:1, one launch (start us, length us, event | category | flops | bytes accessed | tf_op | source)
XLA Modules:
  0.0 423.5 jit_solution(10806735010497547705)
XLA Ops:
  0.9 5.2 %fusion.21 = bf16[2,8,64,256]{3,1,0,2:T(8,128)(2,1)S(1)} fusion(f32[256]{0:T(256)} %param.11, f32[256]{0:T(256)} %param.10, f32[64,256]{1,0:T(8,128)S(1)} %add_add_fusion, f32[16]{0:T(128)} %param.13, bf16[256,16]{0,1:T(8,128)(2,1)S(1)} %copy-done), kind=kOutput, calls=%fused_computation.66 | convolution fusion | flops 164102144 | bytes 600128 | tf_op jit(solution)/shard_map/while/body/eval_jaxpr/rch,hj->jrc/dot_general | solution.py:31
  7.3 6.1 %all-to-all-start = ((bf16[2,8,64,256]{3,0,2,1:T(2,128)(2,1)}), bf16[2,8,64,256]{3,0,2,1:T(2,128)(2,1)S(1)}, u32[]{:S(2)}, u32[]{:S(2)}) async-start(bf16[2,8,64,256]{3,0,2,1:T(2,128)(2,1)} %copy.286), calls=%async_computation | async-start | bytes 1048576 | tf_op jit(solution)/shard_map/all_to_all | solution.py:191
  13.5 7.6 %all-to-all-done = bf16[2,8,64,256]{3,0,2,1:T(2,128)(2,1)S(1)} async-done(((bf16[2,8,64,256]{3,0,2,1:T(2,128)(2,1)}), bf16[2,8,64,256]{3,0,2,1:T(2,128)(2,1)S(1)}, u32[]{:S(2)}, u32[]{:S(2)}) %all-to-all-start) | async-done | bytes 524320 | tf_op jit(solution)/shard_map/all_to_all | solution.py:191
  29.5 3.5 fusion.100
  33.0 3.5 fusion.14
  37.6 3.5 fusion.13
  41.9 7.6 %copy.476 = f32[2,64,2048]{1,0,2:T(2,128)S(1)} copy(f32[2,64,2048]{1,2,0:T(8,128)S(1)} %pad_maximum_fusion) | data formatting | bytes 2097152 | tf_op jit(solution)/shard_map/stack | solution.py:192
  52.6 13.5 %all-to-all-start.1 = ((f32[32,1,8192]{2,1,0:T(1,128)}), f32[32,1,8192]{2,1,0:T(1,128)S(1)}, u32[]{:S(2)}, u32[]{:S(2)}) async-start(f32[32,1,8192]{2,1,0:T(1,128)} %reshape.403), calls=%async_computation.1 | async-start | bytes 2097152 | tf_op jit(solution)/shard_map/all_to_all | solution.py:165
  66.7 27.2 %all-to-all-done.1 = f32[32,1,8192]{2,1,0:T(1,128)S(1)} async-done(((f32[32,1,8192]{2,1,0:T(1,128)}), f32[32,1,8192]{2,1,0:T(1,128)S(1)}, u32[]{:S(2)}, u32[]{:S(2)}) %all-to-all-start.1) | async-done | bytes 1048608 | tf_op jit(solution)/shard_map/all_to_all | solution.py:165
  116.9 4.8 %fusion.35 = (f32[32,64,64]{2,1,0:T(8,128)S(1)}, f32[32,64,64]{2,1,0:T(8,128)S(1)}) fusion(f32[64]{0:T(128)S(1)} %fusion.201, f32[32,64]{1,0:T(8,128)S(1)} %fusion.152, f32[32,64,64]{2,1,0:T(8,128)S(1)} %bitcast.366, f32[32,64,64]{2,1,0:T(8,128)S(1)} %bitcast.364), kind=kLoop, calls=%fused_computation.95 | loop fusion | flops 1966080 | bytes 2105600 | tf_op jit(solution)/shard_map/add | solution.py:110
  136.9 7.6 %copy.475 = f32[2,2048,64]{2,0,1:T(2,128)S(1)} copy(f32[2,2048,64]{2,1,0:T(8,128)S(1)} %pad_maximum_fusion.1) | data formatting | bytes 2097152 | tf_op jit(solution)/shard_map/stack | solution.py:176
  147.7 6.2 %all-to-all-start.2 = ((f32[32,1,8192]{2,1,0:T(1,128)}), f32[32,1,8192]{2,1,0:T(1,128)S(1)}, u32[]{:S(2)}, u32[]{:S(2)}) async-start(f32[32,1,8192]{2,1,0:T(1,128)} %reshape.405), calls=%async_computation.2 | async-start | bytes 2097152 | tf_op jit(solution)/shard_map/all_to_all | solution.py:176
  154.6 3.8 scatter_fusion
  158.4 23.2 %all-to-all-done.2 = f32[32,1,8192]{2,1,0:T(1,128)S(1)} async-done(((f32[32,1,8192]{2,1,0:T(1,128)}), f32[32,1,8192]{2,1,0:T(1,128)S(1)}, u32[]{:S(2)}, u32[]{:S(2)}) %all-to-all-start.2) | async-done | bytes 1048608 | tf_op jit(solution)/shard_map/all_to_all | solution.py:176
  181.6 4.5 %reduce.1 = f32[32,8192]{1,0:T(8,128)} reduce(f32[32,1,8192]{2,1,0:T(1,128)S(1)} %all-to-all-done.2, f32[]{:T(128)} %broadcast.1073), dimensions={1}, to_apply=%all_to_all.72.reduce_sub_computation | reduce | bytes 2097156 | tf_op jit(solution)/shard_map/all_to_all | solution.py:176
  198.8 3.5 fusion.76
  202.3 3.7 fusion.10
  221.1 3.7 fusion.72
  224.8 3.5 fusion.70
  228.3 3.5 fusion.6
  232.5 3.5 fusion.5
  236.8 8.0 %copy.474 = f32[2,64,2048]{1,0,2:T(2,128)S(1)} copy(f32[2,64,2048]{1,2,0:T(8,128)S(1)} %pad_maximum_fusion.2) | data formatting | bytes 2097152 | tf_op jit(solution)/shard_map/stack | solution.py:208
  247.0 33.8 %all_to_all.90 = f32[32,1,8192]{2,1,0:T(1,128)S(1)} all-to-all(f32[32,1,8192]{2,1,0:T(1,128)S(1)} %reshape.407), channel_id=1, replica_groups=mesh['wave'=8,'slab'=32] {'slab'}, dimensions={0} | all-to-all | bytes 2097152 | tf_op jit(solution)/shard_map/all_to_all | solution.py:165
  303.0 4.8 %fusion.33 = (f32[32,64,64]{2,1,0:T(8,128)S(1)}, f32[32,64,64]{2,1,0:T(8,128)S(1)}) fusion(f32[64]{0:T(128)S(1)} %fusion.201, f32[32,64]{1,0:T(8,128)S(1)} %fusion.152, f32[32,64,64]{2,1,0:T(8,128)S(1)} %bitcast.365, f32[32,64,64]{2,1,0:T(8,128)S(1)} %bitcast.363), kind=kLoop, calls=%fused_computation.89 | loop fusion | flops 2097152 | bytes 2105600 | tf_op jit(solution)/shard_map/add | solution.py:110
  323.3 7.6 %copy.473 = f32[2,2048,64]{2,0,1:T(2,128)S(1)} copy(f32[2,2048,64]{2,1,0:T(8,128)S(1)} %pad_maximum_fusion.3) | data formatting | bytes 2097152 | tf_op jit(solution)/shard_map/stack | solution.py:176
  333.1 33.8 %all_to_all.91 = f32[32,1,8192]{2,1,0:T(1,128)S(1)} all-to-all(f32[32,1,8192]{2,1,0:T(1,128)S(1)} %reshape.409), channel_id=1, replica_groups=mesh['wave'=8,'slab'=32] {'slab'}, dimensions={0} | all-to-all | bytes 2097152 | tf_op jit(solution)/shard_map/all_to_all | solution.py:176
  377.6 3.7 fusion.48
  381.3 3.5 fusion.46
  384.8 3.5 fusion.20
  392.8 8.9 %copy.477 = bf16[2,1,64,2048]{2,0,1,3:T(2,128)(2,1)S(1)} copy(bf16[2,1,64,2048]{2,3,1,0:T(8,128)(2,1)S(1)} %pad_maximum_fusion.4) | data formatting | bytes 1048576 | tf_op jit(solution)/shard_map/stack | solution.py:210
  402.5 9.9 %all_to_all.92 = bf16[8,2,16384]{2,1,0:T(2,128)(2,1)S(1)} all-to-all(bf16[8,2,16384]{2,1,0:T(2,128)(2,1)S(1)} %reshape.411), channel_id=1, replica_groups=mesh['wave'=8,'slab'=32] {'wave'}, dimensions={0} | all-to-all | bytes 1048576 | tf_op jit(solution)/shard_map/all_to_all | solution.py:211
  413.8 9.4 %multiply_reduce_fusion = f32[64,256]{1,0:T(8,128)} fusion(f32[256]{0:T(256)S(1)} %copy-done.1, f32[256]{0:T(256)S(1)} %copy-done.2, f32[64,256]{1,0:T(8,128)S(1)} %add_add_fusion, bf16[256,16]{0,1:T(8,128)(2,1)S(1)} %copy-done, bf16[2,1,64,8,256]{4,3,2,0,1:T(8,128)(2,1)S(1)} %copy.375), kind=kOutput, calls=%fused_computation.1 | convolution fusion | flops 184532992 | bytes 665600 | tf_op jit(solution)/shard_map/while/body/eval_jaxpr/jrc,hj->rch/dot_general | solution.py:47
  (122 shorter events, 145.9 us)
Async XLA Ops:
  0.0 0.9 copy-start
  7.3 13.8 %all-to-all-start = ((bf16[2,8,64,256]{3,0,2,1:T(2,128)(2,1)}), bf16[2,8,64,256]{3,0,2,1:T(2,128)(2,1)S(1)}, u32[]{:S(2)}, u32[]{:S(2)}) async-start(bf16[2,8,64,256]{3,0,2,1:T(2,128)(2,1)} %copy.286), calls=%async_computation | async-start | bytes 1048576 | tf_op jit(solution)/shard_map/all_to_all | solution.py:191
  52.6 41.3 %all-to-all-start.1 = ((f32[32,1,8192]{2,1,0:T(1,128)}), f32[32,1,8192]{2,1,0:T(1,128)S(1)}, u32[]{:S(2)}, u32[]{:S(2)}) async-start(f32[32,1,8192]{2,1,0:T(1,128)} %reshape.403), calls=%async_computation.1 | async-start | bytes 2097152 | tf_op jit(solution)/shard_map/all_to_all | solution.py:165
  147.7 34.0 %all-to-all-start.2 = ((f32[32,1,8192]{2,1,0:T(1,128)}), f32[32,1,8192]{2,1,0:T(1,128)S(1)}, u32[]{:S(2)}, u32[]{:S(2)}) async-start(f32[32,1,8192]{2,1,0:T(1,128)} %reshape.405), calls=%async_computation.2 | async-start | bytes 2097152 | tf_op jit(solution)/shard_map/all_to_all | solution.py:176
  402.5 11.3 %copy-start.1 = (f32[256]{0:T(256)S(1)}, f32[256]{0:T(256)}, u32[]{:S(2)}) copy-start(f32[256]{0:T(256)} %param.11) | copy-start | bytes 3076
  402.5 11.3 %copy-start.2 = (f32[256]{0:T(256)S(1)}, f32[256]{0:T(256)}, u32[]{:S(2)}) copy-start(f32[256]{0:T(256)} %param.10) | copy-start | bytes 3076
where the time goes:
time: 432 us; the launch traced here: 424 us
  matrix products  138 us (32%)
  local copies, waits for them, and re-layouts  91.9 us (21%)
  blocking collectives  77.4 us (18%)
  waiting for transfers between devices  58 us (13%)
  other arithmetic  30.8 us (7%)
  starting transfers between devices  25.8 us (6%)
    dot_general x64, matrix products, real_dot(): jnp.einsum(spec, first_op, second_op, precision=lax.Precision.HIGHEST, pr...  124 us
    all_to_all x1, blocking collectives, propagate(): lax.all_to_all(jnp.stack(spatial), 'slab', split_axis=1, concat_axis=2, t...  33.8 us
    all_to_all x1, blocking collectives, propagate(): lax.all_to_all(spectrum_rows, 'slab', split_axis=2, concat_axis=1, tiled=...  33.8 us
    all_to_all x1, waiting for transfers between devices, propagate(): lax.all_to_all(spectrum_rows, 'slab', split_axis=2, concat_axis=1, tiled=...  27.2 us
    all_to_all x1, waiting for transfers between devices, propagate(): lax.all_to_all(jnp.stack(spatial), 'slab', split_axis=1, concat_axis=2, t...  23.2 us
    unnamed x16, local copies, waits for them, and re-layouts  22.6 us
    another operation x2, local copies, waits for them, and re-layouts, propagate(): jnp.stack(spatial)  15.2 us
    all_to_all x1, starting transfers between devices, propagate(): lax.all_to_all(spectrum_rows, 'slab', split_axis=2, concat_axis=1, tiled=...  13.5 us
  transfers between devices with their start and end apart: 3, of which 3 were waited for; matrix products, arithmetic and copies ran while one was open for 1% of the time, Pallas kernels for 0%

commit v1 on v0

v1 whole, which is shorter than its diff:
```python
import math

import jax
import jax.numpy as jnp
import ml_dtypes
import numpy as np
from jax import lax
from jax.experimental import pallas as pl
from jax.experimental.pallas import tpu as pltpu
from jax.sharding import Mesh, PartitionSpec as P


LEVELS = 16
WAVES = 8
SIDE = 2048
FIRST = 32
SECOND = 64
LANES = 2 * SECOND
SLAB = ("xh", "z", "c")
WAVE = ("xl", "y")
PLANE = ("xl", "y", "xh", "c")
VMEM_LIMIT = 48 * 2**20


def split_np(table):
    high = table.astype(np.float32).astype(ml_dtypes.bfloat16)
    low = (table - high.astype(np.float64)).astype(np.float32).astype(ml_dtypes.bfloat16)
    return high, low


def row_tables(direction):
    angle = direction * 2.0 * math.pi / SECOND * (np.arange(SECOND)[:, None] * np.arange(SECOND)[None, :] % SECOND)
    scale = 1.0 if direction < 0 else 1.0 / SIDE
    cos, sin = np.cos(angle) * scale, np.sin(angle) * scale
    high, low = split_np(np.block([[cos, sin], [-sin, cos]]))
    return np.block([[high, low], [high, np.zeros_like(low)]])


def row_twiddles():
    angle = -2.0 * math.pi / SIDE * (np.arange(FIRST)[:, None] * np.arange(SECOND)[None, :])
    cos, sin = np.cos(angle), np.sin(angle)
    return np.stack([np.concatenate([cos, cos], 1), np.concatenate([-sin, sin], 1)], 1).astype(np.float32)


def col_tables(direction):
    place = np.arange(SECOND)
    freq = np.arange(FIRST)[:, None] + FIRST * place[None, :]
    index = freq[:, :, None] * place[None, None, :] % SIDE
    if direction > 0:
        index = np.transpose(index, (0, 2, 1))
    scale = 1.0 if direction < 0 else 1.0 / SIDE
    angle = direction * 2.0 * math.pi / SIDE * index
    table = np.concatenate([np.cos(angle) * scale, np.sin(angle) * scale], 2)
    high, low = split_np(table)
    if direction > 0:
        return np.concatenate([high, low], 1)
    return np.concatenate(
        [np.concatenate([high, high], 2), np.concatenate([low, np.zeros_like(low)], 2)], 1
    )


def lane_signs():
    lane = lax.broadcasted_iota(jnp.int32, (1, LANES), 1)
    return jnp.where(lane < SECOND, -1.0, 1.0).astype(jnp.float32)


def swap(x):
    return pltpu.roll(x, SECOND, x.ndim - 1)


def dft32(parts, direction, signs):
    count = len(parts)
    if count == 1:
        return parts
    even = dft32(parts[0::2], direction, signs)
    odd = dft32(parts[1::2], direction, signs)
    half = count // 2
    lower, upper = [], []
    for k in range(half):
        if k == 0:
            turned = odd[k]
        elif 2 * k == half:
            turned = swap(odd[k]) * (direction * signs)
        else:
            angle = direction * 2.0 * math.pi * k / count
            turned = odd[k] * math.cos(angle) + swap(odd[k]) * (signs * math.sin(angle))
        lower.append(even[k] + turned)
        upper.append(even[k] - turned)
    return lower + upper


def split_pair(x):
    high = x.astype(jnp.bfloat16)
    return high, (x - high.astype(jnp.float32)).astype(jnp.bfloat16)


def matmul(left, right):
    return jnp.dot(left, right, preferred_element_type=jnp.float32)


def col_forward_step(y_ref, w_ref, out_ref, signs, k):
    part = y_ref[k]
    high, low = split_pair(jnp.concatenate([part, swap(part) * signs], 0))
    both = matmul(w_ref[k], jnp.concatenate([high, low], 0))
    out_ref[k] = (both[:SECOND] + both[SECOND:]).astype(jnp.bfloat16)


def col_inverse_step(x_ref, v_ref, y_ref, signs, k):
    part = x_ref[k].astype(jnp.float32)
    data = jnp.concatenate([part, swap(part) * signs], 0).astype(jnp.bfloat16)
    both = matmul(v_ref[k], data)
    y_ref[k] = both[:SECOND] + both[SECOND:]


def col_first_kernel(x_ref, c_ref, w_ref, out_ref, y_ref):
    signs = lane_signs()
    mean = c_ref[0:1, :]
    for g in range(0, SECOND, 16):
        block = [x_ref[a, g : g + 16, :].astype(jnp.float32) - mean for a in range(FIRST)]
        for h in (0, 8):
            for k, part in enumerate(dft32([b[h : h + 8] for b in block], -1.0, signs)):
                y_ref[k, g + h : g + h + 8, :] = part
    for k in range(FIRST):
        col_forward_step(y_ref, w_ref, out_ref, signs, k)


def col_middle_kernel(x_ref, c_ref, s_ref, v_ref, w_ref, out_ref, y_ref):
    signs = lane_signs()
    back = c_ref[1:2, :]
    mean = c_ref[2:3, :]
    for k in range(FIRST):
        col_inverse_step(x_ref, v_ref, y_ref, signs, k)
    for g in range(0, SECOND, 8):
        rows = slice(g, g + 8)
        field = dft32([y_ref[k, rows, :] for k in range(FIRST)], 1.0, signs)
        adjoint = []
        for a in range(FIRST):
            value = field[a] + back
            square = value * value
            weight = (square + swap(square) - s_ref[a, rows, :]) * (1.0 / WAVES)
            adjoint.append(weight * value - mean)
        for k, part in enumerate(dft32(adjoint, -1.0, signs)):
            y_ref[k, rows, :] = part
    for k in range(FIRST):
        col_forward_step(y_ref, w_ref, out_ref, signs, k)


def col_last_kernel(x_ref, c_ref, v_ref, out_ref, y_ref):
    signs = lane_signs()
    back = c_ref[3:4, :]
    for k in range(FIRST):
        col_inverse_step(x_ref, v_ref, y_ref, signs, k)
    for g in range(0, SECOND, 16):
        halves = []
        for h in (0, 8):
            halves.append(dft32([y_ref[k, g + h : g + h + 8, :] for k in range(FIRST)], 1.0, signs))
        for a in range(FIRST):
            whole = jnp.concatenate([halves[0][a], halves[1][a]], 0) + back
            out_ref[a, g : g + 16, :] = whole.astype(jnp.bfloat16)


def row_kernel(x_ref, kr_ref, ki_ref, t_ref, w_ref, v_ref, out_ref, y_ref):
    signs = lane_signs()
    for g in range(0, SECOND, 16):
        block = [x_ref[a, g : g + 16, :].astype(jnp.float32) for a in range(FIRST)]
        for h in (0, 8):
            for k, part in enumerate(dft32([b[h : h + 8] for b in block], -1.0, signs)):
                y_ref[k, g + h : g + h + 8, :] = part * t_ref[k, 0:1, :] + swap(part) * t_ref[k, 1:2, :]
    step = 4
    rows = step * SECOND
    for k in range(0, FIRST, step):
        high, low = split_pair(y_ref[k : k + step].reshape(rows, LANES))
        both = matmul(jnp.concatenate([high, low], 1), w_ref[...])
        freq = both[:, :LANES] + both[:, LANES:]
        kr = kr_ref[k : k + step].reshape(rows, LANES)
        ki = ki_ref[k : k + step].reshape(rows, LANES)
        high, low = split_pair(freq * kr + swap(freq) * ki)
        both = matmul(jnp.concatenate([high, low], 1), v_ref[...])
        place = both[:, :LANES] + both[:, LANES:]
        turned = swap(place)
        for i in range(step):
            part = slice(i * SECOND, (i + 1) * SECOND)
            y_ref[k + i] = place[part] * t_ref[k + i, 0:1, :] - turned[part] * t_ref[k + i, 1:2, :]
    for g in range(0, SECOND, 16):
        halves = []
        for h in (0, 8):
            halves.append(dft32([y_ref[k, g + h : g + h + 8, :] for k in range(FIRST)], 1.0, signs))
        for a in range(FIRST):
            out_ref[a, g : g + 16, :] = jnp.concatenate([halves[0][a], halves[1][a]], 0).astype(jnp.bfloat16)


def pack_kernel(x_ref, out_ref):
    lane = lax.broadcasted_iota(jnp.int32, (1, LANES), 1)
    left = lane < SECOND
    for w in range(WAVES):
        for tile in range(2):
            real = x_ref[w, :, tile * LANES : (tile + 1) * LANES].astype(jnp.float32)
            imag = x_ref[WAVES + w, :, tile * LANES : (tile + 1) * LANES].astype(jnp.float32)
            place = tile * 2 * WAVES + w * 2
            out_ref[place] = jnp.where(left, real, swap(imag)).astype(out_ref.dtype)
            out_ref[place + 1] = jnp.where(left, swap(real), imag).astype(out_ref.dtype)


def combine_kernel(x_ref, d_ref, out_ref):
    lane = lax.broadcasted_iota(jnp.int32, (1, LANES), 1)
    left = lane < SECOND
    for tile in range(2):
        sums = []
        for core in range(2):
            total = None
            for w in range(WAVES):
                place = tile * 2 * WAVES + w * 2 + core
                term = x_ref[place].astype(jnp.float32) * d_ref[place]
                total = term if total is None else total + term
            sums.append(total + swap(total))
        out_ref[:, tile * LANES : (tile + 1) * LANES] = jnp.where(left, sums[0], sums[1])


def call(kernel, out_shape, *args, scratch=True, flops=10**8, name=None):
    size = sum(a.size * a.dtype.itemsize for a in args) + math.prod(out_shape.shape) * out_shape.dtype.itemsize
    return pl.pallas_call(
        kernel,
        out_shape=out_shape,
        scratch_shapes=[pltpu.VMEM((FIRST, SECOND, LANES), jnp.float32)] if scratch else [],
        compiler_params=pltpu.CompilerParams(vmem_limit_bytes=VMEM_LIMIT),
        cost_estimate=pl.CostEstimate(flops=flops, bytes_accessed=size, transcendentals=0),
        name=name,
    )(*args)


def level_widths(levels, offsets):
    return 0.3 + levels.astype(jnp.float32) * (0.4 / (LEVELS - 1)) + offsets


def surrogate_rows(widths, w_in, b_in, w_out, b_out):
    pre_act = widths[..., None] * w_in + b_in
    hidden = (pre_act * jax.nn.sigmoid(pre_act)).astype(jnp.bfloat16)
    mixed_out = (
        jnp.einsum("rch,hj->jrc", hidden, w_out, preferred_element_type=jnp.float32) + b_out[:, None, None]
    )
    return mixed_out.astype(jnp.bfloat16)


def slope_rows(widths, w_in, b_in, w_out):
    pre_act = widths[..., None] * w_in + b_in
    gate = jax.nn.sigmoid(pre_act)
    slope = gate * (1.0 + pre_act * (1.0 - gate)) * w_in
    return jnp.einsum("rch,hj->jrc", slope.astype(jnp.bfloat16), w_out, preferred_element_type=jnp.float32)


def signed_kappa(index):
    signed = jnp.where(index < SIDE // 2, index, index - SIDE)
    return signed.astype(jnp.float32) * (2.0 * math.pi / SIDE)


def transfer(wavelength, kx, ky, focal_length):
    wave_number = 2.0 * math.pi / wavelength
    kz_square = wave_number * wave_number - kx**2 - ky**2
    kz_root = jnp.sqrt(jnp.abs(kz_square))
    is_open = kz_square > 0.0
    phase_angle = jnp.where(is_open, focal_length * kz_root, 0.0)
    amplitude = jnp.where(is_open, 1.0, jnp.exp(-focal_length * kz_root))
    return (amplitude * jnp.cos(phase_angle), amplitude * jnp.sin(phase_angle))


def usual_transmission(w_in, b_in, w_out, b_out):
    nodes, weights = np.polynomial.hermite_e.hermegauss(8)
    weights = weights / weights.sum()
    shifts = np.clip(0.1 * nodes, -0.3, 0.3)
    places = (0.3 + 0.4 * np.arange(LEVELS)[:, None] / (LEVELS - 1) + shifts[None, :]).reshape(-1)
    shares = np.tile(weights / LEVELS, LEVELS).astype(np.float32)
    pre_act = places.astype(np.float32)[:, None] * w_in[None, :] + b_in[None, :]
    hidden = pre_act * jax.nn.sigmoid(pre_act)
    values = jnp.dot(hidden, w_out.astype(jnp.float32)) + b_out
    mean = jnp.sum(values * shares[:, None], 0)
    spread = jnp.sum((values - mean) ** 2 * shares[:, None], 0)
    return mean, spread


def lanes_pair(real, imag):
    return jnp.concatenate([jnp.full((1, SECOND), real), jnp.full((1, SECOND), imag)], 1)


def local(levels, offsets, targets, w_in, b_in, w_out, b_out):
    block = (FIRST, SECOND, LANES)
    packed16 = jax.ShapeDtypeStruct(block, jnp.bfloat16)
    packed32 = jax.ShapeDtypeStruct(block, jnp.float32)
    wave_index = lax.axis_index("z")
    plane_index = lax.axis_index(PLANE)
    wavelength = 1.5 + wave_index.astype(jnp.float32) / (WAVES - 1)
    focal_length = float(SIDE // 16)
    spot_level = float(SIDE // 8)
    col_forward = jnp.asarray(col_tables(-1.0))
    col_inverse = jnp.asarray(col_tables(1.0))
    row_forward = jnp.asarray(row_tables(-1.0))
    row_inverse = jnp.asarray(row_tables(1.0))
    twiddles = jnp.asarray(row_twiddles())

    widths = level_widths(levels, offsets)
    trans = surrogate_rows(widths, w_in, b_in, w_out, b_out)
    sent = call(pack_kernel, packed16, trans, scratch=False, name="pack")
    cols = lax.all_to_all(sent, SLAB, 0, 0, tiled=True)

    mean, spread = usual_transmission(w_in, b_in, w_out, b_out)
    mean_re = lax.dynamic_index_in_dim(mean, wave_index, 0, keepdims=False)
    mean_im = lax.dynamic_index_in_dim(mean, wave_index + WAVES, 0, keepdims=False)
    noise = lax.dynamic_index_in_dim(spread, wave_index, 0, keepdims=False) + lax.dynamic_index_in_dim(
        spread, wave_index + WAVES, 0, keepdims=False
    )
    zero = jnp.zeros((), jnp.float32)
    dc_re, dc_im = transfer(wavelength, zero, zero, focal_length)
    field_re = mean_re * dc_re - mean_im * dc_im
    field_im = mean_re * dc_im + mean_im * dc_re
    spots_mean = spot_level * targets.shape[1] / (SIDE * SIDE)
    gain = (field_re * field_re + field_im * field_im + 2.0 * noise - spots_mean) / WAVES
    adj_re = gain * field_re
    adj_im = gain * field_im
    back_re = adj_re * dc_re + adj_im * dc_im
    back_im = adj_im * dc_re - adj_re * dc_im
    consts = jnp.concatenate(
        [
            lanes_pair(mean_re, mean_im),
            lanes_pair(field_re, field_im),
            lanes_pair(adj_re, adj_im),
            lanes_pair(back_re, back_im),
            jnp.zeros((4, LANES), jnp.float32),
        ],
        0,
    )

    second = jnp.arange(SECOND, dtype=jnp.int32)
    kx = signed_kappa(plane_index + FIRST * second)
    ky = signed_kappa(jnp.arange(FIRST, dtype=jnp.int32)[:, None] + FIRST * second[None, :])
    kern_re, kern_im = transfer(wavelength, kx[None, :, None], ky[:, None, :], focal_length)
    kr = jnp.concatenate([kern_re, kern_re], 2)
    ki = jnp.concatenate([-kern_im, kern_im], 2)
    ki_conj = -ki

    own_targets = lax.dynamic_index_in_dim(targets, wave_index, 0, keepdims=False)
    row_hit = (own_targets[:, 0][None, :] == jnp.arange(SIDE, dtype=jnp.int32)[:, None]).astype(jnp.bfloat16)
    lane_cols = plane_index * SECOND + jnp.arange(LANES, dtype=jnp.int32) % SECOND
    col_hit = (own_targets[:, 1][:, None] == lane_cols[None, :]).astype(jnp.bfloat16)
    spots = (spot_level * jnp.dot(row_hit, col_hit, preferred_element_type=jnp.float32)).reshape(block)

    slopes = call(pack_kernel, packed32, slope_rows(widths, w_in, b_in, w_out), scratch=False, name="pack_slopes")

    def exchange(x):
        return lax.all_to_all(x, PLANE, 0, 0, tiled=True)

    rows = exchange(call(col_first_kernel, packed16, cols, consts, col_forward, name="col_first"))
    rows = call(row_kernel, packed16, rows, kr, ki, twiddles, row_forward, row_inverse, name="row_one")
    cols = exchange(rows)
    cols = call(col_middle_kernel, packed16, cols, consts, spots, col_inverse, col_forward, name="col_middle")
    rows = exchange(cols)
    rows = call(row_kernel, packed16, rows, kr, ki_conj, twiddles, row_forward, row_inverse, name="row_two")
    cols = exchange(rows)
    cotangent = call(col_last_kernel, packed16, cols, consts, col_inverse, name="col_last")
    returned = lax.all_to_all(cotangent, SLAB, 0, 0, tiled=True)
    return call(
        combine_kernel, jax.ShapeDtypeStruct(levels.shape, jnp.float32), returned, slopes, scratch=False, name="combine"
    )


def solution(mesh):
    fine = Mesh(mesh.devices.reshape(2, 4, 2, 8, 2), ("xl", "y", "xh", "z", "c"))
    placed = (P(SLAB, WAVE), P(SLAB, WAVE), P(), P(), P(), P(), P())
    return jax.shard_map(local, mesh=fine, in_specs=placed, out_specs=P(SLAB, WAVE), check_vma=False)
```

time: 432 us -> 154 us (0.36); the launches traced: 424 us -> 154 us
  matrix products: 138 us -> 13.3 us
  local copies, waits for them, and re-layouts: 91.9 us -> 7.82 us
  blocking collectives: 77.4 us -> 30.2 us
  Pallas kernels: 0 us -> 25 us
  other arithmetic: 30.8 us -> 7.97 us
  waiting for transfers between devices: 58 us -> 36.7 us
    dot_general x66 -> x4, matrix products: 138 us -> 13.3 us  [the longest x1 6.44 us: slope_rows(): jnp.einsum('rch,hj->jrc', slope.astype(jnp.bfloat16), w_out, preferred_el...]
    all_to_all x3 -> x2, blocking collectives: 77.4 us -> 30.2 us  [exchange(): return lax.all_to_all(x, PLANE, 0, 0, tiled=True)]
    another operation x5 -> x0, local copies, waits for them, and re-layouts: 39.7 us -> none  [the longest x2 15.2 us: propagate(): jnp.stack(spatial)]
    pallas_call x0 -> x8, Pallas kernels: none -> 25 us  [call(): pl.pallas_call(kernel, out_shape=out_shape, scratch_shapes=[pltpu.VMEM((F...]
    all_to_all x3 -> x4, waiting for transfers between devices: 58 us -> 36.7 us  [the longest x2 15.4 us: exchange(): return lax.all_to_all(x, PLANE, 0, 0, tiled=True)]
    unnamed x16 -> x30, local copies, waits for them, and re-layouts: 22.6 us -> 4.53 us
    all_to_all x4 -> x0, other arithmetic: 14.6 us -> none  [the longest x2 7.86 us: propagate(): lax.all_to_all(jnp.stack(spatial), 'slab', split_axis=1, concat_axis=2, t...]
    all_to_all x6 -> x0, local copies, waits for them, and re-layouts: 9.81 us -> none  [the longest x3 6.67 us: propagate(): lax.all_to_all(spectrum_rows, 'slab', split_axis=2, concat_axis=1, tiled=...]
  transfers between devices with their start and end apart: 3 -> 4, of which waited for: 3 -> 4; matrix products, arithmetic and copies ran while one was open for 1% -> 12% of each run, Pallas kernels for 0% -> 0%
where the time goes in v1:
time: 154 us
  waiting for transfers between devices  36.7 us (24%)
  blocking collectives  30.2 us (20%)
  starting transfers between devices  28 us (18%)
  Pallas kernels  25 us (16%)
  matrix products  13.3 us (9%)
  other arithmetic  7.97 us (5%)
  local copies, waits for them, and re-layouts  7.82 us (5%)
  between operations  4.53 us (3%)
    all_to_all x2, blocking collectives, exchange(): return lax.all_to_all(x, PLANE, 0, 0, tiled=True)  30.2 us
    pallas_call x8, Pallas kernels, call(): pl.pallas_call(kernel, out_shape=out_shape, scratch_shapes=[pltpu.VMEM((F...  25 us
    all_to_all x2, waiting for transfers between devices, exchange(): return lax.all_to_all(x, PLANE, 0, 0, tiled=True)  15.4 us
    all_to_all x1, starting transfers between devices, local(): cols = lax.all_to_all(sent, SLAB, 0, 0, tiled=True)  12.6 us
    all_to_all x2, starting transfers between devices, exchange(): return lax.all_to_all(x, PLANE, 0, 0, tiled=True)  11.5 us
    all_to_all x1, waiting for transfers between devices, local(): returned = lax.all_to_all(cotangent, SLAB, 0, 0, tiled=True)  10.8 us
    all_to_all x1, waiting for transfers between devices, local(): cols = lax.all_to_all(sent, SLAB, 0, 0, tiled=True)  10.5 us
    dot_general x1, matrix products, slope_rows(): jnp.einsum('rch,hj->jrc', slope.astype(jnp.bfloat16), w_out, preferred_el...  6.44 us
  transfers between devices with their start and end apart: 4, of which 4 were waited for; matrix products, arithmetic and copies ran while one was open for 12% of the time, Pallas kernels for 0%

profile of v1, /device:TPU:1, one launch (start us, length us, event | category | flops | bytes accessed | tf_op | source)
XLA Modules:
  0.0 153.5 jit_solution(13273763229758948691)
XLA Ops:
  0.0 0.9 add_add_fusion
  0.9 5.2 %fusion = f32[64,256,16]{1,2,0:T(8,128)S(1)} fusion(f32[256]{0:T(256)} %param.19, f32[256]{0:T(256)} %param.18, f32[64,256]{1,0:T(8,128)S(1)} %add_add_fusion, bf16[256,16]{0,1:T(8,128)(2,1)S(1)} %copy-done), kind=kOutput, calls=%fused_computation.4 | convolution fusion | flops 163577856 | bytes 1124352 | tf_op jit(solution)/shard_map/rch,hj->jrc/dot_general | solution.py:239
  6.2 0.6 fusion.13.x_ref
  6.8 1.0 pack.1
  7.9 12.6 %all-to-all-start = ((bf16[32,64,128]{2,1,0:T(8,128)(2,1)}), bf16[32,64,128]{2,1,0:T(8,128)(2,1)S(1)}, u32[]{:S(2)}, u32[]{:S(2)}) async-start(bf16[32,64,128]{2,1,0:T(8,128)(2,1)} %pack.1), calls=%async_computation | async-start | bytes 1048576 | tf_op jit(solution)/shard_map/all_to_all | solution.py:302
  21.3 0.7 fusion.44
  26.6 0.7 pad_bitcast_fusion.3
  27.3 0.7 dynamic-slice_bitcast_fusion
  28.0 10.5 %all-to-all-done.x_ref = bf16[32,64,128]{2,1,0:T(8,128)(2,1)S(1)} async-done(((bf16[32,64,128]{2,1,0:T(8,128)(2,1)}), bf16[32,64,128]{2,1,0:T(8,128)(2,1)S(1)}, u32[]{:S(2)}, u32[]{:S(2)}) %all-to-all-start) | async-done | bytes 524320 | tf_op jit(solution)/shard_map/all_to_all | solution.py:302
  38.5 2.2 %col_first.1 = bf16[32,64,128]{2,1,0:T(8,128)(2,1)} custom-call(bf16[32,64,128]{2,1,0:T(8,128)(2,1)S(1)} %all-to-all-done.x_ref, f32[8,128]{1,0:T(8,128)S(1)} %concatenate.37.c_ref, bf16[32,128,256]{2,1,0:T(8,128)(2,1)S(1)} %copy-done.1), custom_call_target="tpu_custom_call" | custom-call | flops 100000000 | bytes 3149824 | tf_op jit(solution)/shard_map/col_first/pallas_call | solution.py:221
  40.7 6.8 %all-to-all-start.1 = ((bf16[32,64,128]{2,1,0:T(8,128)(2,1)}), bf16[32,64,128]{2,1,0:T(8,128)(2,1)}, u32[]{:S(2)}, u32[]{:S(2)}) async-start(bf16[32,64,128]{2,1,0:T(8,128)(2,1)} %col_first.1), calls=%async_computation.1 | async-start | bytes 1048576 | tf_op jit(solution)/shard_map/all_to_all | solution.py:348
  47.6 4.3 %fusion.15 = (f32[32,64,64]{2,1,0:T(8,128)S(1)}, f32[32,64,64]{2,1,0:T(8,128)S(1)}, f32[32,64,64]{2,1,0:T(8,128)S(1)}) fusion(f32[32,64]{1,0:T(8,128)S(1)} %fusion.30, f32[64]{0:T(128)S(1)} %fusion.39), kind=kLoop, calls=%fused_computation.28 | loop fusion | flops 1310720 | bytes 1581312 | tf_op jit(solution)/shard_map/neg | solution.py:336
  51.9 1.9 %fusion.43 = (f32[32,64,128]{2,1,0:T(8,128)}, f32[32,64,128]{2,1,0:T(8,128)}, f32[32,64,128]{2,1,0:T(8,128)S(1)}) fusion(f32[32,64,64]{2,1,0:T(8,128)S(1)} %get-tuple-element.8, f32[32,64,64]{2,1,0:T(8,128)S(1)} %get-tuple-element.7, f32[32,64,64]{2,1,0:T(8,128)S(1)} %get-tuple-element.9), kind=kLoop, calls=%fused_computation.70 | loop fusion | flops 786432 | bytes 4718592 | tf_op jit(solution)/shard_map/neg | solution.py:337
  53.9 5.2 %all-to-all-done.1.x_ref = bf16[32,64,128]{2,1,0:T(8,128)(2,1)} async-done(((bf16[32,64,128]{2,1,0:T(8,128)(2,1)}), bf16[32,64,128]{2,1,0:T(8,128)(2,1)}, u32[]{:S(2)}, u32[]{:S(2)}) %all-to-all-start.1) | async-done | bytes 524320 | tf_op jit(solution)/shard_map/all_to_all | solution.py:348
  59.1 1.2 copy-done.4
  60.3 8.0 %row_one.1 = bf16[32,64,128]{2,1,0:T(8,128)(2,1)S(1)} custom-call(bf16[32,64,128]{2,1,0:T(8,128)(2,1)} %all-to-all-done.1.x_ref, f32[32,64,128]{2,1,0:T(8,128)S(1)} %get-tuple-element.20.kr_ref, f32[32,64,128]{2,1,0:T(8,128)S(1)} %copy-done.4, f32[32,2,128]{2,1,0:T(2,128)S(1)} %copy-done.9, bf16[256,256]{1,0:T(8,128)(2,1)S(1)} %copy-done.7, ...), custom_call_target="tpu_custom_call" | custom-call | flops 100000000 | bytes 3440640 | tf_op jit(solution)/shard_map/row_one/pallas_call | solution.py:221
  68.3 0.8 copy-done.6
  69.1 4.6 %all-to-all-start.2 = ((bf16[32,64,128]{2,1,0:T(8,128)(2,1)}), bf16[32,64,128]{2,1,0:T(8,128)(2,1)}, u32[]{:S(2)}, u32[]{:S(2)}) async-start(bf16[32,64,128]{2,1,0:T(8,128)(2,1)} %copy-done.6), calls=%async_computation.2 | async-start | bytes 1048576 | tf_op jit(solution)/shard_map/all_to_all | solution.py:348
  73.8 1.3 convolution_multiply_fusion
  75.1 10.2 %all-to-all-done.2.x_ref = bf16[32,64,128]{2,1,0:T(8,128)(2,1)} async-done(((bf16[32,64,128]{2,1,0:T(8,128)(2,1)}), bf16[32,64,128]{2,1,0:T(8,128)(2,1)}, u32[]{:S(2)}, u32[]{:S(2)}) %all-to-all-start.2) | async-done | bytes 524320 | tf_op jit(solution)/shard_map/all_to_all | solution.py:348
  85.3 1.2 copy-done.2
  86.5 1.2 copy-done.5
  87.7 3.7 %col_middle.1 = bf16[32,64,128]{2,1,0:T(8,128)(2,1)S(1)} custom-call(bf16[32,64,128]{2,1,0:T(8,128)(2,1)} %all-to-all-done.2.x_ref, f32[8,128]{1,0:T(8,128)S(1)} %concatenate.37.c_ref, f32[32,64,128]{2,1,0:T(8,128)S(1)} %bitcast.30, bf16[32,128,128]{2,1,0:T(8,128)(2,1)S(1)} %copy-done.2, bf16[32,128,256]{2,1,0:T(8,128)(2,1)S(1)} %copy-done.1), custom_call_target="tpu_custom_call" | custom-call | flops 100000000 | bytes 5246976 | tf_op jit(solution)/shard_map/col_middle/pallas_call | solution.py:221
  91.5 15.1 %all_to_all.30.x_ref = bf16[32,64,128]{2,1,0:T(8,128)(2,1)S(1)} all-to-all(bf16[32,64,128]{2,1,0:T(8,128)(2,1)S(1)} %col_middle.1), channel_id=1, replica_groups=mesh['xl'=2,'y'=4,'xh'=2,'z'=8,'c'=2] {'xl','y','xh','c'}, dimensions={0} | all-to-all | bytes 1048576 | tf_op jit(solution)/shard_map/all_to_all | solution.py:348
  106.6 7.1 %row_two.1 = bf16[32,64,128]{2,1,0:T(8,128)(2,1)S(1)} custom-call(bf16[32,64,128]{2,1,0:T(8,128)(2,1)S(1)} %all_to_all.30.x_ref, f32[32,64,128]{2,1,0:T(8,128)S(1)} %get-tuple-element.20.kr_ref, f32[32,64,128]{2,1,0:T(8,128)S(1)} %copy-done.3, f32[32,2,128]{2,1,0:T(2,128)S(1)} %copy-done.9, bf16[256,256]{1,0:T(8,128)(2,1)S(1)} %copy-done.7, ...), custom_call_target="tpu_custom_call" | custom-call | flops 100000000 | bytes 3440640 | tf_op jit(solution)/shard_map/row_two/pallas_call | solution.py:221
  113.7 15.1 %all_to_all.31.x_ref = bf16[32,64,128]{2,1,0:T(8,128)(2,1)S(1)} all-to-all(bf16[32,64,128]{2,1,0:T(8,128)(2,1)S(1)} %row_two.1), channel_id=1, replica_groups=mesh['xl'=2,'y'=4,'xh'=2,'z'=8,'c'=2] {'xl','y','xh','c'}, dimensions={0} | all-to-all | bytes 1048576 | tf_op jit(solution)/shard_map/all_to_all | solution.py:348
  128.8 1.8 %col_last.1 = bf16[32,64,128]{2,1,0:T(8,128)(2,1)} custom-call(bf16[32,64,128]{2,1,0:T(8,128)(2,1)S(1)} %all_to_all.31.x_ref, f32[8,128]{1,0:T(8,128)S(1)} %concatenate.37.c_ref, bf16[32,128,128]{2,1,0:T(8,128)(2,1)S(1)} %copy-done.2), custom_call_target="tpu_custom_call" | custom-call | flops 100000000 | bytes 2101248 | tf_op jit(solution)/shard_map/col_last/pallas_call | solution.py:221
  130.6 3.9 %all-to-all-start.5 = ((bf16[32,64,128]{2,1,0:T(8,128)(2,1)}), bf16[32,64,128]{2,1,0:T(8,128)(2,1)S(1)}, u32[]{:S(2)}, u32[]{:S(2)}) async-start(bf16[32,64,128]{2,1,0:T(8,128)(2,1)} %col_last.1), calls=%async_computation.5 | async-start | bytes 1048576 | tf_op jit(solution)/shard_map/all_to_all | solution.py:358
  134.5 6.4 %fusion.1 = f32[64,256,16]{1,2,0:T(8,128)S(1)} fusion(f32[256]{0:T(256)S(1)} %copy-done.12, f32[256]{0:T(256)S(1)} %copy-done.13, f32[64,256]{1,0:T(8,128)S(1)} %add_add_fusion, bf16[256,16]{0,1:T(8,128)(2,1)S(1)} %copy-done), kind=kOutput, calls=%fused_computation.5 | convolution fusion | flops 180355072 | bytes 1124352 | tf_op jit(solution)/shard_map/rch,hj->jrc/dot_general | solution.py:248
  140.9 0.6 copy.24
  141.9 10.8 %all-to-all-done.5.x_ref = bf16[32,64,128]{2,1,0:T(8,128)(2,1)S(1)} async-done(((bf16[32,64,128]{2,1,0:T(8,128)(2,1)}), bf16[32,64,128]{2,1,0:T(8,128)(2,1)S(1)}, u32[]{:S(2)}, u32[]{:S(2)}) %all-to-all-start.5) | async-done | bytes 524320 | tf_op jit(solution)/shard_map/all_to_all | solution.py:358
  152.7 0.8 combine.1
  (43 shorter events, 1.6 us)
Async XLA Ops:
  0.0 0.9 copy-start
  0.9 5.2 %copy-start.10 = (f32[16]{0:T(128)S(1)}, f32[16]{0:T(128)}, u32[]{:S(2)}) copy-start(f32[16]{0:T(128)} %param.21) | copy-start | bytes 196
  6.1 14.3 %copy-start.11 = (f32[128]{0:T(128)S(1)}, f32[128]{0:T(128)}, u32[]{:S(2)}) copy-start(f32[128]{0:T(128)} %constant.141) | copy-start | bytes 1540
  6.2 14.3 %copy-start.12 = (f32[256]{0:T(256)S(1)}, f32[256]{0:T(256)}, u32[]{:S(2)}) copy-start(f32[256]{0:T(256)} %param.19) | copy-start | bytes 3076
  6.2 14.3 %copy-start.13 = (f32[256]{0:T(256)S(1)}, f32[256]{0:T(256)}, u32[]{:S(2)}) copy-start(f32[256]{0:T(256)} %param.18) | copy-start | bytes 3076
  6.2 14.3 %copy-start.14 = (f32[128]{0:T(128)S(1)}, f32[128]{0:T(128)}, u32[]{:S(2)}) copy-start(f32[128]{0:T(128)} %constant.140) | copy-start | bytes 1540
  6.2 32.3 %copy-start.1 = (bf16[32,128,256]{2,1,0:T(8,128)(2,1)S(1)}, bf16[32,128,256]{2,1,0:T(8,128)(2,1)}, u32[]{:S(2)}) copy-start(bf16[32,128,256]{2,1,0:T(8,128)(2,1)} %constant.125.clone.w_ref) | copy-start | bytes 6291460
  7.9 30.7 %all-to-all-start = ((bf16[32,64,128]{2,1,0:T(8,128)(2,1)}), bf16[32,64,128]{2,1,0:T(8,128)(2,1)S(1)}, u32[]{:S(2)}, u32[]{:S(2)}) async-start(bf16[32,64,128]{2,1,0:T(8,128)(2,1)} %pack.1), calls=%async_computation | async-start | bytes 1048576 | tf_op jit(solution)/shard_map/all_to_all | solution.py:302
  40.7 18.3 %all-to-all-start.1 = ((bf16[32,64,128]{2,1,0:T(8,128)(2,1)}), bf16[32,64,128]{2,1,0:T(8,128)(2,1)}, u32[]{:S(2)}, u32[]{:S(2)}) async-start(bf16[32,64,128]{2,1,0:T(8,128)(2,1)} %col_first.1), calls=%async_computation.1 | async-start | bytes 1048576 | tf_op jit(solution)/shard_map/all_to_all | solution.py:348
  51.9 7.2 %copy-start.7 = (bf16[256,256]{1,0:T(8,128)(2,1)S(1)}, bf16[256,256]{1,0:T(8,128)(2,1)}, u32[]{:S(2)}) copy-start(bf16[256,256]{1,0:T(8,128)(2,1)} %constant.127.clone.w_ref) | copy-start | bytes 393220
  51.9 7.2 %copy-start.8 = (bf16[256,256]{1,0:T(8,128)(2,1)S(1)}, bf16[256,256]{1,0:T(8,128)(2,1)}, u32[]{:S(2)}) copy-start(bf16[256,256]{1,0:T(8,128)(2,1)} %constant.128.clone.v_ref) | copy-start | bytes 393220
  51.9 7.2 %copy-start.9 = (f32[32,2,128]{2,1,0:T(2,128)S(1)}, f32[32,2,128]{2,1,0:T(2,128)}, u32[]{:S(2)}) copy-start(f32[32,2,128]{2,1,0:T(2,128)} %constant.129.clone.t_ref) | copy-start | bytes 98308
  59.1 1.2 copy-start.4
  68.3 0.8 copy-start.6
  69.1 16.2 %all-to-all-start.2 = ((bf16[32,64,128]{2,1,0:T(8,128)(2,1)}), bf16[32,64,128]{2,1,0:T(8,128)(2,1)}, u32[]{:S(2)}, u32[]{:S(2)}) async-start(bf16[32,64,128]{2,1,0:T(8,128)(2,1)} %copy-done.6), calls=%async_computation.2 | async-start | bytes 1048576 | tf_op jit(solution)/shard_map/all_to_all | solution.py:348
  85.3 1.2 copy-start.2
  86.5 1.2 copy-start.5
  87.7 18.8 %copy-start.3 = (f32[32,64,128]{2,1,0:T(8,128)S(1)}, f32[32,64,128]{2,1,0:T(8,128)}, u32[]{:S(2)}) copy-start(f32[32,64,128]{2,1,0:T(8,128)} %get-tuple-element.5.ki_ref) | copy-start | bytes 3145732
  130.6 22.1 %all-to-all-start.5 = ((bf16[32,64,128]{2,1,0:T(8,128)(2,1)}), bf16[32,64,128]{2,1,0:T(8,128)(2,1)S(1)}, u32[]{:S(2)}, u32[]{:S(2)}) async-start(bf16[32,64,128]{2,1,0:T(8,128)(2,1)} %col_last.1), calls=%async_computation.5 | async-start | bytes 1048576 | tf_op jit(solution)/shard_map/all_to_all | solution.py:358

commit v2 on v1

v2 whole, which is shorter than its diff:
```python
import functools
import math

import jax
import jax.numpy as jnp
import ml_dtypes
import numpy as np
from jax import lax
from jax.experimental import pallas as pl
from jax.experimental.pallas import tpu as pltpu
from jax.sharding import Mesh, PartitionSpec as P


LEVELS = 16
WAVES = 8
SIDE = 2048
FIRST = 32
SECOND = 64
LANES = 2 * SECOND
ROWS = SECOND // 2
SLAB = ("xh", "z", "c")
WAVE = ("xl", "y")
PLANE = ("xl", "y", "xh", "c")
VMEM_LIMIT = 16 * 2**20


def split_np(table):
    high = table.astype(np.float32).astype(ml_dtypes.bfloat16)
    low = (table - high.astype(np.float64)).astype(np.float32).astype(ml_dtypes.bfloat16)
    return high, low


def small_dft(direction):
    place = np.arange(SECOND)
    angle = direction * 2.0 * math.pi / SECOND * (place[:, None] * place[None, :] % SECOND)
    scale = 1.0 if direction < 0 else 1.0 / SIDE
    return np.cos(angle) * scale, np.sin(angle) * scale


def row_tables(direction):
    cos, sin = small_dft(direction)
    pair = np.eye(2)
    table = np.block([[np.kron(pair, cos), np.kron(pair, sin)], [-np.kron(pair, sin), np.kron(pair, cos)]])
    high, low = split_np(table)
    return np.concatenate([high, high, low], 0)


def col_tables(direction):
    cos, sin = small_dft(direction)
    halves = []
    for cut in (slice(0, ROWS), slice(ROWS, SECOND)):
        halves.append((np.concatenate([cos[:, cut], -sin[:, cut]], 1), np.concatenate([sin[:, cut], cos[:, cut]], 1)))
    high, low = split_np(np.concatenate([halves[0][0], halves[1][0], halves[0][1], halves[1][1]], 0))
    return np.concatenate([high, high, low] if direction < 0 else [high, low], 1)


def row_twiddles():
    angle = -2.0 * math.pi / SIDE * (np.arange(FIRST)[:, None] * np.arange(SECOND)[None, :])
    return np.stack([np.tile(np.cos(angle), (1, 2)), np.tile(np.sin(angle), (1, 2))], 1).astype(np.float32)


def col_twiddles():
    place = np.arange(ROWS)[:, None] + ROWS * (np.arange(LANES) // SECOND)[None, :]
    angle = -2.0 * math.pi / SIDE * (np.arange(FIRST)[:, None, None] * place[None])
    return np.stack([np.cos(angle), np.sin(angle)]).astype(np.float32)


def left_lanes():
    return lax.broadcasted_iota(jnp.int32, (1, LANES), 1) < SECOND


def swap(x):
    return pltpu.roll(x, SECOND, x.ndim - 1)


def dft(real, imag, direction):
    count = len(real)
    if count == 1:
        return real, imag
    even_re, even_im = dft(real[0::2], imag[0::2], direction)
    odd_re, odd_im = dft(real[1::2], imag[1::2], direction)
    half = count // 2
    lower_re, lower_im, upper_re, upper_im = [], [], [], []
    for k in range(half):
        a, b = odd_re[k], odd_im[k]
        if k == 0:
            turn_re, turn_im = a, b
        elif 2 * k == half:
            turn_re, turn_im = (b, -a) if direction < 0 else (-b, a)
        else:
            angle = direction * 2.0 * math.pi * k / count
            cos, sin = math.cos(angle), math.sin(angle)
            turn_re, turn_im = a * cos - b * sin, a * sin + b * cos
        lower_re.append(even_re[k] + turn_re)
        lower_im.append(even_im[k] + turn_im)
        upper_re.append(even_re[k] - turn_re)
        upper_im.append(even_im[k] - turn_im)
    return lower_re + upper_re, lower_im + upper_im


def split_pair(x):
    high = x.astype(jnp.bfloat16)
    return high, (x - high.astype(jnp.float32)).astype(jnp.bfloat16)


def matmul(left, right):
    return jnp.dot(left, right, preferred_element_type=jnp.float32)


def load_groups(x_ref, g):
    real = [x_ref[a, g : g + 16, :].astype(jnp.float32) for a in range(FIRST)]
    imag = [x_ref[a, ROWS + g : ROWS + g + 16, :].astype(jnp.float32) for a in range(FIRST)]
    return [([r[h : h + 8] for r in real], [i[h : h + 8] for i in imag]) for h in (0, 8)]


def store_groups(out_ref, g, halves):
    for part in range(2):
        for a in range(FIRST):
            whole = jnp.concatenate([halves[0][part][a], halves[1][part][a]], 0)
            out_ref[a, part * ROWS + g : part * ROWS + g + 16, :] = whole.astype(jnp.bfloat16)


def join_halves(both):
    left = left_lanes()
    parts = []
    for first in (0, 2 * SECOND):
        low, high = both[first : first + SECOND], both[first + SECOND : first + 2 * SECOND]
        base = jnp.where(left, low[:ROWS], high[ROWS:])
        moved = jnp.where(left, low[ROWS:], high[:ROWS])
        parts.append(base + swap(moved))
    return parts


def col_forward(y_ref, w_ref, out_ref):
    for k in range(0, FIRST, 2):
        data = [jnp.concatenate([y_ref[0, k + i], y_ref[1, k + i]], 0) for i in range(2)]
        high, low = split_pair(jnp.concatenate(data, 1))
        both = matmul(w_ref[...], jnp.concatenate([high, low, high], 0))
        for i in range(2):
            real, imag = join_halves(both[:, i * LANES : (i + 1) * LANES])
            out_ref[k + i] = jnp.concatenate([real, imag], 0).astype(jnp.bfloat16)


def col_inverse(x_ref, v_ref, t_ref, y_ref):
    for k in range(0, FIRST, 2):
        data = jnp.concatenate([x_ref[k], x_ref[k + 1]], 1)
        both = matmul(v_ref[...], jnp.concatenate([data, data], 0))
        for i in range(2):
            real, imag = join_halves(both[:, i * LANES : (i + 1) * LANES])
            cos, sin = t_ref[0, k + i], t_ref[1, k + i]
            y_ref[0, k + i] = real * cos + imag * sin
            y_ref[1, k + i] = imag * cos - real * sin


def turn_and_keep(y_ref, t_ref, rows, real, imag):
    for k in range(FIRST):
        cos, sin = t_ref[0, k, rows, :], t_ref[1, k, rows, :]
        y_ref[0, k, rows, :] = real[k] * cos - imag[k] * sin
        y_ref[1, k, rows, :] = real[k] * sin + imag[k] * cos


def col_first_kernel(x_ref, c_ref, t_ref, w_ref, out_ref, y_ref):
    mean_re, mean_im = c_ref[0:1, :], c_ref[1:2, :]
    for g in range(0, ROWS, 16):
        for h, (real, imag) in enumerate(load_groups(x_ref, g)):
            real, imag = dft([r - mean_re for r in real], [i - mean_im for i in imag], -1.0)
            turn_and_keep(y_ref, t_ref, slice(g + 8 * h, g + 8 * h + 8), real, imag)
    col_forward(y_ref, w_ref, out_ref)


def col_middle_kernel(x_ref, c_ref, s_ref, t_ref, v_ref, w_ref, out_ref, y_ref):
    field_re, field_im = c_ref[2:3, :], c_ref[3:4, :]
    mean_re, mean_im = c_ref[4:5, :], c_ref[5:6, :]
    col_inverse(x_ref, v_ref, t_ref, y_ref)
    for g in range(0, ROWS, 8):
        rows = slice(g, g + 8)
        real, imag = dft(
            [y_ref[0, k, rows, :] for k in range(FIRST)], [y_ref[1, k, rows, :] for k in range(FIRST)], 1.0
        )
        for a in range(FIRST):
            value_re, value_im = real[a] + field_re, imag[a] + field_im
            weight = (value_re * value_re + value_im * value_im - s_ref[a, rows, :]) * (1.0 / WAVES)
            real[a] = weight * value_re - mean_re
            imag[a] = weight * value_im - mean_im
        real, imag = dft(real, imag, -1.0)
        turn_and_keep(y_ref, t_ref, rows, real, imag)
    col_forward(y_ref, w_ref, out_ref)


def col_last_kernel(x_ref, c_ref, t_ref, v_ref, out_ref, y_ref):
    back_re, back_im = c_ref[6:7, :], c_ref[7:8, :]
    col_inverse(x_ref, v_ref, t_ref, y_ref)
    for g in range(0, ROWS, 16):
        halves = []
        for h in (0, 8):
            rows = slice(g + h, g + h + 8)
            real, imag = dft(
                [y_ref[0, k, rows, :] for k in range(FIRST)], [y_ref[1, k, rows, :] for k in range(FIRST)], 1.0
            )
            halves.append(([r + back_re for r in real], [i + back_im for i in imag]))
        store_groups(out_ref, g, halves)


def row_step(real, imag, w_ref):
    high, low = split_pair(jnp.concatenate([real, imag], 1))
    both = matmul(jnp.concatenate([high, low, high], 1), w_ref[...])
    return both[:, :LANES], both[:, LANES:]


def row_kernel(conjugate, x_ref, kr_ref, ki_ref, t_ref, w_ref, v_ref, out_ref, y_ref):
    for g in range(0, ROWS, 16):
        for h, (real, imag) in enumerate(load_groups(x_ref, g)):
            real, imag = dft(real, imag, -1.0)
            rows = slice(g + 8 * h, g + 8 * h + 8)
            for k in range(FIRST):
                cos, sin = t_ref[k, 0:1, :], t_ref[k, 1:2, :]
                y_ref[0, k, rows, :] = real[k] * cos - imag[k] * sin
                y_ref[1, k, rows, :] = real[k] * sin + imag[k] * cos
    step = 8
    rows = step * ROWS
    for k in range(0, FIRST, step):
        real, imag = row_step(
            y_ref[0, k : k + step].reshape(rows, LANES), y_ref[1, k : k + step].reshape(rows, LANES), w_ref
        )
        kr = kr_ref[k : k + step].reshape(rows, LANES)
        ki = ki_ref[k : k + step].reshape(rows, LANES)
        if conjugate:
            real, imag = real * kr + imag * ki, imag * kr - real * ki
        else:
            real, imag = real * kr - imag * ki, imag * kr + real * ki
        real, imag = row_step(real, imag, v_ref)
        for i in range(step):
            part = slice(i * ROWS, (i + 1) * ROWS)
            cos, sin = t_ref[k + i, 0:1, :], t_ref[k + i, 1:2, :]
            y_ref[0, k + i] = real[part] * cos + imag[part] * sin
            y_ref[1, k + i] = imag[part] * cos - real[part] * sin
    for g in range(0, ROWS, 16):
        halves = []
        for h in (0, 8):
            rows = slice(g + h, g + h + 8)
            halves.append(
                dft([y_ref[0, k, rows, :] for k in range(FIRST)], [y_ref[1, k, rows, :] for k in range(FIRST)], 1.0)
            )
        store_groups(out_ref, g, halves)


def pack_kernel(x_ref, out_ref):
    left = left_lanes()
    for w in range(WAVES):
        for tile in range(2):
            lanes = slice(tile * LANES, (tile + 1) * LANES)
            place = tile * 2 * WAVES + w * 2
            for part in range(2):
                whole = x_ref[part * WAVES + w, :, lanes].astype(jnp.float32)
                top, low = whole[:ROWS], whole[ROWS:]
                rows = slice(part * ROWS, (part + 1) * ROWS)
                out_ref[place, rows, :] = jnp.where(left, top, swap(low)).astype(out_ref.dtype)
                out_ref[place + 1, rows, :] = jnp.where(left, swap(top), low).astype(out_ref.dtype)


def combine_kernel(x_ref, d_ref, out_ref):
    left = left_lanes()
    for tile in range(2):
        sums = []
        for core in range(2):
            total = None
            for w in range(WAVES):
                place = tile * 2 * WAVES + w * 2 + core
                term = x_ref[place].astype(jnp.float32) * d_ref[place]
                total = term if total is None else total + term
            sums.append(total[:ROWS] + total[ROWS:])
        lanes = slice(tile * LANES, (tile + 1) * LANES)
        out_ref[:ROWS, lanes] = jnp.where(left, sums[0], swap(sums[1]))
        out_ref[ROWS:, lanes] = jnp.where(left, swap(sums[0]), sums[1])


def call(kernel, out_shape, *args, scratch=True, flops=10**8, name=None):
    size = sum(a.size * a.dtype.itemsize for a in args) + math.prod(out_shape.shape) * out_shape.dtype.itemsize
    return pl.pallas_call(
        kernel,
        out_shape=out_shape,
        scratch_shapes=[pltpu.VMEM((2, FIRST, ROWS, LANES), jnp.float32)] if scratch else [],
        compiler_params=pltpu.CompilerParams(vmem_limit_bytes=VMEM_LIMIT),
        cost_estimate=pl.CostEstimate(flops=flops, bytes_accessed=size, transcendentals=0),
        name=name,
    )(*args)


def level_widths(levels, offsets):
    return 0.3 + levels.astype(jnp.float32) * (0.4 / (LEVELS - 1)) + offsets


def surrogate_rows(widths, w_in, b_in, w_out, b_out):
    pre_act = widths[..., None] * w_in + b_in
    hidden = (pre_act * jax.nn.sigmoid(pre_act)).astype(jnp.bfloat16)
    mixed_out = (
        jnp.einsum("rch,hj->jrc", hidden, w_out, preferred_element_type=jnp.float32) + b_out[:, None, None]
    )
    return mixed_out.astype(jnp.bfloat16)


def slope_rows(widths, w_in, b_in, w_out):
    pre_act = widths[..., None] * w_in + b_in
    gate = jax.nn.sigmoid(pre_act)
    slope = gate * (1.0 + pre_act * (1.0 - gate)) * w_in
    return jnp.einsum("rch,hj->jrc", slope.astype(jnp.bfloat16), w_out, preferred_element_type=jnp.float32)


def signed_kappa(index):
    signed = jnp.where(index < SIDE // 2, index, index - SIDE)
    return signed.astype(jnp.float32) * (2.0 * math.pi / SIDE)


def transfer(wavelength, kx, ky, focal_length):
    wave_number = 2.0 * math.pi / wavelength
    kz_square = wave_number * wave_number - kx**2 - ky**2
    kz_root = jnp.sqrt(jnp.abs(kz_square))
    is_open = kz_square > 0.0
    phase_angle = jnp.where(is_open, focal_length * kz_root, 0.0)
    amplitude = jnp.where(is_open, 1.0, jnp.exp(-focal_length * kz_root))
    return (amplitude * jnp.cos(phase_angle), amplitude * jnp.sin(phase_angle))


def usual_transmission(w_in, b_in, w_out, b_out):
    nodes, weights = np.polynomial.hermite_e.hermegauss(8)
    weights = weights / weights.sum()
    shifts = np.clip(0.1 * nodes, -0.3, 0.3)
    places = (0.3 + 0.4 * np.arange(LEVELS)[:, None] / (LEVELS - 1) + shifts[None, :]).reshape(-1)
    shares = np.tile(weights / LEVELS, LEVELS).astype(np.float32)
    pre_act = places.astype(np.float32)[:, None] * w_in[None, :] + b_in[None, :]
    hidden = pre_act * jax.nn.sigmoid(pre_act)
    values = jnp.dot(hidden, w_out.astype(jnp.float32)) + b_out
    mean = jnp.sum(values * shares[:, None], 0)
    spread = jnp.sum((values - mean) ** 2 * shares[:, None], 0)
    return mean, spread


def local(levels, offsets, targets, w_in, b_in, w_out, b_out):
    block = (FIRST, SECOND, LANES)
    packed16 = jax.ShapeDtypeStruct(block, jnp.bfloat16)
    packed32 = jax.ShapeDtypeStruct(block, jnp.float32)
    wave_index = lax.axis_index("z")
    plane_index = lax.axis_index(PLANE)
    wavelength = 1.5 + wave_index.astype(jnp.float32) / (WAVES - 1)
    focal_length = float(SIDE // 16)
    spot_level = float(SIDE // 8)
    forward_cols = jnp.asarray(col_tables(-1.0))
    inverse_cols = jnp.asarray(col_tables(1.0))
    forward_rows = jnp.asarray(row_tables(-1.0))
    inverse_rows = jnp.asarray(row_tables(1.0))
    turns_cols = jnp.asarray(col_twiddles())
    turns_rows = jnp.asarray(row_twiddles())

    widths = level_widths(levels, offsets)
    trans = surrogate_rows(widths, w_in, b_in, w_out, b_out)
    sent = call(pack_kernel, packed16, trans, scratch=False, name="pack")
    cols = lax.all_to_all(sent, SLAB, 0, 0, tiled=True)

    mean, spread = usual_transmission(w_in, b_in, w_out, b_out)
    mean_re = lax.dynamic_index_in_dim(mean, wave_index, 0, keepdims=False)
    mean_im = lax.dynamic_index_in_dim(mean, wave_index + WAVES, 0, keepdims=False)
    noise = lax.dynamic_index_in_dim(spread, wave_index, 0, keepdims=False) + lax.dynamic_index_in_dim(
        spread, wave_index + WAVES, 0, keepdims=False
    )
    zero = jnp.zeros((), jnp.float32)
    dc_re, dc_im = transfer(wavelength, zero, zero, focal_length)
    field_re = mean_re * dc_re - mean_im * dc_im
    field_im = mean_re * dc_im + mean_im * dc_re
    spots_mean = spot_level * targets.shape[1] / (SIDE * SIDE)
    gain = (field_re * field_re + field_im * field_im + 2.0 * noise - spots_mean) / WAVES
    adj_re = gain * field_re
    adj_im = gain * field_im
    back_re = adj_re * dc_re + adj_im * dc_im
    back_im = adj_im * dc_re - adj_re * dc_im
    consts = jnp.stack([mean_re, mean_im, field_re, field_im, adj_re, adj_im, back_re, back_im])
    consts = jnp.broadcast_to(consts[:, None], (8, LANES))

    lane = jnp.arange(LANES, dtype=jnp.int32)
    first = jnp.arange(FIRST, dtype=jnp.int32)
    row = jnp.arange(ROWS, dtype=jnp.int32)[:, None] + ROWS * (lane // SECOND)[None, :]
    kx = signed_kappa(plane_index + FIRST * row)
    ky = signed_kappa(first[:, None] + FIRST * (lane % SECOND)[None, :])
    kern_re, kern_im = transfer(wavelength, kx[None], ky[:, None, :], focal_length)

    own_targets = lax.dynamic_index_in_dim(targets, wave_index, 0, keepdims=False)
    place = (first[:, None] * SECOND + jnp.arange(ROWS, dtype=jnp.int32)[None, :]).reshape(-1)
    row_hits, col_hits = [], []
    for half in range(2):
        row_hits.append(place[:, None] + half * ROWS == own_targets[:, 0][None, :])
        col_hit = own_targets[:, 1][:, None] == (plane_index * SECOND + lane % SECOND)[None, :]
        col_hits.append(col_hit & (lane // SECOND == half)[None, :])
    row_hits = jnp.concatenate(row_hits, 1).astype(jnp.bfloat16)
    col_hits = jnp.concatenate(col_hits, 0).astype(jnp.bfloat16)
    spots = spot_level * jnp.dot(row_hits, col_hits, preferred_element_type=jnp.float32)
    spots = spots.reshape(FIRST, ROWS, LANES)

    slopes = call(pack_kernel, packed32, slope_rows(widths, w_in, b_in, w_out), scratch=False, name="pack_slopes")

    def exchange(x):
        return lax.all_to_all(x, PLANE, 0, 0, tiled=True)

    def filtered(x, conjugate, name):
        kernel = functools.partial(row_kernel, conjugate)
        return call(kernel, packed16, x, kern_re, kern_im, turns_rows, forward_rows, inverse_rows, name=name)

    cols = call(col_first_kernel, packed16, cols, consts, turns_cols, forward_cols, name="col_first")
    rows = filtered(exchange(cols), False, "row_one")
    cols = exchange(rows)
    cols = call(
        col_middle_kernel, packed16, cols, consts, spots, turns_cols, inverse_cols, forward_cols, name="col_middle"
    )
    rows = filtered(exchange(cols), True, "row_two")
    cols = exchange(rows)
    cotangent = call(col_last_kernel, packed16, cols, consts, turns_cols, inverse_cols, name="col_last")
    returned = lax.all_to_all(cotangent, SLAB, 0, 0, tiled=True)
    return call(
        combine_kernel, jax.ShapeDtypeStruct(levels.shape, jnp.float32), returned, slopes, scratch=False, name="combine"
    )


def solution(mesh):
    fine = Mesh(mesh.devices.reshape(2, 4, 2, 8, 2), ("xl", "y", "xh", "z", "c"))
    placed = (P(SLAB, WAVE), P(SLAB, WAVE), P(), P(), P(), P(), P())
    return jax.shard_map(local, mesh=fine, in_specs=placed, out_specs=P(SLAB, WAVE), check_vma=False)
```

time: 154 us -> 141 us (0.916)
  Pallas kernels: 25 us -> 13.4 us
  waiting for transfers between devices: 36.7 us -> 40.1 us
  other arithmetic: 7.97 us -> 4.95 us
  local copies, waits for them, and re-layouts: 7.82 us -> 5.9 us
    pallas_call x8, Pallas kernels: 25 us -> 13.4 us  [call(): pl.pallas_call(kernel, out_shape=out_shape, scratch_shapes=[pltpu.VMEM((2...]
    neg x2 -> x0, other arithmetic: 6.23 us -> none  [the longest x1 4.3 us: local(): ki = jnp.concatenate([-kern_im, kern_im], 2)]
    all_to_all x2, waiting for transfers between devices: 15.4 us -> 19.4 us  [exchange(): return lax.all_to_all(x, PLANE, 0, 0, tiled=True)]
    mul x1 -> x4, other arithmetic: 0.01 us -> 2.12 us  [the longest x1 2.11 us: transfer(): return (amplitude * jnp.cos(phase_angle), amplitude * jnp.sin(phase_angle))]
    unnamed x30 -> x38, local copies, waits for them, and re-layouts: 4.53 us -> 2.45 us
  transfers between devices with their start and end apart: 4 -> 4, of which waited for: 4 -> 4; matrix products, arithmetic and copies ran while one was open for 12% -> 10% of each run, Pallas kernels for 0% -> 0%
where the time goes in v2:
time: 141 us; the launch traced here: 140 us
  waiting for transfers between devices  40.1 us (28%)
  blocking collectives  30.5 us (22%)
  starting transfers between devices  27.6 us (20%)
  Pallas kernels  13.4 us (10%)
  matrix products  13 us (9%)
  local copies, waits for them, and re-layouts  5.9 us (4%)
  other arithmetic  4.95 us (4%)
  between operations  4.35 us (3%)
    all_to_all x2, blocking collectives, exchange(): return lax.all_to_all(x, PLANE, 0, 0, tiled=True)  30.5 us
    all_to_all x2, waiting for transfers between devices, exchange(): return lax.all_to_all(x, PLANE, 0, 0, tiled=True)  19.4 us
    pallas_call x8, Pallas kernels, call(): pl.pallas_call(kernel, out_shape=out_shape, scratch_shapes=[pltpu.VMEM((2...  13.4 us
    all_to_all x1, starting transfers between devices, local(): cols = lax.all_to_all(sent, SLAB, 0, 0, tiled=True)  12.7 us
    all_to_all x2, starting transfers between devices, exchange(): return lax.all_to_all(x, PLANE, 0, 0, tiled=True)  10.8 us
    all_to_all x1, waiting for transfers between devices, local(): returned = lax.all_to_all(cotangent, SLAB, 0, 0, tiled=True)  10.8 us
    all_to_all x1, waiting for transfers between devices, local(): cols = lax.all_to_all(sent, SLAB, 0, 0, tiled=True)  9.92 us
    dot_general x1, matrix products, slope_rows(): jnp.einsum('rch,hj->jrc', slope.astype(jnp.bfloat16), w_out, preferred_el...  6.44 us
  transfers between devices with their start and end apart: 4, of which 4 were waited for; matrix products, arithmetic and copies ran while one was open for 10% of the time, Pallas kernels for 0%

profile of v2, /device:TPU:1, one launch (start us, length us, event | category | flops | bytes accessed | tf_op | source)
XLA Modules:
  0.0 139.7 jit_solution(10172716972256914499)
XLA Ops:
  0.0 0.9 add_add_fusion
  0.9 0.6 copy-done.11
  1.5 5.2 %fusion = f32[64,256,16]{1,2,0:T(8,128)S(1)} fusion(f32[256]{0:T(256)} %param.20, f32[256]{0:T(256)} %param.19, f32[64,256]{1,0:T(8,128)S(1)} %add_add_fusion, bf16[256,16]{0,1:T(8,128)(2,1)S(1)} %copy-done), kind=kOutput, calls=%fused_computation.4 | convolution fusion | flops 163577856 | bytes 1124352 | tf_op jit(solution)/shard_map/rch,hj->jrc/dot_general | solution.py:297
  6.8 0.6 fusion.13.x_ref
  7.4 1.0 pack.1
  8.5 12.7 %all-to-all-start = ((bf16[32,64,128]{2,1,0:T(8,128)(2,1)}), bf16[32,64,128]{2,1,0:T(8,128)(2,1)S(1)}, u32[]{:S(2)}, u32[]{:S(2)}) async-start(bf16[32,64,128]{2,1,0:T(8,128)(2,1)} %pack.1), calls=%async_computation | async-start | bytes 1048576 | tf_op jit(solution)/shard_map/all_to_all | solution.py:357
  21.3 0.3 multiply_reduce_fusion.1
  22.1 0.7 fusion.44
  26.6 1.3 stack.29
  27.9 0.7 dynamic-slice_bitcast_fusion
  28.7 0.7 compare_and_fusion.1
  29.4 9.9 %all-to-all-done.x_ref = bf16[32,64,128]{2,1,0:T(8,128)(2,1)S(1)} async-done(((bf16[32,64,128]{2,1,0:T(8,128)(2,1)}), bf16[32,64,128]{2,1,0:T(8,128)(2,1)S(1)}, u32[]{:S(2)}, u32[]{:S(2)}) %all-to-all-start) | async-done | bytes 524320 | tf_op jit(solution)/shard_map/all_to_all | solution.py:357
  39.4 2.1 %col_first.1 = bf16[32,64,128]{2,1,0:T(8,128)(2,1)} custom-call(bf16[32,64,128]{2,1,0:T(8,128)(2,1)S(1)} %all-to-all-done.x_ref, f32[8,128]{1,0:T(8,128)S(1)} %broadcast_in_dim.6.c_ref, f32[2,32,32,128]{3,2,1,0:T(8,128)S(1)} %copy-done.1, bf16[256,192]{1,0:T(8,128)(2,1)S(1)} %copy-done.5), custom_call_target="tpu_custom_call" | custom-call | flops 100000000 | bytes 2199552 | tf_op jit(solution)/shard_map/col_first/pallas_call | solution.py:279
  41.5 6.9 %all-to-all-start.1 = ((bf16[32,64,128]{2,1,0:T(8,128)(2,1)}), bf16[32,64,128]{2,1,0:T(8,128)(2,1)S(1)}, u32[]{:S(2)}, u32[]{:S(2)}) async-start(bf16[32,64,128]{2,1,0:T(8,128)(2,1)} %col_first.1), calls=%async_computation.1 | async-start | bytes 1048576 | tf_op jit(solution)/shard_map/all_to_all | solution.py:400
  48.5 2.1 %fusion.9 = (f32[32,32,128]{2,1,0:T(8,128)S(1)}, f32[32,32,128]{2,1,0:T(8,128)S(1)}) fusion(f32[32,128]{1,0:T(8,128)S(1)} %get-tuple-element.22, f32[32,128]{1,0:T(8,128)S(1)} %get-tuple-element.21), kind=kLoop, calls=%fused_computation.19 | loop fusion | flops 1179648 | bytes 1081344 | tf_op jit(solution)/shard_map/mul | solution.py:321
  50.6 9.2 %all-to-all-done.1.x_ref = bf16[32,64,128]{2,1,0:T(8,128)(2,1)S(1)} async-done(((bf16[32,64,128]{2,1,0:T(8,128)(2,1)}), bf16[32,64,128]{2,1,0:T(8,128)(2,1)S(1)}, u32[]{:S(2)}, u32[]{:S(2)}) %all-to-all-start.1) | async-done | bytes 524320 | tf_op jit(solution)/shard_map/all_to_all | solution.py:400
  59.8 2.8 %row_one.1 = bf16[32,64,128]{2,1,0:T(8,128)(2,1)} custom-call(bf16[32,64,128]{2,1,0:T(8,128)(2,1)S(1)} %all-to-all-done.1.x_ref, f32[32,32,128]{2,1,0:T(8,128)S(1)} %get-tuple-element.6.kr_ref, f32[32,32,128]{2,1,0:T(8,128)S(1)} %get-tuple-element.5.ki_ref, f32[32,2,128]{2,1,0:T(2,128)S(1)} %copy-done.9, bf16[768,256]{1,0:T(8,128)(2,1)S(1)} %copy-done.2, ...), custom_call_target="tpu_custom_call" | custom-call | flops 100000000 | bytes 2916352 | tf_op jit(solution)/shard_map/row_one/pallas_call | solution.py:279
  62.6 3.9 %all-to-all-start.2 = ((bf16[32,64,128]{2,1,0:T(8,128)(2,1)}), bf16[32,64,128]{2,1,0:T(8,128)(2,1)S(1)}, u32[]{:S(2)}, u32[]{:S(2)}) async-start(bf16[32,64,128]{2,1,0:T(8,128)(2,1)} %row_one.1), calls=%async_computation.2 | async-start | bytes 1048576 | tf_op jit(solution)/shard_map/all_to_all | solution.py:400
  66.9 1.0 convolution_multiply_fusion
  67.9 10.2 %all-to-all-done.2.x_ref = bf16[32,64,128]{2,1,0:T(8,128)(2,1)S(1)} async-done(((bf16[32,64,128]{2,1,0:T(8,128)(2,1)}), bf16[32,64,128]{2,1,0:T(8,128)(2,1)S(1)}, u32[]{:S(2)}, u32[]{:S(2)}) %all-to-all-start.2) | async-done | bytes 524320 | tf_op jit(solution)/shard_map/all_to_all | solution.py:400
  78.1 0.9 copy-done.6
  79.0 0.8 copy-done.7
  79.8 2.4 %col_middle.1 = bf16[32,64,128]{2,1,0:T(8,128)(2,1)S(1)} custom-call(bf16[32,64,128]{2,1,0:T(8,128)(2,1)S(1)} %all-to-all-done.2.x_ref, f32[8,128]{1,0:T(8,128)S(1)} %broadcast_in_dim.6.c_ref, f32[32,32,128]{2,1,0:T(8,128)S(1)} %bitcast.28, f32[2,32,32,128]{3,2,1,0:T(8,128)S(1)} %copy-done.1, bf16[256,128]{1,0:T(8,128)(2,1)S(1)} %copy-done.7, ...), custom_call_target="tpu_custom_call" | custom-call | flops 100000000 | bytes 2789376 | tf_op jit(solution)/shard_map/col_middle/pallas_call | solution.py:279
  82.3 15.2 %all_to_all.30.x_ref = bf16[32,64,128]{2,1,0:T(8,128)(2,1)S(1)} all-to-all(bf16[32,64,128]{2,1,0:T(8,128)(2,1)S(1)} %col_middle.1), channel_id=1, replica_groups=mesh['xl'=2,'y'=4,'xh'=2,'z'=8,'c'=2] {'xl','y','xh','c'}, dimensions={0} | all-to-all | bytes 1048576 | tf_op jit(solution)/shard_map/all_to_all | solution.py:400
  97.5 1.9 %row_two.1 = bf16[32,64,128]{2,1,0:T(8,128)(2,1)S(1)} custom-call(bf16[32,64,128]{2,1,0:T(8,128)(2,1)S(1)} %all_to_all.30.x_ref, f32[32,32,128]{2,1,0:T(8,128)S(1)} %get-tuple-element.6.kr_ref, f32[32,32,128]{2,1,0:T(8,128)S(1)} %get-tuple-element.5.ki_ref, f32[32,2,128]{2,1,0:T(2,128)S(1)} %copy-done.10, bf16[768,256]{1,0:T(8,128)(2,1)S(1)} %copy-done.2, ...), custom_call_target="tpu_custom_call" | custom-call | flops 100000000 | bytes 2916352 | tf_op jit(solution)/shard_map/row_two/pallas_call | solution.py:279
  99.5 15.2 %all_to_all.31.x_ref = bf16[32,64,128]{2,1,0:T(8,128)(2,1)S(1)} all-to-all(bf16[32,64,128]{2,1,0:T(8,128)(2,1)S(1)} %row_two.1), channel_id=1, replica_groups=mesh['xl'=2,'y'=4,'xh'=2,'z'=8,'c'=2] {'xl','y','xh','c'}, dimensions={0} | all-to-all | bytes 1048576 | tf_op jit(solution)/shard_map/all_to_all | solution.py:400
  114.7 2.0 %col_last.1 = bf16[32,64,128]{2,1,0:T(8,128)(2,1)} custom-call(bf16[32,64,128]{2,1,0:T(8,128)(2,1)S(1)} %all_to_all.31.x_ref, f32[8,128]{1,0:T(8,128)S(1)} %broadcast_in_dim.6.c_ref, f32[2,32,32,128]{3,2,1,0:T(8,128)S(1)} %copy-done.1, bf16[256,128]{1,0:T(8,128)(2,1)S(1)} %copy-done.8), custom_call_target="tpu_custom_call" | custom-call | flops 100000000 | bytes 2166784 | tf_op jit(solution)/shard_map/col_last/pallas_call | solution.py:279
  116.7 4.0 %all-to-all-start.5 = ((bf16[32,64,128]{2,1,0:T(8,128)(2,1)}), bf16[32,64,128]{2,1,0:T(8,128)(2,1)S(1)}, u32[]{:S(2)}, u32[]{:S(2)}) async-start(bf16[32,64,128]{2,1,0:T(8,128)(2,1)} %col_last.1), calls=%async_computation.5 | async-start | bytes 1048576 | tf_op jit(solution)/shard_map/all_to_all | solution.py:415
  120.7 6.4 %fusion.1 = f32[64,256,16]{1,2,0:T(8,128)S(1)} fusion(f32[256]{0:T(256)S(1)} %copy-done.15, f32[256]{0:T(256)S(1)} %copy-done.17, f32[64,256]{1,0:T(8,128)S(1)} %copy-done.12, bf16[256,16]{0,1:T(8,128)(2,1)S(1)} %copy-done), kind=kOutput, calls=%fused_computation.5 | convolution fusion | flops 180355072 | bytes 1124352 | tf_op jit(solution)/shard_map/rch,hj->jrc/dot_general | solution.py:306
  127.2 0.6 copy.25
  128.1 10.8 %all-to-all-done.5.x_ref = bf16[32,64,128]{2,1,0:T(8,128)(2,1)S(1)} async-done(((bf16[32,64,128]{2,1,0:T(8,128)(2,1)}), bf16[32,64,128]{2,1,0:T(8,128)(2,1)S(1)}, u32[]{:S(2)}, u32[]{:S(2)}) %all-to-all-start.5) | async-done | bytes 524320 | tf_op jit(solution)/shard_map/all_to_all | solution.py:415
  138.9 0.8 combine.1
  (49 shorter events, 1.2 us)
Async XLA Ops:
  0.0 1.5 %copy-start = (bf16[256,16]{0,1:T(8,128)(2,1)S(1)}, bf16[256,16]{0,1:T(8,128)(2,1)}, u32[]{:S(2)}) copy-start(bf16[256,16]{0,1:T(8,128)(2,1)} %param.21) | copy-start | bytes 24580
  0.9 0.6 copy-start.11
  1.5 5.2 %copy-start.13 = (f32[16]{0:T(128)S(1)}, f32[16]{0:T(128)}, u32[]{:S(2)}) copy-start(f32[16]{0:T(128)} %param.22) | copy-start | bytes 196
  7.4 13.8 %copy-start.14 = (f32[128]{0:T(128)S(1)}, f32[128]{0:T(128)}, u32[]{:S(2)}) copy-start(f32[128]{0:T(128)} %constant.165) | copy-start | bytes 1540
  7.4 13.8 %copy-start.15 = (f32[256]{0:T(256)S(1)}, f32[256]{0:T(256)}, u32[]{:S(2)}) copy-start(f32[256]{0:T(256)} %param.20) | copy-start | bytes 3076
  7.4 13.8 %copy-start.16 = (f32[256]{0:T(256)S(1)}, f32[256]{0:T(256)}, u32[]{:S(2)}) copy-start(f32[256]{0:T(256)} %param.19) | copy-start | bytes 3076
  7.4 13.8 %copy-start.18 = (f32[128]{0:T(128)S(1)}, f32[128]{0:T(128)}, u32[]{:S(2)}) copy-start(f32[128]{0:T(128)} %constant.164) | copy-start | bytes 1540
  8.5 30.9 %copy-start.1 = (f32[2,32,32,128]{3,2,1,0:T(8,128)S(1)}, f32[2,32,32,128]{3,2,1,0:T(8,128)}, u32[]{:S(2)}) copy-start(f32[2,32,32,128]{3,2,1,0:T(8,128)} %constant.160.clone.t_ref) | copy-start | bytes 3145732
  8.5 30.9 %copy-start.5 = (bf16[256,192]{1,0:T(8,128)(2,1)S(1)}, bf16[256,192]{1,0:T(8,128)(2,1)}, u32[]{:S(2)}) copy-start(bf16[256,192]{1,0:T(8,128)(2,1)} %constant.156.clone.w_ref) | copy-start | bytes 294916
  8.5 30.8 %all-to-all-start = ((bf16[32,64,128]{2,1,0:T(8,128)(2,1)}), bf16[32,64,128]{2,1,0:T(8,128)(2,1)S(1)}, u32[]{:S(2)}, u32[]{:S(2)}) async-start(bf16[32,64,128]{2,1,0:T(8,128)(2,1)} %pack.1), calls=%async_computation | async-start | bytes 1048576 | tf_op jit(solution)/shard_map/all_to_all | solution.py:357
  41.5 18.4 %copy-start.2 = (bf16[768,256]{1,0:T(8,128)(2,1)S(1)}, bf16[768,256]{1,0:T(8,128)(2,1)}, u32[]{:S(2)}) copy-start(bf16[768,256]{1,0:T(8,128)(2,1)} %constant.158.clone.w_ref) | copy-start | bytes 1179652
  41.5 18.4 %copy-start.3 = (bf16[768,256]{1,0:T(8,128)(2,1)S(1)}, bf16[768,256]{1,0:T(8,128)(2,1)}, u32[]{:S(2)}) copy-start(bf16[768,256]{1,0:T(8,128)(2,1)} %constant.159.clone.v_ref) | copy-start | bytes 1179652
  41.5 18.4 %copy-start.9 = (f32[32,2,128]{2,1,0:T(2,128)S(1)}, f32[32,2,128]{2,1,0:T(2,128)}, u32[]{:S(2)}) copy-start(f32[32,2,128]{2,1,0:T(2,128)} %constant.161.clone.t_ref) | copy-start | bytes 98308
  41.5 18.4 %all-to-all-start.1 = ((bf16[32,64,128]{2,1,0:T(8,128)(2,1)}), bf16[32,64,128]{2,1,0:T(8,128)(2,1)S(1)}, u32[]{:S(2)}, u32[]{:S(2)}) async-start(bf16[32,64,128]{2,1,0:T(8,128)(2,1)} %col_first.1), calls=%async_computation.1 | async-start | bytes 1048576 | tf_op jit(solution)/shard_map/all_to_all | solution.py:400
  62.6 15.5 %all-to-all-start.2 = ((bf16[32,64,128]{2,1,0:T(8,128)(2,1)}), bf16[32,64,128]{2,1,0:T(8,128)(2,1)S(1)}, u32[]{:S(2)}, u32[]{:S(2)}) async-start(bf16[32,64,128]{2,1,0:T(8,128)(2,1)} %row_one.1), calls=%async_computation.2 | async-start | bytes 1048576 | tf_op jit(solution)/shard_map/all_to_all | solution.py:400
  78.1 0.9 copy-start.6
  79.0 0.8 copy-start.7
  82.2 15.3 %copy-start.4 = (bf16[768,256]{1,0:T(8,128)(2,1)S(1)}, bf16[768,256]{1,0:T(8,128)(2,1)}, u32[]{:S(2)}) copy-start(bf16[768,256]{1,0:T(8,128)(2,1)} %constant.159.clone.v_ref) | copy-start | bytes 1179652
  82.3 15.2 %copy-start.10 = (f32[32,2,128]{2,1,0:T(2,128)S(1)}, f32[32,2,128]{2,1,0:T(2,128)}, u32[]{:S(2)}) copy-start(f32[32,2,128]{2,1,0:T(2,128)} %constant.161.clone.t_ref) | copy-start | bytes 98308
  99.4 15.2 %copy-start.8 = (bf16[256,128]{1,0:T(8,128)(2,1)S(1)}, bf16[256,128]{1,0:T(8,128)(2,1)}, u32[]{:S(2)}) copy-start(bf16[256,128]{1,0:T(8,128)(2,1)} %constant.157.clone.v_ref) | copy-start | bytes 196612
  116.7 4.1 %copy-start.12 = (f32[64,256]{1,0:T(8,128)S(1)}, f32[64,256]{1,0:T(8,128)}, u32[]{:S(2)}) copy-start(f32[64,256]{1,0:T(8,128)} %copy-done.11) | copy-start | bytes 196612
  116.7 4.1 %copy-start.17 = (f32[256]{0:T(256)S(1)}, f32[256]{0:T(256)}, u32[]{:S(2)}) copy-start(f32[256]{0:T(256)} %param.19) | copy-start | bytes 3076
  116.7 22.3 %all-to-all-start.5 = ((bf16[32,64,128]{2,1,0:T(8,128)(2,1)}), bf16[32,64,128]{2,1,0:T(8,128)(2,1)S(1)}, u32[]{:S(2)}, u32[]{:S(2)}) async-start(bf16[32,64,128]{2,1,0:T(8,128)(2,1)} %col_last.1), calls=%async_computation.5 | async-start | bytes 1048576 | tf_op jit(solution)/shard_map/all_to_all | solution.py:415

commit v3 on v2

v3 whole, which is shorter than its diff:
```python
import functools
import math

import jax
import jax.numpy as jnp
import ml_dtypes
import numpy as np
from jax import lax
from jax.experimental import pallas as pl
from jax.experimental.pallas import tpu as pltpu
from jax.sharding import Mesh, PartitionSpec as P


LEVELS = 16
WAVES = 8
SIDE = 2048
FIRST = 32
SECOND = 64
LANES = 2 * SECOND
ROWS = SECOND // 2
OUTER = 16
GROUP = 8
SLAB = ("xh", "z", "c")
WAVE = ("xl", "y")
PLANE = ("xh", "c", "xl", "y")
EVERY = ("xh", "z", "c", "xl", "y")
VMEM_LIMIT = 16 * 2**20


def split_np(table):
    high = table.astype(np.float32).astype(ml_dtypes.bfloat16)
    low = (table - high.astype(np.float64)).astype(np.float32).astype(ml_dtypes.bfloat16)
    return high, low


def small_dft(direction):
    place = np.arange(SECOND)
    angle = direction * 2.0 * math.pi / SECOND * (place[:, None] * place[None, :] % SECOND)
    scale = 1.0 if direction < 0 else 1.0 / SIDE
    return np.cos(angle) * scale, np.sin(angle) * scale


def row_tables(direction):
    cos, sin = small_dft(direction)
    pair = np.eye(2)
    table = np.block([[np.kron(pair, cos), np.kron(pair, sin)], [-np.kron(pair, sin), np.kron(pair, cos)]])
    high, low = split_np(table)
    return np.concatenate([high, high, low] if direction < 0 else [high, low], 0)


def col_tables(direction):
    cos, sin = small_dft(direction)
    halves = []
    for cut in (slice(0, ROWS), slice(ROWS, SECOND)):
        halves.append((np.concatenate([cos[:, cut], -sin[:, cut]], 1), np.concatenate([sin[:, cut], cos[:, cut]], 1)))
    high, low = split_np(np.concatenate([halves[0][0], halves[1][0], halves[0][1], halves[1][1]], 0))
    return np.concatenate([high, high, low], 1)


def whole_row_tables(direction):
    place = np.arange(LANES)[:, None]
    freq = np.concatenate([np.arange(0, LANES, 2), np.arange(1, LANES, 2)])[None, :]
    angle = direction * 2.0 * math.pi / LANES * (place * freq % LANES)
    cos, sin = np.cos(angle), np.sin(angle)
    cuts = (slice(0, SECOND), slice(SECOND, LANES))
    if direction < 0:
        table = np.block([[part for cut in cuts for part in (cos[:, cut], sin[:, cut])],
                          [part for cut in cuts for part in (-sin[:, cut], cos[:, cut])]])
        high, low = split_np(table)
        return np.concatenate([high, high, low], 0)
    cos, sin = cos.T / SIDE, sin.T / SIDE
    table = np.concatenate([np.block([[cos[cut], sin[cut]], [-sin[cut], cos[cut]]]) for cut in cuts], 0)
    high, low = split_np(table)
    return np.concatenate([high, low], 0)


def row_twiddles():
    angle = -2.0 * math.pi / SIDE * (np.arange(FIRST)[:, None] * np.arange(SECOND)[None, :])
    return np.stack([np.tile(np.cos(angle), (1, 2)), np.tile(np.sin(angle), (1, 2))], 1).astype(np.float32)


def whole_row_twiddles():
    angle = -2.0 * math.pi / SIDE * (np.arange(OUTER)[:, None] * np.arange(LANES)[None, :])
    return np.stack([np.cos(angle), np.sin(angle)], 1).astype(np.float32)


def col_twiddles():
    place = np.arange(ROWS)[:, None] + ROWS * (np.arange(LANES) // SECOND)[None, :]
    angle = -2.0 * math.pi / SIDE * (np.arange(FIRST)[:, None, None] * place[None])
    return np.stack([np.cos(angle), np.sin(angle)]).astype(np.float32)


def left_lanes():
    return lax.broadcasted_iota(jnp.int32, (1, LANES), 1) < SECOND


def swap(x):
    return pltpu.roll(x, SECOND, x.ndim - 1)


def dft(real, imag, direction):
    count = len(real)
    if count == 1:
        return real, imag
    even_re, even_im = dft(real[0::2], imag[0::2], direction)
    odd_re, odd_im = dft(real[1::2], imag[1::2], direction)
    half = count // 2
    lower_re, lower_im, upper_re, upper_im = [], [], [], []
    for k in range(half):
        a, b = odd_re[k], odd_im[k]
        if k == 0:
            turn_re, turn_im = a, b
        elif 2 * k == half:
            turn_re, turn_im = (b, -a) if direction < 0 else (-b, a)
        else:
            angle = direction * 2.0 * math.pi * k / count
            cos, sin = math.cos(angle), math.sin(angle)
            turn_re, turn_im = a * cos - b * sin, a * sin + b * cos
        lower_re.append(even_re[k] + turn_re)
        lower_im.append(even_im[k] + turn_im)
        upper_re.append(even_re[k] - turn_re)
        upper_im.append(even_im[k] - turn_im)
    return lower_re + upper_re, lower_im + upper_im


def split_pair(x):
    high = x.astype(jnp.bfloat16)
    return high, (x - high.astype(jnp.float32)).astype(jnp.bfloat16)


def matmul(left, right):
    return jnp.dot(left, right, preferred_element_type=jnp.float32)


def load_groups(x_ref, g):
    real = [x_ref[a, g : g + 16, :].astype(jnp.float32) for a in range(FIRST)]
    imag = [x_ref[a, ROWS + g : ROWS + g + 16, :].astype(jnp.float32) for a in range(FIRST)]
    return [([r[h : h + 8] for r in real], [i[h : h + 8] for i in imag]) for h in (0, 8)]


def store_groups(out_ref, g, halves):
    for part in range(2):
        for a in range(FIRST):
            whole = jnp.concatenate([halves[0][part][a], halves[1][part][a]], 0)
            out_ref[a, part * ROWS + g : part * ROWS + g + 16, :] = whole.astype(jnp.bfloat16)


def join_halves(both):
    left = left_lanes()
    parts = []
    for first in (0, 2 * SECOND):
        low, high = both[first : first + SECOND], both[first + SECOND : first + 2 * SECOND]
        base = jnp.where(left, low[:ROWS], high[ROWS:])
        moved = jnp.where(left, low[ROWS:], high[:ROWS])
        parts.append(base + swap(moved))
    return parts


def parts_of(y_ref, rows):
    return [y_ref[0, k, rows, :] for k in range(FIRST)], [y_ref[1, k, rows, :] for k in range(FIRST)]


def turn(real, imag, cos, sin):
    return real * cos - imag * sin, imag * cos + real * sin


def turn_back(real, imag, cos, sin):
    return real * cos + imag * sin, imag * cos - real * sin


def first_kernel(x_ref, a_ref, b_ref, o_ref, m_ref, t_ref, w_ref, out_ref, h_ref, y_ref):
    def block(m, carry):
        for i in range(GROUP):
            tiles = []
            for tile in range(2):
                half = x_ref[m, i : i + 1, tile * LANES : (tile + 1) * LANES] * a_ref[...] + b_ref[...]
                tiles.append((half + half * jnp.tanh(half)).astype(jnp.bfloat16))
            mixed = matmul(o_ref[...], jnp.concatenate(tiles, 1))
            for tile in range(2):
                part = mixed[:, tile * LANES : (tile + 1) * LANES] + m_ref[0]
                part = part.astype(jnp.bfloat16).astype(jnp.float32) - m_ref[1]
                h_ref[2 * m + tile, pl.ds(i, 2 * WAVES, stride=GROUP), :] = part
        return carry

    lax.fori_loop(0, WAVES, block, 0)
    for w in range(WAVES):
        rows_re, rows_im = slice(w * GROUP, (w + 1) * GROUP), slice((WAVES + w) * GROUP, (WAVES + w + 1) * GROUP)
        real, imag = dft(
            [h_ref[a, rows_re, :] for a in range(OUTER)], [h_ref[a, rows_im, :] for a in range(OUTER)], -1.0
        )
        for k in range(OUTER):
            rows = slice((w * OUTER + k) * GROUP, (w * OUTER + k + 1) * GROUP)
            y_ref[rows, :LANES], y_ref[rows, LANES:] = turn(real[k], imag[k], t_ref[k, 0:1, :], t_ref[k, 1:2, :])
    step = 256
    for r in range(0, 1024, step):
        high, low = split_pair(y_ref[r : r + step])
        both = matmul(jnp.concatenate([high, low, high], 1), w_ref[...]).astype(jnp.bfloat16)
        out_ref[r : r + step] = both[:, :LANES]
        out_ref[1024 + r : 1024 + r + step] = both[:, LANES:]


def last_kernel(x_ref, c_ref, d_ref, t_ref, v_ref, out_ref, y_ref):
    step = 256
    for r in range(0, 1024, step):
        data = jnp.concatenate([x_ref[r : r + step], x_ref[1024 + r : 1024 + r + step]], 1)
        y_ref[r : r + step] = matmul(jnp.concatenate([data, data], 1), v_ref[...])
    for a in range(OUTER):
        out_ref[a // 2, :, (a % 2) * LANES : (a % 2 + 1) * LANES] = jnp.zeros((GROUP, LANES), jnp.float32)
    for w in range(WAVES):
        real, imag = [], []
        for k in range(OUTER):
            rows = slice((w * OUTER + k) * GROUP, (w * OUTER + k + 1) * GROUP)
            re, im = turn_back(y_ref[rows, :LANES], y_ref[rows, LANES:], t_ref[k, 0:1, :], t_ref[k, 1:2, :])
            real.append(re)
            imag.append(im)
        real, imag = dft(real, imag, 1.0)
        for a in range(OUTER):
            lanes = slice((a % 2) * LANES, (a % 2 + 1) * LANES)
            total = out_ref[a // 2, :, lanes]
            for j, part in ((w, real[a]), (WAVES + w, imag[a])):
                cotangent = (part + c_ref[j : j + 1, :]).astype(jnp.bfloat16).astype(jnp.float32)
                total = total + cotangent * d_ref[a // 2, j * GROUP : (j + 1) * GROUP, lanes]
            out_ref[a // 2, :, lanes] = total


def load_lanes(x_ref, g):
    left = left_lanes()
    real, imag = [], []
    for a in range(FIRST):
        top = x_ref[a * SECOND + g : a * SECOND + g + 16, :].astype(jnp.float32)
        low = x_ref[a * SECOND + ROWS + g : a * SECOND + ROWS + g + 16, :].astype(jnp.float32)
        real.append(jnp.where(left, top, swap(low)))
        imag.append(jnp.where(left, swap(top), low))
    return [([r[h : h + 8] for r in real], [i[h : h + 8] for i in imag]) for h in (0, 8)]


def store_lanes(out_ref, g, halves):
    left = left_lanes()
    for a in range(FIRST):
        real = jnp.concatenate([halves[0][0][a], halves[1][0][a]], 0)
        imag = jnp.concatenate([halves[0][1][a], halves[1][1][a]], 0)
        top = jnp.where(left, real, swap(imag)).astype(jnp.bfloat16)
        low = jnp.where(left, swap(real), imag).astype(jnp.bfloat16)
        out_ref[a * SECOND + g : a * SECOND + g + 16, :] = top
        out_ref[a * SECOND + ROWS + g : a * SECOND + ROWS + g + 16, :] = low


def col_step(parts, w_ref):
    data = jnp.concatenate([jnp.concatenate(part, 0) for part in parts], 1)
    high, low = split_pair(data)
    both = matmul(w_ref[...], jnp.concatenate([high, low, high], 0))
    return [join_halves(both[:, i * LANES : (i + 1) * LANES]) for i in range(len(parts))]


def col_kernel(conjugate, x_ref, kr_ref, ki_ref, t_ref, w_ref, v_ref, out_ref, y_ref):
    for g in range(0, ROWS, 16):
        halves = load_groups(x_ref, g) if conjugate else load_lanes(x_ref, g)
        for h, (real, imag) in enumerate(halves):
            real, imag = dft(real, imag, -1.0)
            rows = slice(g + 8 * h, g + 8 * h + 8)
            for k in range(FIRST):
                y_ref[0, k, rows, :], y_ref[1, k, rows, :] = turn(
                    real[k], imag[k], t_ref[0, k, rows, :], t_ref[1, k, rows, :]
                )
    for k in range(0, FIRST, 2):
        parts = col_step([(y_ref[0, k + i], y_ref[1, k + i]) for i in range(2)], w_ref)
        for i in range(2):
            turned = turn_back if conjugate else turn
            parts[i] = turned(parts[i][0], parts[i][1], kr_ref[k + i], ki_ref[k + i])
        parts = col_step(parts, v_ref)
        for i in range(2):
            y_ref[0, k + i], y_ref[1, k + i] = turn_back(
                parts[i][0], parts[i][1], t_ref[0, k + i], t_ref[1, k + i]
            )
    for g in range(0, ROWS, 16):
        halves = [dft(*parts_of(y_ref, slice(g + h, g + h + 8)), 1.0) for h in (0, 8)]
        if conjugate:
            store_lanes(out_ref, g, halves)
        else:
            store_groups(out_ref, g, halves)


def middle_kernel(x_ref, c_ref, s_ref, t_ref, v_ref, w_ref, out_ref, y_ref):
    field_re, field_im = c_ref[0:1, :], c_ref[1:2, :]
    mean_re, mean_im = c_ref[2:3, :], c_ref[3:4, :]
    step = 8
    rows = step * ROWS
    for k in range(0, FIRST, step):
        real = jnp.concatenate([x_ref[k + i, :ROWS, :] for i in range(step)], 0)
        imag = jnp.concatenate([x_ref[k + i, ROWS:, :] for i in range(step)], 0)
        both = matmul(jnp.concatenate([real, imag, real, imag], 1), v_ref[...])
        for i in range(step):
            part = slice(i * ROWS, (i + 1) * ROWS)
            y_ref[0, k + i], y_ref[1, k + i] = turn_back(
                both[part, :LANES], both[part, LANES:], t_ref[k + i, 0:1, :], t_ref[k + i, 1:2, :]
            )
    for g in range(0, ROWS, 8):
        part = slice(g, g + 8)
        real, imag = dft(*parts_of(y_ref, part), 1.0)
        for a in range(FIRST):
            value_re, value_im = real[a] + field_re, imag[a] + field_im
            weight = (value_re * value_re + value_im * value_im - s_ref[a, part, :]) * (1.0 / WAVES)
            real[a] = weight * value_re - mean_re
            imag[a] = weight * value_im - mean_im
        real, imag = dft(real, imag, -1.0)
        for k in range(FIRST):
            y_ref[0, k, part, :], y_ref[1, k, part, :] = turn(
                real[k], imag[k], t_ref[k, 0:1, :], t_ref[k, 1:2, :]
            )
    for k in range(0, FIRST, step):
        real = y_ref[0, k : k + step].reshape(rows, LANES)
        imag = y_ref[1, k : k + step].reshape(rows, LANES)
        high, low = split_pair(jnp.concatenate([real, imag], 1))
        both = matmul(jnp.concatenate([high, low, high], 1), w_ref[...]).astype(jnp.bfloat16)
        for i in range(step):
            part = slice(i * ROWS, (i + 1) * ROWS)
            out_ref[k + i] = jnp.concatenate([both[part, :LANES], both[part, LANES:]], 0)


def call(kernel, out_shape, scratch, *args, name=None):
    size = sum(a.size * a.dtype.itemsize for a in args) + math.prod(out_shape.shape) * out_shape.dtype.itemsize
    return pl.pallas_call(
        kernel,
        out_shape=out_shape,
        scratch_shapes=[pltpu.VMEM(shape, jnp.float32) for shape in scratch],
        compiler_params=pltpu.CompilerParams(vmem_limit_bytes=VMEM_LIMIT),
        cost_estimate=pl.CostEstimate(flops=10**8, bytes_accessed=size, transcendentals=0),
        name=name,
    )(*args)


def level_widths(levels, offsets):
    return 0.3 + levels.astype(jnp.float32) * (0.4 / (LEVELS - 1)) + offsets


def slope_rows(widths, w_in, b_in, w_out):
    pre_act = widths[..., None] * w_in + b_in
    gate = jax.nn.sigmoid(pre_act)
    slope = gate * (1.0 + pre_act * (1.0 - gate)) * w_in
    return jnp.einsum("mich,hj->mjic", slope.astype(jnp.bfloat16), w_out, preferred_element_type=jnp.float32)


def signed_kappa(index):
    signed = jnp.where(index < SIDE // 2, index, index - SIDE)
    return signed.astype(jnp.float32) * (2.0 * math.pi / SIDE)


def transfer(wavelength, kx, ky, focal_length):
    wave_number = 2.0 * math.pi / wavelength
    kz_square = wave_number * wave_number - kx**2 - ky**2
    kz_root = jnp.sqrt(jnp.abs(kz_square))
    is_open = kz_square > 0.0
    phase_angle = jnp.where(is_open, focal_length * kz_root, 0.0)
    amplitude = jnp.where(is_open, 1.0, jnp.exp(-focal_length * kz_root))
    return (amplitude * jnp.cos(phase_angle), amplitude * jnp.sin(phase_angle))


def usual_transmission(w_in, b_in, w_out, b_out):
    nodes, weights = np.polynomial.hermite_e.hermegauss(8)
    weights = weights / weights.sum()
    shifts = np.clip(0.1 * nodes, -0.3, 0.3)
    places = (0.3 + 0.4 * np.arange(LEVELS)[:, None] / (LEVELS - 1) + shifts[None, :]).reshape(-1)
    shares = np.tile(weights / LEVELS, LEVELS).astype(np.float32)
    pre_act = places.astype(np.float32)[:, None] * w_in[None, :] + b_in[None, :]
    hidden = pre_act * jax.nn.sigmoid(pre_act)
    values = jnp.dot(hidden, w_out.astype(jnp.float32)) + b_out
    mean = jnp.sum(values * shares[:, None], 0)
    spread = jnp.sum((values - mean) ** 2 * shares[:, None], 0)
    return mean, spread


def local(levels, offsets, targets, w_in, b_in, w_out, b_out):
    block = (FIRST, SECOND, LANES)
    halves = (2, FIRST, ROWS, LANES)
    packed = jax.ShapeDtypeStruct(block, jnp.bfloat16)
    lined = jax.ShapeDtypeStruct((SIDE, LANES), jnp.bfloat16)
    wave_index = lax.axis_index("z")
    plane_index = lax.axis_index(PLANE)
    focal_length = float(SIDE // 16)
    spot_level = float(SIDE // 8)
    forward_cols = jnp.asarray(col_tables(-1.0))
    inverse_cols = jnp.asarray(col_tables(1.0))
    forward_rows = jnp.asarray(row_tables(-1.0))
    inverse_rows = jnp.asarray(row_tables(1.0))
    forward_whole = jnp.asarray(whole_row_tables(-1.0))
    inverse_whole = jnp.asarray(whole_row_tables(1.0))
    turns_cols = jnp.asarray(col_twiddles())
    turns_rows = jnp.asarray(row_twiddles())
    turns_whole = jnp.asarray(whole_row_twiddles())

    rows_here, cols_here = levels.shape
    widths = level_widths(levels, offsets).reshape(WAVES, GROUP, cols_here)
    widths = lax.all_to_all(widths, WAVE, 0, 0, tiled=True)

    mean, spread = usual_transmission(w_in, b_in, w_out, b_out)
    mean_re, mean_im = mean[:WAVES], mean[WAVES:]
    noise = spread[:WAVES] + spread[WAVES:]
    wavelengths = 1.5 + jnp.arange(WAVES, dtype=jnp.int32).astype(jnp.float32) / (WAVES - 1)
    zero = jnp.zeros((), jnp.float32)
    dc_re, dc_im = transfer(wavelengths, zero, zero, focal_length)
    field_re = mean_re * dc_re - mean_im * dc_im
    field_im = mean_re * dc_im + mean_im * dc_re
    spots_mean = spot_level * targets.shape[1] / (SIDE * SIDE)
    gain = (field_re * field_re + field_im * field_im + 2.0 * noise - spots_mean) / WAVES
    adj_re = gain * field_re
    adj_im = gain * field_im
    back = jnp.concatenate([adj_re * dc_re + adj_im * dc_im, adj_im * dc_re - adj_re * dc_im])
    back = jnp.broadcast_to(back[:, None], (2 * WAVES, LANES))
    own = lax.dynamic_index_in_dim(jnp.stack([field_re, field_im, adj_re, adj_im]), wave_index, 1, keepdims=True)
    own = jnp.broadcast_to(own, (4, LANES))
    shifts = jnp.broadcast_to(jnp.stack([b_out, mean])[:, :, None], (2, 2 * WAVES, LANES))

    sent = call(
        first_kernel,
        lined,
        [(OUTER, 2 * WAVES * GROUP, LANES), (1024, 2 * LANES)],
        widths,
        jnp.broadcast_to(0.5 * w_in[:, None], (w_in.shape[0], LANES)),
        jnp.broadcast_to(0.5 * b_in[:, None], (b_in.shape[0], LANES)),
        w_out.T,
        shifts,
        turns_whole,
        forward_whole,
        name="first",
    )
    cols = lax.all_to_all(sent, EVERY, 0, 0, tiled=True)

    lane = jnp.arange(LANES, dtype=jnp.int32)
    first = jnp.arange(FIRST, dtype=jnp.int32)
    row = jnp.arange(ROWS, dtype=jnp.int32)[:, None] + ROWS * (lane // SECOND)[None, :]
    kx = signed_kappa(first[:, None, None] + FIRST * row[None])
    ky = signed_kappa(plane_index + FIRST * (lane % SECOND))
    wavelength = 1.5 + wave_index.astype(jnp.float32) / (WAVES - 1)
    kern_re, kern_im = transfer(wavelength, kx, ky[None, None, :], focal_length)

    own_targets = lax.dynamic_index_in_dim(targets, wave_index, 0, keepdims=False)
    place_row = plane_index * SECOND + jnp.arange(ROWS, dtype=jnp.int32)
    hit_a = own_targets[:, 1][None, :] // SECOND == first[:, None]
    near, far = [], []
    for half in range(2):
        hit_row = own_targets[:, 0][None, :] == (place_row + half * ROWS)[:, None]
        near.append((hit_a[:, None, :] & hit_row[None, :, :]).reshape(FIRST * ROWS, -1))
        hit_col = (own_targets[:, 1] % SECOND)[:, None] == (lane % SECOND)[None, :]
        far.append(hit_col & (lane // SECOND == half)[None, :])
    near = jnp.concatenate(near, 1).astype(jnp.bfloat16)
    far = jnp.concatenate(far, 0).astype(jnp.bfloat16)
    spots = spot_level * jnp.dot(near, far, preferred_element_type=jnp.float32)
    spots = spots.reshape(FIRST, ROWS, LANES)

    slopes = slope_rows(widths, w_in, b_in, w_out).reshape(WAVES, 2 * WAVES * GROUP, cols_here)

    def filtered(x, out_shape, conjugate, name):
        kernel = functools.partial(col_kernel, conjugate)
        return call(
            kernel, out_shape, [halves], x, kern_re, kern_im, turns_cols, forward_cols, inverse_cols, name=name
        )

    def exchange(x):
        return lax.all_to_all(x, PLANE, 0, 0, tiled=True)

    rows = exchange(filtered(cols, packed, False, "filter"))
    rows = call(middle_kernel, packed, [halves], rows, own, spots, turns_rows, inverse_rows, forward_rows, name="middle")
    cols = filtered(exchange(rows), lined, True, "filter_back")
    lines = lax.all_to_all(cols, EVERY, 0, 0, tiled=True)
    gradient = call(
        last_kernel,
        jax.ShapeDtypeStruct((WAVES, GROUP, cols_here), jnp.float32),
        [(1024, 2 * LANES)],
        lines,
        back,
        slopes,
        turns_whole,
        inverse_whole,
        name="last",
    )
    return lax.all_to_all(gradient, WAVE, 0, 0, tiled=True).reshape(rows_here, cols_here)


def solution(mesh):
    fine = Mesh(mesh.devices.reshape(2, 4, 2, 8, 2), ("xl", "y", "xh", "z", "c"))
    placed = (P(SLAB, WAVE), P(SLAB, WAVE), P(), P(), P(), P(), P())
    return jax.shard_map(local, mesh=fine, in_specs=placed, out_specs=P(SLAB, WAVE), check_vma=False)
```

time: 141 us -> 132 us (0.936)
  blocking collectives: 30.5 us -> 8.45 us
  waiting for transfers between devices: 40.1 us -> 52.7 us
  starting transfers between devices: 27.6 us -> 34.5 us
  matrix products: 13 us -> 7.85 us
  between operations: 4.35 us -> 0.33 us
  other arithmetic: 4.95 us -> 7.14 us
    all_to_all x2 -> x1, blocking collectives: 30.5 us -> 8.45 us  [local(): lax.all_to_all(gradient, WAVE, 0, 0, tiled=True)]
    all_to_all x2 -> x3, waiting for transfers between devices: 20.7 us -> 30.4 us  [the longest x1 16.5 us: local(): cols = lax.all_to_all(sent, EVERY, 0, 0, tiled=True)]
    all_to_all x2 -> x3, starting transfers between devices: 16.8 us -> 25.6 us  [the longest x1 14 us: local(): cols = lax.all_to_all(sent, EVERY, 0, 0, tiled=True)]
    dot_general x3 -> x2, matrix products: 12.7 us -> 6.77 us  [the longest x1 6.45 us: slope_rows(): jnp.einsum('mich,hj->mjic', slope.astype(jnp.bfloat16), w_out, preferred_...]
    all_to_all x2, waiting for transfers between devices: 19.4 us -> 22.3 us  [exchange(): return lax.all_to_all(x, PLANE, 0, 0, tiled=True)]
    all_to_all x2, starting transfers between devices: 10.8 us -> 8.97 us  [exchange(): return lax.all_to_all(x, PLANE, 0, 0, tiled=True)]
    reshape x0 -> x1, other arithmetic: none -> 1.58 us  [local(): widths = level_widths(levels, offsets).reshape(WAVES, GROUP, cols_here)]
    pallas_call x8 -> x5, Pallas kernels: 13.4 us -> 14.8 us  [call(): pl.pallas_call(kernel, out_shape=out_shape, scratch_shapes=[pltpu.VMEM(sh...]
  transfers between devices with their start and end apart: 4 -> 5, of which waited for: 4 -> 5; matrix products, arithmetic and copies ran while one was open for 10% -> 11% of each run, Pallas kernels for 0% -> 0%
where the time goes in v3:
time: 132 us
  waiting for transfers between devices  52.7 us (40%)
  starting transfers between devices  34.5 us (26%)
  Pallas kernels  14.8 us (11%)
  blocking collectives  8.45 us (6%)
  matrix products  7.85 us (6%)
  other arithmetic  7.14 us (5%)
  local copies, waits for them, and re-layouts  5.82 us (4%)
    all_to_all x2, waiting for transfers between devices, exchange(): return lax.all_to_all(x, PLANE, 0, 0, tiled=True)  22.3 us
    all_to_all x1, waiting for transfers between devices, local(): cols = lax.all_to_all(sent, EVERY, 0, 0, tiled=True)  16.5 us
    pallas_call x5, Pallas kernels, call(): pl.pallas_call(kernel, out_shape=out_shape, scratch_shapes=[pltpu.VMEM(sh...  14.8 us
    all_to_all x1, starting transfers between devices, local(): cols = lax.all_to_all(sent, EVERY, 0, 0, tiled=True)  14 us
    all_to_all x1, waiting for transfers between devices, local(): lines = lax.all_to_all(cols, EVERY, 0, 0, tiled=True)  12.7 us
    all_to_all x2, starting transfers between devices, exchange(): return lax.all_to_all(x, PLANE, 0, 0, tiled=True)  8.97 us
    all_to_all x1, blocking collectives, local(): lax.all_to_all(gradient, WAVE, 0, 0, tiled=True)  8.45 us
    dot_general x1, matrix products, slope_rows(): jnp.einsum('mich,hj->mjic', slope.astype(jnp.bfloat16), w_out, preferred_...  6.45 us
  transfers between devices with their start and end apart: 5, of which 5 were waited for; matrix products, arithmetic and copies ran while one was open for 11% of the time, Pallas kernels for 0%

profile of v3, /device:TPU:1, one launch (start us, length us, event | category | flops | bytes accessed | tf_op | source)
XLA Modules:
  0.0 131.6 jit_solution(13516497324686941681)
XLA Ops:
  0.1 1.6 %add_bitcast_fusion = f32[8,8,256]{2,1,0:T(8,128)} fusion(f32[64,256]{1,0:T(8,128)} %param.20, s32[64,256]{1,0:T(8,128)} %param.19), kind=kLoop, calls=%fused_computation.34 | loop fusion | flops 65536 | bytes 196608 | tf_op jit(solution)/shard_map/reshape | solution.py:392
  1.6 5.9 %all-to-all-start = ((f32[8,8,256]{2,1,0:T(8,128)}), f32[8,8,256]{2,1,0:T(8,128)S(1)}, u32[]{:S(2)}, u32[]{:S(2)}) async-start(f32[8,8,256]{2,1,0:T(8,128)} %add_bitcast_fusion), calls=%async_computation | async-start | bytes 131072 | tf_op jit(solution)/shard_map/all_to_all | solution.py:393
  7.7 0.7 broadcast_multiply_fusion.1
  8.3 0.7 broadcast_multiply_fusion
  9.0 1.1 multiply_reduce_fusion.1
  10.3 0.7 multiply_add_fusion
  11.0 0.7 multiply_subtract_fusion
  11.7 1.1 all-to-all-done.x_ref
  13.1 5.6 %first.1 = bf16[2048,128]{1,0:T(8,128)(2,1)} custom-call(f32[8,8,256]{2,1,0:T(8,128)S(1)} %all-to-all-done.x_ref, f32[256,128]{1,0:T(8,128)S(1)} %broadcast_in_dim.22.a_ref, f32[256,128]{1,0:T(8,128)S(1)} %broadcast_in_dim.23.b_ref, bf16[16,256]{1,0:T(8,128)(2,1)S(1)} %bitcast.48, f32[2,16,128]{2,1,0:T(8,128)S(1)} %broadcast_in_dim.24.m_ref, ...), custom_call_target="tpu_custom_call" | custom-call | flops 100000000 | bytes 1286144 | tf_op jit(solution)/shard_map/first/pallas_call | solution.py:322
  18.7 14.0 %all-to-all-start.1 = ((bf16[256,8,128]{2,1,0:T(8,128)(2,1)}), bf16[256,8,128]{2,1,0:T(8,128)(2,1)S(1)}, u32[]{:S(2)}, u32[]{:S(2)}) async-start(bf16[256,8,128]{2,1,0:T(8,128)(2,1)} %bitcast.4), calls=%async_computation.1 | async-start | bytes 1048576 | tf_op jit(solution)/shard_map/all_to_all | solution.py:426
  32.8 0.7 dynamic-slice_reduce_fusion
  33.7 2.2 %sine_multiply_fusion = (f32[32,32,128]{2,1,0:T(8,128)S(1)}, f32[32,32,128]{2,1,0:T(8,128)S(1)}) fusion(f32[128]{0:T(128)S(1)} %fusion.30, s32[32,128]{1,0:T(8,128)S(1)} %add_multiply_fusion, f32[]{:T(128)S(6)} %mul.282), kind=kLoop, calls=%fused_computation.12 | loop fusion | flops 2228224 | bytes 1065476 | tf_op jit(solution)/shard_map/mul | solution.py:355
  35.9 16.5 %all-to-all-done.1 = bf16[256,8,128]{2,1,0:T(8,128)(2,1)S(1)} async-done(((bf16[256,8,128]{2,1,0:T(8,128)(2,1)}), bf16[256,8,128]{2,1,0:T(8,128)(2,1)S(1)}, u32[]{:S(2)}, u32[]{:S(2)}) %all-to-all-start.1) | async-done | bytes 524320 | tf_op jit(solution)/shard_map/all_to_all | solution.py:426
  52.5 3.4 %filter.1 = bf16[32,64,128]{2,1,0:T(8,128)(2,1)} custom-call(bf16[2048,128]{1,0:T(8,128)(2,1)S(1)} %bitcast.46, f32[32,32,128]{2,1,0:T(8,128)S(1)} %get-tuple-element.10.kr_ref, f32[32,32,128]{2,1,0:T(8,128)S(1)} %get-tuple-element.9.ki_ref, f32[2,32,32,128]{3,2,1,0:T(8,128)S(1)} %copy-done.1, bf16[256,192]{1,0:T(8,128)(2,1)S(1)} %copy-done.3, ...), custom_call_target="tpu_custom_call" | custom-call | flops 100000000 | bytes 3342336 | tf_op jit(solution)/shard_map/filter/pallas_call | solution.py:322
  55.8 4.9 %all-to-all-start.2 = ((bf16[32,64,128]{2,1,0:T(8,128)(2,1)}), bf16[32,64,128]{2,1,0:T(8,128)(2,1)S(1)}, u32[]{:S(2)}, u32[]{:S(2)}) async-start(bf16[32,64,128]{2,1,0:T(8,128)(2,1)} %filter.1), calls=%async_computation.2 | async-start | bytes 1048576 | tf_op jit(solution)/shard_map/all_to_all | solution.py:459
  60.8 0.3 convolution_multiply_fusion
  61.2 11.0 %all-to-all-done.2.x_ref = bf16[32,64,128]{2,1,0:T(8,128)(2,1)S(1)} async-done(((bf16[32,64,128]{2,1,0:T(8,128)(2,1)}), bf16[32,64,128]{2,1,0:T(8,128)(2,1)S(1)}, u32[]{:S(2)}, u32[]{:S(2)}) %all-to-all-start.2) | async-done | bytes 524320 | tf_op jit(solution)/shard_map/all_to_all | solution.py:459
  72.1 0.7 broadcast_in_dim.28.c_ref
  72.9 1.0 copy-done.5
  73.9 0.9 copy-done.7
  74.8 1.8 %middle.1 = bf16[32,64,128]{2,1,0:T(8,128)(2,1)S(1)} custom-call(bf16[32,64,128]{2,1,0:T(8,128)(2,1)S(1)} %all-to-all-done.2.x_ref, f32[4,128]{1,0:T(4,128)S(1)} %broadcast_in_dim.28.c_ref, f32[32,32,128]{2,1,0:T(8,128)S(1)} %bitcast.45, f32[32,2,128]{2,1,0:T(2,128)S(1)} %copy-done.10, bf16[512,256]{1,0:T(8,128)(2,1)S(1)} %copy-done.7, ...), custom_call_target="tpu_custom_call" | custom-call | flops 100000000 | bytes 2263040 | tf_op jit(solution)/shard_map/middle/pallas_call | solution.py:322
  76.6 0.8 copy-done.2
  77.5 4.1 %all-to-all-start.3 = ((bf16[32,64,128]{2,1,0:T(8,128)(2,1)}), bf16[32,64,128]{2,1,0:T(8,128)(2,1)S(1)}, u32[]{:S(2)}, u32[]{:S(2)}) async-start(bf16[32,64,128]{2,1,0:T(8,128)(2,1)} %copy-done.2), calls=%async_computation.3 | async-start | bytes 1048576 | tf_op jit(solution)/shard_map/all_to_all | solution.py:459
  81.7 11.3 %all-to-all-done.3.x_ref = bf16[32,64,128]{2,1,0:T(8,128)(2,1)S(1)} async-done(((bf16[32,64,128]{2,1,0:T(8,128)(2,1)}), bf16[32,64,128]{2,1,0:T(8,128)(2,1)S(1)}, u32[]{:S(2)}, u32[]{:S(2)}) %all-to-all-start.3) | async-done | bytes 524320 | tf_op jit(solution)/shard_map/all_to_all | solution.py:459
  93.0 3.2 %filter_back.1 = bf16[2048,128]{1,0:T(8,128)(2,1)} custom-call(bf16[32,64,128]{2,1,0:T(8,128)(2,1)S(1)} %all-to-all-done.3.x_ref, f32[32,32,128]{2,1,0:T(8,128)S(1)} %get-tuple-element.10.kr_ref, f32[32,32,128]{2,1,0:T(8,128)S(1)} %get-tuple-element.9.ki_ref, f32[2,32,32,128]{3,2,1,0:T(8,128)S(1)} %copy-done.1, bf16[256,192]{1,0:T(8,128)(2,1)S(1)} %copy-done.3, ...), custom_call_target="tpu_custom_call" | custom-call | flops 100000000 | bytes 3342336 | tf_op jit(solution)/shard_map/filter_back/pallas_call | solution.py:322
  96.3 5.6 %all-to-all-start.4 = ((bf16[256,8,128]{2,1,0:T(8,128)(2,1)}), bf16[256,8,128]{2,1,0:T(8,128)(2,1)S(1)}, u32[]{:S(2)}, u32[]{:S(2)}) async-start(bf16[256,8,128]{2,1,0:T(8,128)(2,1)} %bitcast.17), calls=%async_computation.4 | async-start | bytes 1048576 | tf_op jit(solution)/shard_map/all_to_all | solution.py:464
  101.9 6.4 %fusion.1 = f32[8,16,8,256]{3,1,2,0:T(8,128)S(1)} fusion(f32[256]{0:T(256)S(1)} %copy-done.13, f32[256]{0:T(256)S(1)} %copy-done.12, f32[8,8,256]{2,1,0:T(8,128)S(1)} %all-to-all-done.x_ref, bf16[256,16]{0,1:T(8,128)(2,1)S(1)} %copy-done.11), kind=kOutput, calls=%fused_computation.3 | convolution fusion | flops 180355072 | bytes 1124352 | tf_op jit(solution)/shard_map/mich,hj->mjic/dot_general | solution.py:340
  108.3 0.6 copy.24
  108.9 12.7 %all-to-all-done.4 = bf16[256,8,128]{2,1,0:T(8,128)(2,1)S(1)} async-done(((bf16[256,8,128]{2,1,0:T(8,128)(2,1)}), bf16[256,8,128]{2,1,0:T(8,128)(2,1)S(1)}, u32[]{:S(2)}, u32[]{:S(2)}) %all-to-all-start.4) | async-done | bytes 524320 | tf_op jit(solution)/shard_map/all_to_all | solution.py:464
  121.7 0.8 last.1
  122.5 8.4 %all_to_all.42 = f32[8,8,256]{2,1,0:T(8,128)S(1)} all-to-all(f32[8,8,256]{2,1,0:T(8,128)S(1)} %last.1), channel_id=1, replica_groups=mesh['xl'=2,'y'=4,'xh'=2,'z'=8,'c'=2] {'xl','y'}, dimensions={0} | all-to-all | bytes 131072 | tf_op jit(solution)/shard_map/all_to_all | solution.py:476
  130.9 0.6 copy.34
  (53 shorter events, 1.0 us)
Async XLA Ops:
  0.0 7.6 %copy-start = (s32[8,64,2]{1,2,0:T(2,128)S(1)}, s32[8,64,2]{1,2,0:T(2,128)}, u32[]{:S(2)}) copy-start(s32[8,64,2]{1,2,0:T(2,128)} %param.21) | copy-start | bytes 12292
  0.0 10.1 %copy-start.14 = (f32[128]{0:T(128)S(1)}, f32[128]{0:T(128)}, u32[]{:S(2)}) copy-start(f32[128]{0:T(128)} %constant.196) | copy-start | bytes 1540
  0.0 13.0 %copy-start.9 = (f32[16,2,128]{2,1,0:T(2,128)S(1)}, f32[16,2,128]{2,1,0:T(2,128)}, u32[]{:S(2)}) copy-start(f32[16,2,128]{2,1,0:T(2,128)} %constant.192.clone.t_ref) | copy-start | bytes 49156
  0.0 13.0 %copy-start.6 = (bf16[768,256]{1,0:T(8,128)(2,1)S(1)}, bf16[768,256]{1,0:T(8,128)(2,1)}, u32[]{:S(2)}) copy-start(bf16[768,256]{1,0:T(8,128)(2,1)} %constant.188.clone.w_ref) | copy-start | bytes 1179652
  0.0 13.0 %copy-start.11 = (bf16[256,16]{0,1:T(8,128)(2,1)S(1)}, bf16[256,16]{0,1:T(8,128)(2,1)}, u32[]{:S(2)}) copy-start(bf16[256,16]{0,1:T(8,128)(2,1)} %param.24) | copy-start | bytes 24580
  0.0 11.6 %copy-start.15 = (f32[16]{0:T(128)S(1)}, f32[16]{0:T(128)}, u32[]{:S(2)}) copy-start(f32[16]{0:T(128)} %param.25) | copy-start | bytes 196
  1.6 11.1 %all-to-all-start = ((f32[8,8,256]{2,1,0:T(8,128)}), f32[8,8,256]{2,1,0:T(8,128)S(1)}, u32[]{:S(2)}, u32[]{:S(2)}) async-start(f32[8,8,256]{2,1,0:T(8,128)} %add_bitcast_fusion), calls=%async_computation | async-start | bytes 131072 | tf_op jit(solution)/shard_map/all_to_all | solution.py:393
  18.7 33.8 %copy-start.1 = (f32[2,32,32,128]{3,2,1,0:T(8,128)S(1)}, f32[2,32,32,128]{3,2,1,0:T(8,128)}, u32[]{:S(2)}) copy-start(f32[2,32,32,128]{3,2,1,0:T(8,128)} %constant.190.clone.t_ref) | copy-start | bytes 3145732
  18.7 33.8 %copy-start.3 = (bf16[256,192]{1,0:T(8,128)(2,1)S(1)}, bf16[256,192]{1,0:T(8,128)(2,1)}, u32[]{:S(2)}) copy-start(bf16[256,192]{1,0:T(8,128)(2,1)} %constant.184.clone.w_ref) | copy-start | bytes 294916
  18.7 33.8 %copy-start.4 = (bf16[256,192]{1,0:T(8,128)(2,1)S(1)}, bf16[256,192]{1,0:T(8,128)(2,1)}, u32[]{:S(2)}) copy-start(bf16[256,192]{1,0:T(8,128)(2,1)} %constant.185.clone.v_ref) | copy-start | bytes 294916
  18.7 33.8 %all-to-all-start.1 = ((bf16[256,8,128]{2,1,0:T(8,128)(2,1)}), bf16[256,8,128]{2,1,0:T(8,128)(2,1)S(1)}, u32[]{:S(2)}, u32[]{:S(2)}) async-start(bf16[256,8,128]{2,1,0:T(8,128)(2,1)} %bitcast.4), calls=%async_computation.1 | async-start | bytes 1048576 | tf_op jit(solution)/shard_map/all_to_all | solution.py:426
  55.8 17.0 %copy-start.10 = (f32[32,2,128]{2,1,0:T(2,128)S(1)}, f32[32,2,128]{2,1,0:T(2,128)}, u32[]{:S(2)}) copy-start(f32[32,2,128]{2,1,0:T(2,128)} %constant.191.clone.t_ref) | copy-start | bytes 98308
  55.8 16.3 %all-to-all-start.2 = ((bf16[32,64,128]{2,1,0:T(8,128)(2,1)}), bf16[32,64,128]{2,1,0:T(8,128)(2,1)S(1)}, u32[]{:S(2)}, u32[]{:S(2)}) async-start(bf16[32,64,128]{2,1,0:T(8,128)(2,1)} %filter.1), calls=%async_computation.2 | async-start | bytes 1048576 | tf_op jit(solution)/shard_map/all_to_all | solution.py:459
  72.9 1.0 copy-start.5
  73.9 0.9 copy-start.7
  76.6 0.8 copy-start.2
  77.4 4.1 %copy-start.16 = (f32[8]{0:T(128)S(1)}, f32[8]{0:T(128)}, u32[]{:S(2)}) copy-start(f32[8]{0:T(128)} %get-tuple-element.13) | copy-start | bytes 100
  77.4 4.1 %copy-start.17 = (f32[8]{0:T(128)S(1)}, f32[8]{0:T(128)}, u32[]{:S(2)}) copy-start(f32[8]{0:T(128)} %get-tuple-element.5) | copy-start | bytes 100
  77.5 15.6 %all-to-all-start.3 = ((bf16[32,64,128]{2,1,0:T(8,128)(2,1)}), bf16[32,64,128]{2,1,0:T(8,128)(2,1)S(1)}, u32[]{:S(2)}, u32[]{:S(2)}) async-start(bf16[32,64,128]{2,1,0:T(8,128)(2,1)} %copy-done.2), calls=%async_computation.3 | async-start | bytes 1048576 | tf_op jit(solution)/shard_map/all_to_all | solution.py:459
  96.3 5.6 %copy-start.12 = (f32[256]{0:T(256)S(1)}, f32[256]{0:T(256)}, u32[]{:S(2)}) copy-start(f32[256]{0:T(256)} %param.22) | copy-start | bytes 3076
  96.3 5.6 %copy-start.13 = (f32[256]{0:T(256)S(1)}, f32[256]{0:T(256)}, u32[]{:S(2)}) copy-start(f32[256]{0:T(256)} %param.23) | copy-start | bytes 3076
  96.3 25.4 %all-to-all-start.4 = ((bf16[256,8,128]{2,1,0:T(8,128)(2,1)}), bf16[256,8,128]{2,1,0:T(8,128)(2,1)S(1)}, u32[]{:S(2)}, u32[]{:S(2)}) async-start(bf16[256,8,128]{2,1,0:T(8,128)(2,1)} %bitcast.17), calls=%async_computation.4 | async-start | bytes 1048576 | tf_op jit(solution)/shard_map/all_to_all | solution.py:464
  108.3 13.4 %copy-start.8 = (bf16[512,256]{1,0:T(8,128)(2,1)S(1)}, bf16[512,256]{1,0:T(8,128)(2,1)}, u32[]{:S(2)}) copy-start(bf16[512,256]{1,0:T(8,128)(2,1)} %constant.189.clone.v_ref) | copy-start | bytes 786436

commit v4 on v3

--- a/solution.py
+++ b/solution.py
@@ -14,6 +14,9 @@
 LEVELS = 16
 WAVES = 8
 SIDE = 2048
+FOCAL = 128.0
+SPOT_LEVEL = 256.0
+SPOTS_MEAN = SPOT_LEVEL * 64 / (SIDE * SIDE)
 FIRST = 32
 SECOND = 64
 LANES = 2 * SECOND
@@ -25,6 +28,8 @@
 PLANE = ("xh", "c", "xl", "y")
 EVERY = ("xh", "z", "c", "xl", "y")
 VMEM_LIMIT = 16 * 2**20
+COPIES = {'filter': 0, 'middle': 0}
+FLOPS = {'prepare': 20000000000, 'first': 100000000, 'filter': 100000000, 'middle': 6000000000, 'spots': 20000000000}
 
 
 def split_np(table):
@@ -88,6 +93,9 @@
     place = np.arange(ROWS)[:, None] + ROWS * (np.arange(LANES) // SECOND)[None, :]
     angle = -2.0 * math.pi / SIDE * (np.arange(FIRST)[:, None, None] * place[None])
     return np.stack([np.cos(angle), np.sin(angle)]).astype(np.float32)
+
+
+WHOLE_TURN = FIRST
 
 
 def left_lanes():
@@ -132,6 +140,25 @@
     return jnp.dot(left, right, preferred_element_type=jnp.float32)
 
 
+class Writer:
+    def __init__(self, out_ref, keep):
+        self.out_ref = out_ref
+        self.keep_ref = keep[0] if keep else out_ref
+        self.sems = keep[1] if keep else None
+        self.copies = []
+
+    def send(self, *place):
+        if self.sems is not None:
+            sem = self.sems.at[len(self.copies)]
+            copy = pltpu.make_async_copy(self.keep_ref.at[place], self.out_ref.at[place], sem)
+            copy.start()
+            self.copies.append(copy)
+
+    def wait(self):
+        for copy in self.copies:
+            copy.wait()
+
+
 def load_groups(x_ref, g):
     real = [x_ref[a, g : g + 16, :].astype(jnp.float32) for a in range(FIRST)]
     imag = [x_ref[a, ROWS + g : ROWS + g + 16, :].astype(jnp.float32) for a in range(FIRST)]
@@ -168,21 +195,48 @@
     return real * cos + imag * sin, imag * cos - real * sin
 
 
-def first_kernel(x_ref, a_ref, b_ref, o_ref, m_ref, t_ref, w_ref, out_ref, h_ref, y_ref):
-    def block(m, carry):
+def column(row):
+    return jnp.transpose(jnp.broadcast_to(row, (LANES, row.shape[1])))
+
+
+def constants_of(values, shares, dc_ref, c_ref):
+    mean = jnp.sum(values * shares, axis=1, keepdims=True)
+    spread = jnp.sum((values - mean) ** 2 * shares, axis=1, keepdims=True)
+    mean = jnp.broadcast_to(mean, (2 * WAVES, LANES))
+    mean_re, mean_im = mean[:WAVES], mean[WAVES:]
+    noise = jnp.broadcast_to(spread[:WAVES] + spread[WAVES:], (WAVES, LANES))
+    dc_re, dc_im = dc_ref[0], dc_ref[1]
+    field_re, field_im = turn(mean_re, mean_im, dc_re, dc_im)
+    gain = (field_re * field_re + field_im * field_im + 2.0 * noise - SPOTS_MEAN) * (1.0 / WAVES)
+    adj_re, adj_im = gain * field_re, gain * field_im
+    back = turn_back(adj_re, adj_im, dc_re, dc_im)
+    for i, part in enumerate((field_re, field_im, adj_re, adj_im) + back):
+        c_ref[i * WAVES : (i + 1) * WAVES, :] = part
+    return mean
+
+
+def prepare_kernel(p_ref, q_ref, b_ref, o_ref, u_ref, dc_ref, s_ref, m_ref, c_ref):
+    scale, shift = 0.5 * column(p_ref[...]), 0.5 * column(q_ref[...])
+    bias = column(b_ref[...])
+    s_ref[0], s_ref[1], m_ref[0] = scale, shift, bias
+    half = u_ref[0:1, :] * scale + shift
+    usual = matmul(o_ref[...], (half + half * jnp.tanh(half)).astype(jnp.bfloat16)) + bias
+    m_ref[1] = constants_of(usual, u_ref[1:2, :], dc_ref, c_ref)
+
+
+def first_kernel(x_ref, s_ref, m_ref, o_ref, t_ref, w_ref, out_ref, h_ref, y_ref):
+    def hidden(row):
+        half = row * s_ref[0] + s_ref[1]
+        return (half + half * jnp.tanh(half)).astype(jnp.bfloat16)
+
+    for m in range(WAVES):
         for i in range(GROUP):
-            tiles = []
-            for tile in range(2):
-                half = x_ref[m, i : i + 1, tile * LANES : (tile + 1) * LANES] * a_ref[...] + b_ref[...]
-                tiles.append((half + half * jnp.tanh(half)).astype(jnp.bfloat16))
+            tiles = [hidden(x_ref[m, i : i + 1, tile * LANES : (tile + 1) * LANES]) for tile in range(2)]
             mixed = matmul(o_ref[...], jnp.concatenate(tiles, 1))
             for tile in range(2):
                 part = mixed[:, tile * LANES : (tile + 1) * LANES] + m_ref[0]
                 part = part.astype(jnp.bfloat16).astype(jnp.float32) - m_ref[1]
                 h_ref[2 * m + tile, pl.ds(i, 2 * WAVES, stride=GROUP), :] = part
-        return carry
-
-    lax.fori_loop(0, WAVES, block, 0)
     for w in range(WAVES):
         rows_re, rows_im = slice(w * GROUP, (w + 1) * GROUP), slice((WAVES + w) * GROUP, (WAVES + w + 1) * GROUP)
         real, imag = dft(
@@ -190,45 +244,53 @@
         )
         for k in range(OUTER):
             rows = slice((w * OUTER + k) * GROUP, (w * OUTER + k + 1) * GROUP)
-            y_ref[rows, :LANES], y_ref[rows, LANES:] = turn(real[k], imag[k], t_ref[k, 0:1, :], t_ref[k, 1:2, :])
+            y_ref[rows, :LANES], y_ref[rows, LANES:] = turn(
+                real[k], imag[k], t_ref[WHOLE_TURN + k, 0:1, :], t_ref[WHOLE_TURN + k, 1:2, :]
+            )
     step = 256
     for r in range(0, 1024, step):
         high, low = split_pair(y_ref[r : r + step])
         both = matmul(jnp.concatenate([high, low, high], 1), w_ref[...]).astype(jnp.bfloat16)
-        out_ref[r : r + step] = both[:, :LANES]
-        out_ref[1024 + r : 1024 + r + step] = both[:, LANES:]
-
-
-def last_kernel(x_ref, c_ref, d_ref, t_ref, v_ref, out_ref, y_ref):
+        for h in range(2):
+            rows = slice(h * 1024 + r, h * 1024 + r + step)
+            out_ref[rows] = both[:, h * LANES : (h + 1) * LANES]
+
+
+def last_kernel(x_ref, c_ref, d_ref, t_ref, w_ref, out_ref, y_ref):
     step = 256
     for r in range(0, 1024, step):
         data = jnp.concatenate([x_ref[r : r + step], x_ref[1024 + r : 1024 + r + step]], 1)
-        y_ref[r : r + step] = matmul(jnp.concatenate([data, data], 1), v_ref[...])
+        y_ref[r : r + step] = matmul(jnp.concatenate([data, data], 1), w_ref[...])
     for a in range(OUTER):
-        out_ref[a // 2, :, (a % 2) * LANES : (a % 2 + 1) * LANES] = jnp.zeros((GROUP, LANES), jnp.float32)
+        out_ref[(a // 2) * GROUP : (a // 2 + 1) * GROUP, (a % 2) * LANES : (a % 2 + 1) * LANES] = jnp.zeros(
+            (GROUP, LANES), jnp.float32
+        )
     for w in range(WAVES):
         real, imag = [], []
         for k in range(OUTER):
             rows = slice((w * OUTER + k) * GROUP, (w * OUTER + k + 1) * GROUP)
-            re, im = turn_back(y_ref[rows, :LANES], y_ref[rows, LANES:], t_ref[k, 0:1, :], t_ref[k, 1:2, :])
+            re, im = turn_back(
+                y_ref[rows, :LANES], y_ref[rows, LANES:], t_ref[WHOLE_TURN + k, 0:1, :], t_ref[WHOLE_TURN + k, 1:2, :]
+            )
             real.append(re)
             imag.append(im)
         real, imag = dft(real, imag, 1.0)
         for a in range(OUTER):
             lanes = slice((a % 2) * LANES, (a % 2 + 1) * LANES)
-            total = out_ref[a // 2, :, lanes]
+            place = slice((a // 2) * GROUP, (a // 2 + 1) * GROUP)
+            total = out_ref[place, lanes]
             for j, part in ((w, real[a]), (WAVES + w, imag[a])):
-                cotangent = (part + c_ref[j : j + 1, :]).astype(jnp.bfloat16).astype(jnp.float32)
+                cotangent = (part + c_ref[4 * WAVES + j : 4 * WAVES + j + 1, :]).astype(jnp.bfloat16).astype(jnp.float32)
                 total = total + cotangent * d_ref[a // 2, j * GROUP : (j + 1) * GROUP, lanes]
-            out_ref[a // 2, :, lanes] = total
+            out_ref[place, lanes] = total
 
 
 def load_lanes(x_ref, g):
     left = left_lanes()
     real, imag = [], []
     for a in range(FIRST):
-        top = x_ref[a * SECOND + g : a * SECOND + g + 16, :].astype(jnp.float32)
-        low = x_ref[a * SECOND + ROWS + g : a * SECOND + ROWS + g + 16, :].astype(jnp.float32)
+        top = x_ref[a, g : g + 16, :].astype(jnp.float32)
+        low = x_ref[a, ROWS + g : ROWS + g + 16, :].astype(jnp.float32)
         real.append(jnp.where(left, top, swap(low)))
         imag.append(jnp.where(left, swap(top), low))
     return [([r[h : h + 8] for r in real], [i[h : h + 8] for i in imag]) for h in (0, 8)]
@@ -239,20 +301,18 @@
     for a in range(FIRST):
         real = jnp.concatenate([halves[0][0][a], halves[1][0][a]], 0)
         imag = jnp.concatenate([halves[0][1][a], halves[1][1][a]], 0)
-        top = jnp.where(left, real, swap(imag)).astype(jnp.bfloat16)
-        low = jnp.where(left, swap(real), imag).astype(jnp.bfloat16)
-        out_ref[a * SECOND + g : a * SECOND + g + 16, :] = top
-        out_ref[a * SECOND + ROWS + g : a * SECOND + ROWS + g + 16, :] = low
-
-
-def col_step(parts, w_ref):
+        out_ref[a, g : g + 16, :] = jnp.where(left, real, swap(imag)).astype(jnp.bfloat16)
+        out_ref[a, ROWS + g : ROWS + g + 16, :] = jnp.where(left, swap(real), imag).astype(jnp.bfloat16)
+
+
+def col_step(parts, table):
     data = jnp.concatenate([jnp.concatenate(part, 0) for part in parts], 1)
     high, low = split_pair(data)
-    both = matmul(w_ref[...], jnp.concatenate([high, low, high], 0))
+    both = matmul(table, jnp.concatenate([high, low, high], 0))
     return [join_halves(both[:, i * LANES : (i + 1) * LANES]) for i in range(len(parts))]
 
 
-def col_kernel(conjugate, x_ref, kr_ref, ki_ref, t_ref, w_ref, v_ref, out_ref, y_ref):
+def col_kernel(conjugate, x_ref, kr_ref, ki_ref, t_ref, w_ref, v_ref, out_ref, y_ref, *keep):
     for g in range(0, ROWS, 16):
         halves = load_groups(x_ref, g) if conjugate else load_lanes(x_ref, g)
         for h, (real, imag) in enumerate(halves):
@@ -263,26 +323,31 @@
                     real[k], imag[k], t_ref[0, k, rows, :], t_ref[1, k, rows, :]
                 )
     for k in range(0, FIRST, 2):
-        parts = col_step([(y_ref[0, k + i], y_ref[1, k + i]) for i in range(2)], w_ref)
+        parts = col_step([(y_ref[0, k + i], y_ref[1, k + i]) for i in range(2)], w_ref[...])
         for i in range(2):
             turned = turn_back if conjugate else turn
             parts[i] = turned(parts[i][0], parts[i][1], kr_ref[k + i], ki_ref[k + i])
-        parts = col_step(parts, v_ref)
+        parts = col_step(parts, v_ref[...])
         for i in range(2):
             y_ref[0, k + i], y_ref[1, k + i] = turn_back(
                 parts[i][0], parts[i][1], t_ref[0, k + i], t_ref[1, k + i]
             )
+    writer = Writer(out_ref, keep)
     for g in range(0, ROWS, 16):
         halves = [dft(*parts_of(y_ref, slice(g + h, g + h + 8)), 1.0) for h in (0, 8)]
         if conjugate:
-            store_lanes(out_ref, g, halves)
+            store_lanes(writer.keep_ref, g, halves)
         else:
-            store_groups(out_ref, g, halves)
-
-
-def middle_kernel(x_ref, c_ref, s_ref, t_ref, v_ref, w_ref, out_ref, y_ref):
-    field_re, field_im = c_ref[0:1, :], c_ref[1:2, :]
-    mean_re, mean_im = c_ref[2:3, :], c_ref[3:4, :]
+            store_groups(writer.keep_ref, g, halves)
+        for start in (g, ROWS + g):
+            place = (slice(None), slice(start, start + 16))
+            writer.send(*place)
+    writer.wait()
+
+
+def middle_kernel(x_ref, c_ref, s_ref, t_ref, w_ref, v_ref, out_ref, y_ref, *keep):
+    wave = lax.axis_index("z")
+    field_re, field_im, mean_re, mean_im = [c_ref[pl.ds(i * WAVES + wave, 1), :] for i in range(4)]
     step = 8
     rows = step * ROWS
     for k in range(0, FIRST, step):
@@ -307,6 +372,7 @@
             y_ref[0, k, part, :], y_ref[1, k, part, :] = turn(
                 real[k], imag[k], t_ref[k, 0:1, :], t_ref[k, 1:2, :]
             )
+    writer = Writer(out_ref, keep)
     for k in range(0, FIRST, step):
         real = y_ref[0, k : k + step].reshape(rows, LANES)
         imag = y_ref[1, k : k + step].reshape(rows, LANES)
@@ -314,17 +380,30 @@
         both = matmul(jnp.concatenate([high, low, high], 1), w_ref[...]).astype(jnp.bfloat16)
         for i in range(step):
             part = slice(i * ROWS, (i + 1) * ROWS)
-            out_ref[k + i] = jnp.concatenate([both[part, :LANES], both[part, LANES:]], 0)
-
-
-def call(kernel, out_shape, scratch, *args, name=None):
-    size = sum(a.size * a.dtype.itemsize for a in args) + math.prod(out_shape.shape) * out_shape.dtype.itemsize
+            writer.keep_ref[k + i] = jnp.concatenate([both[part, :LANES], both[part, LANES:]], 0)
+        writer.send(slice(k, k + step))
+    writer.wait()
+
+
+def spots_kernel(near_ref, far_ref, out_ref):
+    out_ref[...] = (SPOT_LEVEL * matmul(near_ref[...], far_ref[...])).reshape(FIRST, ROWS, LANES)
+
+
+def call(kernel, out_shape, scratch, copies, *args, flops=10**8, size=None, limit=VMEM_LIMIT, name=None):
+    outs = out_shape if isinstance(out_shape, tuple) else (out_shape,)
+    if size is None:
+        size = sum(a.size * a.dtype.itemsize for a in args + outs)
+    shapes = [pltpu.VMEM(shape, jnp.float32) for shape in scratch]
+    if copies:
+        shapes += [pltpu.VMEM(out_shape.shape, out_shape.dtype), pltpu.SemaphoreType.DMA((copies,))]
+    where = pl.BlockSpec(memory_space=pltpu.HBM if copies else pltpu.VMEM)
     return pl.pallas_call(
         kernel,
         out_shape=out_shape,
-        scratch_shapes=[pltpu.VMEM(shape, jnp.float32) for shape in scratch],
-        compiler_params=pltpu.CompilerParams(vmem_limit_bytes=VMEM_LIMIT),
-        cost_estimate=pl.CostEstimate(flops=10**8, bytes_accessed=size, transcendentals=0),
+        out_specs=(where,) * len(outs) if isinstance(out_shape, tuple) else where,
+        scratch_shapes=shapes,
+        compiler_params=pltpu.CompilerParams(vmem_limit_bytes=limit),
+        cost_estimate=pl.CostEstimate(flops=flops, bytes_accessed=size, transcendentals=0),
         name=name,
     )(*args)
 
@@ -355,18 +434,18 @@
     return (amplitude * jnp.cos(phase_angle), amplitude * jnp.sin(phase_angle))
 
 
-def usual_transmission(w_in, b_in, w_out, b_out):
+def usual_widths():
     nodes, weights = np.polynomial.hermite_e.hermegauss(8)
-    weights = weights / weights.sum()
     shifts = np.clip(0.1 * nodes, -0.3, 0.3)
     places = (0.3 + 0.4 * np.arange(LEVELS)[:, None] / (LEVELS - 1) + shifts[None, :]).reshape(-1)
-    shares = np.tile(weights / LEVELS, LEVELS).astype(np.float32)
-    pre_act = places.astype(np.float32)[:, None] * w_in[None, :] + b_in[None, :]
-    hidden = pre_act * jax.nn.sigmoid(pre_act)
-    values = jnp.dot(hidden, w_out.astype(jnp.float32)) + b_out
-    mean = jnp.sum(values * shares[:, None], 0)
-    spread = jnp.sum((values - mean) ** 2 * shares[:, None], 0)
-    return mean, spread
+    shares = np.tile(weights / weights.sum() / LEVELS, LEVELS)
+    return np.stack([places, shares]).astype(np.float32)
+
+
+def dc_turns():
+    angle = FOCAL * 2.0 * math.pi / (1.5 + np.arange(WAVES) / (WAVES - 1))
+    turns = np.stack([np.cos(angle), np.sin(angle)]).astype(np.float32)
+    return np.ascontiguousarray(np.broadcast_to(turns[:, :, None], (2, WAVES, LANES)))
 
 
 def local(levels, offsets, targets, w_in, b_in, w_out, b_out):
@@ -376,8 +455,6 @@
     lined = jax.ShapeDtypeStruct((SIDE, LANES), jnp.bfloat16)
     wave_index = lax.axis_index("z")
     plane_index = lax.axis_index(PLANE)
-    focal_length = float(SIDE // 16)
-    spot_level = float(SIDE // 8)
     forward_cols = jnp.asarray(col_tables(-1.0))
     inverse_cols = jnp.asarray(col_tables(1.0))
     forward_rows = jnp.asarray(row_tables(-1.0))
@@ -385,42 +462,46 @@
     forward_whole = jnp.asarray(whole_row_tables(-1.0))
     inverse_whole = jnp.asarray(whole_row_tables(1.0))
     turns_cols = jnp.asarray(col_twiddles())
-    turns_rows = jnp.asarray(row_twiddles())
-    turns_whole = jnp.asarray(whole_row_twiddles())
+    turns_rows = jnp.asarray(np.concatenate([row_twiddles(), whole_row_twiddles()], 0))
 
     rows_here, cols_here = levels.shape
-    widths = level_widths(levels, offsets).reshape(WAVES, GROUP, cols_here)
-    widths = lax.all_to_all(widths, WAVE, 0, 0, tiled=True)
-
-    mean, spread = usual_transmission(w_in, b_in, w_out, b_out)
-    mean_re, mean_im = mean[:WAVES], mean[WAVES:]
-    noise = spread[:WAVES] + spread[WAVES:]
-    wavelengths = 1.5 + jnp.arange(WAVES, dtype=jnp.int32).astype(jnp.float32) / (WAVES - 1)
-    zero = jnp.zeros((), jnp.float32)
-    dc_re, dc_im = transfer(wavelengths, zero, zero, focal_length)
-    field_re = mean_re * dc_re - mean_im * dc_im
-    field_im = mean_re * dc_im + mean_im * dc_re
-    spots_mean = spot_level * targets.shape[1] / (SIDE * SIDE)
-    gain = (field_re * field_re + field_im * field_im + 2.0 * noise - spots_mean) / WAVES
-    adj_re = gain * field_re
-    adj_im = gain * field_im
-    back = jnp.concatenate([adj_re * dc_re + adj_im * dc_im, adj_im * dc_re - adj_re * dc_im])
-    back = jnp.broadcast_to(back[:, None], (2 * WAVES, LANES))
-    own = lax.dynamic_index_in_dim(jnp.stack([field_re, field_im, adj_re, adj_im]), wave_index, 1, keepdims=True)
-    own = jnp.broadcast_to(own, (4, LANES))
-    shifts = jnp.broadcast_to(jnp.stack([b_out, mean])[:, :, None], (2, 2 * WAVES, LANES))
+    widths = lax.all_to_all(level_widths(levels, offsets), WAVE, 0, 0, tiled=True)
+    widths = widths.reshape(WAVES, GROUP, cols_here)
+
+    each = 2 * WAVES
+    pairs, moments, consts = call(
+        prepare_kernel,
+        (
+            jax.ShapeDtypeStruct((2, w_in.shape[0], LANES), jnp.float32),
+            jax.ShapeDtypeStruct((2, each, LANES), jnp.float32),
+            jax.ShapeDtypeStruct((3 * each, LANES), jnp.float32),
+        ),
+        [],
+        0,
+        w_in.reshape(1, -1),
+        b_in.reshape(1, -1),
+        b_out.reshape(1, -1),
+        w_out.T,
+        jnp.asarray(usual_widths()),
+        jnp.asarray(dc_turns()),
+        flops=FLOPS["prepare"],
+        size=0,
+        limit=63 * 2**20,
+        name="prepare",
+    )
 
     sent = call(
         first_kernel,
         lined,
-        [(OUTER, 2 * WAVES * GROUP, LANES), (1024, 2 * LANES)],
+        [(OUTER, each * GROUP, LANES), (1024, 2 * LANES)],
+        0,
         widths,
-        jnp.broadcast_to(0.5 * w_in[:, None], (w_in.shape[0], LANES)),
-        jnp.broadcast_to(0.5 * b_in[:, None], (b_in.shape[0], LANES)),
+        pairs,
+        moments,
         w_out.T,
-        shifts,
-        turns_whole,
+        turns_rows,
         forward_whole,
+        flops=FLOPS["first"],
         name="first",
     )
     cols = lax.all_to_all(sent, EVERY, 0, 0, tiled=True)
@@ -431,7 +512,7 @@
     kx = signed_kappa(first[:, None, None] + FIRST * row[None])
     ky = signed_kappa(plane_index + FIRST * (lane % SECOND))
     wavelength = 1.5 + wave_index.astype(jnp.float32) / (WAVES - 1)
-    kern_re, kern_im = transfer(wavelength, kx, ky[None, None, :], focal_length)
+    kern_re, kern_im = transfer(wavelength, kx, ky[None, None, :], FOCAL)
 
     own_targets = lax.dynamic_index_in_dim(targets, wave_index, 0, keepdims=False)
     place_row = plane_index * SECOND + jnp.arange(ROWS, dtype=jnp.int32)
@@ -444,36 +525,71 @@
         far.append(hit_col & (lane // SECOND == half)[None, :])
     near = jnp.concatenate(near, 1).astype(jnp.bfloat16)
     far = jnp.concatenate(far, 0).astype(jnp.bfloat16)
-    spots = spot_level * jnp.dot(near, far, preferred_element_type=jnp.float32)
-    spots = spots.reshape(FIRST, ROWS, LANES)
+    spots = call(
+        spots_kernel,
+        jax.ShapeDtypeStruct((FIRST, ROWS, LANES), jnp.float32),
+        [],
+        0,
+        near,
+        far,
+        flops=FLOPS["spots"],
+        name="spots",
+    )
 
     slopes = slope_rows(widths, w_in, b_in, w_out).reshape(WAVES, 2 * WAVES * GROUP, cols_here)
-
-    def filtered(x, out_shape, conjugate, name):
+    together = (cols, kern_re, kern_im, spots, consts, slopes)
+    cols, kern_re, kern_im, spots, consts, slopes = lax.optimization_barrier(together)
+
+    def filtered(x, conjugate, name):
         kernel = functools.partial(col_kernel, conjugate)
         return call(
-            kernel, out_shape, [halves], x, kern_re, kern_im, turns_cols, forward_cols, inverse_cols, name=name
+            kernel,
+            packed,
+            [halves],
+            COPIES["filter"],
+            x.reshape(block),
+            kern_re,
+            kern_im,
+            turns_cols,
+            forward_cols,
+            inverse_cols,
+            flops=FLOPS["filter"],
+            name=name,
         )
 
     def exchange(x):
         return lax.all_to_all(x, PLANE, 0, 0, tiled=True)
 
-    rows = exchange(filtered(cols, packed, False, "filter"))
-    rows = call(middle_kernel, packed, [halves], rows, own, spots, turns_rows, inverse_rows, forward_rows, name="middle")
-    cols = filtered(exchange(rows), lined, True, "filter_back")
+    rows = exchange(filtered(cols, False, "filter"))
+    rows = call(
+        middle_kernel,
+        packed,
+        [halves],
+        COPIES["middle"],
+        rows,
+        consts,
+        spots,
+        turns_rows,
+        forward_rows,
+        inverse_rows,
+        flops=FLOPS["middle"],
+        name="middle",
+    )
+    cols = filtered(exchange(rows), True, "filter_back").reshape(SIDE, LANES)
     lines = lax.all_to_all(cols, EVERY, 0, 0, tiled=True)
     gradient = call(
         last_kernel,
-        jax.ShapeDtypeStruct((WAVES, GROUP, cols_here), jnp.float32),
+        jax.ShapeDtypeStruct((rows_here, cols_here), jnp.float32),
         [(1024, 2 * LANES)],
+        0,
         lines,
-        back,
+        consts,
         slopes,
-        turns_whole,
+        turns_rows,
         inverse_whole,
         name="last",
     )
-    return lax.all_to_all(gradient, WAVE, 0, 0, tiled=True).reshape(rows_here, cols_here)
+    return lax.all_to_all(gradient, WAVE, 0, 0, tiled=True)
 
 
 def solution(mesh):

time: 132 us -> 125 us (0.947)
  blocking collectives: 8.45 us -> 64.7 us
  waiting for transfers between devices: 52.7 us -> 11.6 us
  starting transfers between devices: 34.5 us -> 21.1 us
  local copies, waits for them, and re-layouts: 5.82 us -> 2.33 us
  other arithmetic: 7.14 us -> 4.34 us
  matrix products: 7.85 us -> 6.44 us
    all_to_all x1 -> x4, blocking collectives: 8.45 us -> 64.7 us  [the longest x2 30.9 us: exchange(): return lax.all_to_all(x, PLANE, 0, 0, tiled=True)]
    all_to_all x4 -> x1, waiting for transfers between devices: 36.2 us -> 0.01 us  [local(): lax.all_to_all(level_widths(levels, offsets), WAVE, 0, 0, tiled=True)]
    all_to_all x4 -> x1, starting transfers between devices: 20.5 us -> 5.95 us  [local(): lax.all_to_all(level_widths(levels, offsets), WAVE, 0, 0, tiled=True)]
    all_to_all x1, waiting for transfers between devices: 16.5 us -> 11.6 us  [local(): cols = lax.all_to_all(sent, EVERY, 0, 0, tiled=True)]
    unnamed x37, local copies, waits for them, and re-layouts: 3.46 us -> 0.72 us
    reshape x1 -> x0, other arithmetic: 1.58 us -> none  [local(): widths = level_widths(levels, offsets).reshape(WAVES, GROUP, cols_here)]
    all_to_all x0 -> x1, other arithmetic: none -> 1.53 us  [local(): lax.all_to_all(level_widths(levels, offsets), WAVE, 0, 0, tiled=True)]
    dot_general x2 -> x0, matrix products: 1.4 us -> none  [the longest x1 1.08 us: usual_transmission(): values = jnp.dot(hidden, w_out.astype(jnp.float32)) + b_out]
  transfers between devices with their start and end apart: 5 -> 2, of which waited for: 5 -> 1; matrix products, arithmetic and copies ran while one was open for 11% -> 9% of each run, Pallas kernels for 0% -> 2%
where the time goes in v4:
time: 125 us
  blocking collectives  64.7 us (52%)
  starting transfers between devices  21.1 us (17%)
  Pallas kernels  14 us (11%)
  waiting for transfers between devices  11.6 us (9%)
  matrix products  6.44 us (5%)
  other arithmetic  4.34 us (3%)
  local copies, waits for them, and re-layouts  2.33 us (2%)
    all_to_all x2, blocking collectives, exchange(): return lax.all_to_all(x, PLANE, 0, 0, tiled=True)  30.9 us
    all_to_all x1, blocking collectives, local(): lines = lax.all_to_all(cols, EVERY, 0, 0, tiled=True)  25.4 us
    all_to_all x1, starting transfers between devices, local(): cols = lax.all_to_all(sent, EVERY, 0, 0, tiled=True)  15.1 us
    pallas_call x7, Pallas kernels, call(): pl.pallas_call(kernel, out_shape=out_shape, out_specs=(where,) * len(outs...  14 us
    all_to_all x1, waiting for transfers between devices, local(): cols = lax.all_to_all(sent, EVERY, 0, 0, tiled=True)  11.6 us
    all_to_all x1, blocking collectives, local(): return lax.all_to_all(gradient, WAVE, 0, 0, tiled=True)  8.45 us
    dot_general x1, matrix products, slope_rows(): jnp.einsum('mich,hj->mjic', slope.astype(jnp.bfloat16), w_out, preferred_...  6.44 us
    all_to_all x1, starting transfers between devices, local(): lax.all_to_all(level_widths(levels, offsets), WAVE, 0, 0, tiled=True)  5.95 us
  transfers between devices with their start and end apart: 2, of which 1 were waited for; matrix products, arithmetic and copies ran while one was open for 9% of the time, Pallas kernels for 2%

profile of v4, /device:TPU:1, one launch (start us, length us, event | category | flops | bytes accessed | tf_op | source)
XLA Modules:
  0.0 124.9 jit_solution(3538851236560659634)
XLA Ops:
  0.0 1.5 %add_bitcast_fusion = f32[8,8,256]{2,1,0:T(8,128)} fusion(f32[64,256]{1,0:T(8,128)} %param.18, s32[64,256]{1,0:T(8,128)} %param.17), kind=kLoop, calls=%fused_computation.19 | loop fusion | flops 65536 | bytes 196608 | tf_op jit(solution)/shard_map/all_to_all | solution.py:468
  1.5 5.9 %all-to-all-start = ((f32[8,8,256]{2,1,0:T(8,128)}), f32[8,8,256]{2,1,0:T(8,128)S(1)}, u32[]{:S(2)}, u32[]{:S(2)}) async-start(f32[8,8,256]{2,1,0:T(8,128)} %add_bitcast_fusion), calls=%async_computation | async-start | bytes 131072 | tf_op jit(solution)/shard_map/all_to_all | solution.py:468
  7.7 0.1 compare_and_fusion.1
  7.8 0.1 broadcast_compare_fusion.1
  7.9 0.1 broadcast_and_fusion.1
  8.0 0.2 add_convert_fusion.near_ref
  8.2 0.2 spots.1.s_ref
  8.4 2.0 %prepare.1 = (f32[2,256,128]{2,1,0:T(8,128)}, f32[2,16,128]{2,1,0:T(8,128)}, f32[48,128]{1,0:T(8,128)}) custom-call(f32[1,256]{1,0:T(1,128)} %bitcast.49, f32[1,256]{1,0:T(1,128)} %bitcast.50, f32[1,16]{1,0:T(1,128)} %bitcast.51, bf16[16,256]{1,0:T(8,128)(2,1)} %bitcast.44, f32[2,128]{1,0:T(2,128)} %constant.166.clone.u_ref, f32[2,8,128]{2,1,0:T(8,128)} %constant.167.clone.dc_ref), custom_call_target="tpu_custom_call" | custom-call | flops 20000000000 | tf_op jit(solution)/shard_map/prepare/pallas_call | solution.py:400
  10.5 0.0 copy-start.8
  10.5 0.0 copy-start.11
  10.5 2.2 %sine_multiply_fusion = (f32[32,32,128]{2,1,0:T(8,128)S(1)}, f32[32,32,128]{2,1,0:T(8,128)S(1)}) fusion(f32[128]{0:T(128)S(1)} %fusion.13, s32[32,128]{1,0:T(8,128)S(1)} %add_multiply_fusion, f32[]{:T(128)S(6)} %mul.112), kind=kLoop, calls=%fused_computation.10 | loop fusion | flops 2228224 | bytes 1065476 | tf_op jit(solution)/shard_map/mul | solution.py:434
  12.7 0.0 all-to-all-done.x_ref
  12.8 0.0 copy-start.16
  12.8 0.0 copy-start.17
  12.8 4.7 %first.1 = bf16[2048,128]{1,0:T(8,128)(2,1)} custom-call(f32[8,8,256]{2,1,0:T(8,128)S(1)} %all-to-all-done.x_ref, f32[2,256,128]{2,1,0:T(8,128)S(1)} %copy-done.7, f32[2,16,128]{2,1,0:T(8,128)S(1)} %copy-done.10, bf16[16,256]{1,0:T(8,128)(2,1)S(1)} %bitcast.45, f32[48,2,128]{2,1,0:T(2,128)S(1)} %copy-done.8, bf16[768,256]{1,0:T(8,128)(2,1)S(1)} %copy-done.5), custom_call_target="tpu_custom_call" | custom-call | flops 100000000 | bytes 1318912 | tf_op jit(solution)/shard_map/first/pallas_call | solution.py:400
  17.5 15.1 %all-to-all-start.1 = ((bf16[256,8,128]{2,1,0:T(8,128)(2,1)}), bf16[256,8,128]{2,1,0:T(8,128)(2,1)S(1)}, u32[]{:S(2)}, u32[]{:S(2)}) async-start(bf16[256,8,128]{2,1,0:T(8,128)(2,1)} %bitcast.5), calls=%async_computation.1 | async-start | bytes 1048576 | tf_op jit(solution)/shard_map/all_to_all | solution.py:507
  32.7 6.4 %fusion.1 = f32[8,16,8,256]{3,1,2,0:T(8,128)S(1)} fusion(f32[256]{0:T(256)S(1)} %copy-done.17, f32[256]{0:T(256)S(1)} %copy-done.16, f32[8,8,256]{2,1,0:T(8,128)S(1)} %all-to-all-done.x_ref, bf16[256,16]{0,1:T(8,128)(2,1)S(1)} %copy-done.11), kind=kOutput, calls=%fused_computation.3 | convolution fusion | flops 180355072 | bytes 1124352 | tf_op jit(solution)/shard_map/mich,hj->mjic/dot_general | solution.py:419
  39.1 1.6 %copy.21 = f32[8,16,8,256]{3,2,1,0:T(8,128)} copy(f32[8,16,8,256]{3,1,2,0:T(8,128)S(1)} %fusion.1) | data formatting | bytes 2097152 | tf_op jit(solution)/shard_map/mich,hj->mjic/transpose | solution.py:419
  40.7 11.6 %all-to-all-done.1 = bf16[256,8,128]{2,1,0:T(8,128)(2,1)S(1)} async-done(((bf16[256,8,128]{2,1,0:T(8,128)(2,1)}), bf16[256,8,128]{2,1,0:T(8,128)(2,1)S(1)}, u32[]{:S(2)}, u32[]{:S(2)}) %all-to-all-start.1) | async-done | bytes 524320 | tf_op jit(solution)/shard_map/all_to_all | solution.py:507
  52.4 0.0 copy-done.1
  52.4 2.3 %filter.1 = bf16[32,64,128]{2,1,0:T(8,128)(2,1)S(1)} custom-call(bf16[32,64,128]{2,1,0:T(8,128)(2,1)S(1)} %bitcast.40, f32[32,32,128]{2,1,0:T(8,128)S(1)} %get-tuple-element.18.kr_ref, f32[32,32,128]{2,1,0:T(8,128)S(1)} %get-tuple-element.19.ki_ref, f32[2,32,32,128]{3,2,1,0:T(8,128)S(1)} %copy-done.1, bf16[256,192]{1,0:T(8,128)(2,1)S(1)} %copy-done.4, ...), custom_call_target="tpu_custom_call" | custom-call | flops 100000000 | bytes 3342336 | tf_op jit(solution)/shard_map/filter/pallas_call | solution.py:400
  54.8 0.0 copy-start.12
  54.8 0.0 copy-start.13
  54.8 15.8 %all_to_all.54.x_ref = bf16[32,64,128]{2,1,0:T(8,128)(2,1)S(1)} all-to-all(bf16[32,64,128]{2,1,0:T(8,128)(2,1)S(1)} %filter.1), channel_id=1, replica_groups=mesh['xl'=2,'y'=4,'xh'=2,'z'=8,'c'=2] {'xh','c','xl','y'}, dimensions={0} | all-to-all | bytes 1048576 | tf_op jit(solution)/shard_map/all_to_all | solution.py:561
  70.6 0.0 copy-done.15
  70.6 1.8 %middle.1 = bf16[32,64,128]{2,1,0:T(8,128)(2,1)S(1)} custom-call(bf16[32,64,128]{2,1,0:T(8,128)(2,1)S(1)} %all_to_all.54.x_ref, f32[48,128]{1,0:T(8,128)S(1)} %copy-done.9, f32[32,32,128]{2,1,0:T(8,128)S(1)} %copy-done.15, f32[48,2,128]{2,1,0:T(2,128)S(1)} %copy-done.8, bf16[768,256]{1,0:T(8,128)(2,1)S(1)} %copy-done.12, bf16[512,256]{1,0:T(8,128)(2,1)S(1)} %copy-done.13), custom_call_target="tpu_custom_call" | custom-call | flops 6000000000 | bytes 2301952 | tf_op jit(solution)/shard_map/middle/pallas_call | solution.py:400
  72.4 15.1 %all_to_all.55.x_ref = bf16[32,64,128]{2,1,0:T(8,128)(2,1)S(1)} all-to-all(bf16[32,64,128]{2,1,0:T(8,128)(2,1)S(1)} %middle.1), channel_id=1, replica_groups=mesh['xl'=2,'y'=4,'xh'=2,'z'=8,'c'=2] {'xh','c','xl','y'}, dimensions={0} | all-to-all | bytes 1048576 | tf_op jit(solution)/shard_map/all_to_all | solution.py:561
  87.5 2.2 %filter_back.1 = bf16[32,64,128]{2,1,0:T(8,128)(2,1)S(1)} custom-call(bf16[32,64,128]{2,1,0:T(8,128)(2,1)S(1)} %all_to_all.55.x_ref, f32[32,32,128]{2,1,0:T(8,128)S(1)} %get-tuple-element.18.kr_ref, f32[32,32,128]{2,1,0:T(8,128)S(1)} %get-tuple-element.19.ki_ref, f32[2,32,32,128]{3,2,1,0:T(8,128)S(1)} %copy-done.1, bf16[256,192]{1,0:T(8,128)(2,1)S(1)} %copy-done.4, ...), custom_call_target="tpu_custom_call" | custom-call | flops 100000000 | bytes 3342336 | tf_op jit(solution)/shard_map/filter_back/pallas_call | solution.py:400
  89.7 25.4 %all_to_all.56 = bf16[256,8,128]{2,1,0:T(8,128)(2,1)S(1)} all-to-all(bf16[256,8,128]{2,1,0:T(8,128)(2,1)S(1)} %bitcast.41), channel_id=1, replica_groups=mesh['xl'=2,'y'=4,'xh'=2,'z'=8,'c'=2] {'xh','z','c','xl','y'}, dimensions={0} | all-to-all | bytes 1048576 | tf_op jit(solution)/shard_map/all_to_all | solution.py:579
  115.1 0.7 last.1
  115.8 8.4 %all_to_all.57 = f32[8,8,256]{2,1,0:T(8,128)S(1)} all-to-all(f32[8,8,256]{2,1,0:T(8,128)S(1)} %bitcast.43), channel_id=1, replica_groups=mesh['xl'=2,'y'=4,'xh'=2,'z'=8,'c'=2] {'xl','y'}, dimensions={0} | all-to-all | bytes 131072 | tf_op jit(solution)/shard_map/all_to_all | solution.py:592
  124.3 0.6 copy.23
  (39 shorter events, 0.1 us)
Async XLA Ops:
  0.0 7.5 %copy-start = (s32[8,64,2]{1,2,0:T(2,128)S(1)}, s32[8,64,2]{1,2,0:T(2,128)}, u32[]{:S(2)}) copy-start(s32[8,64,2]{1,2,0:T(2,128)} %param.19) | copy-start | bytes 12292
  1.5 11.2 %all-to-all-start = ((f32[8,8,256]{2,1,0:T(8,128)}), f32[8,8,256]{2,1,0:T(8,128)S(1)}, u32[]{:S(2)}, u32[]{:S(2)}) async-start(f32[8,8,256]{2,1,0:T(8,128)} %add_bitcast_fusion), calls=%async_computation | async-start | bytes 131072 | tf_op jit(solution)/shard_map/all_to_all | solution.py:468
  8.4 2.0 %copy-start.14 = (f32[32,32,128]{2,1,0:T(8,128)}, f32[32,32,128]{2,1,0:T(8,128)S(1)}, u32[]{:S(2)}) copy-start(f32[32,32,128]{2,1,0:T(8,128)S(1)} %spots.1.s_ref) | copy-start | bytes 1572868
  10.4 2.3 %copy-start.5 = (bf16[768,256]{1,0:T(8,128)(2,1)S(1)}, bf16[768,256]{1,0:T(8,128)(2,1)}, u32[]{:S(2)}) copy-start(bf16[768,256]{1,0:T(8,128)(2,1)} %constant.162.clone.w_ref) | copy-start | bytes 1179652
  10.4 2.3 %copy-start.7 = (f32[2,256,128]{2,1,0:T(8,128)S(1)}, f32[2,256,128]{2,1,0:T(8,128)}, u32[]{:S(2)}) copy-start(f32[2,256,128]{2,1,0:T(8,128)} %get-tuple-element.14.s_ref) | copy-start | bytes 786436
  10.5 2.3 %copy-start.8 = (f32[48,2,128]{2,1,0:T(2,128)S(1)}, f32[48,2,128]{2,1,0:T(2,128)}, u32[]{:S(2)}) copy-start(f32[48,2,128]{2,1,0:T(2,128)} %constant.165.clone.t_ref) | copy-start | bytes 147460
  10.5 2.3 %copy-start.10 = (f32[2,16,128]{2,1,0:T(8,128)S(1)}, f32[2,16,128]{2,1,0:T(8,128)}, u32[]{:S(2)}) copy-start(f32[2,16,128]{2,1,0:T(8,128)} %get-tuple-element.15.m_ref) | copy-start | bytes 49156
  10.5 2.3 %copy-start.11 = (bf16[256,16]{0,1:T(8,128)(2,1)S(1)}, bf16[256,16]{0,1:T(8,128)(2,1)}, u32[]{:S(2)}) copy-start(bf16[256,16]{0,1:T(8,128)(2,1)} %param.22) | copy-start | bytes 24580
  12.8 19.9 %copy-start.16 = (f32[256]{0:T(256)S(1)}, f32[256]{0:T(256)}, u32[]{:S(2)}) copy-start(f32[256]{0:T(256)} %param.20) | copy-start | bytes 3076
  12.8 19.9 %copy-start.17 = (f32[256]{0:T(256)S(1)}, f32[256]{0:T(256)}, u32[]{:S(2)}) copy-start(f32[256]{0:T(256)} %param.21) | copy-start | bytes 3076
  17.5 34.9 %all-to-all-start.1 = ((bf16[256,8,128]{2,1,0:T(8,128)(2,1)}), bf16[256,8,128]{2,1,0:T(8,128)(2,1)S(1)}, u32[]{:S(2)}, u32[]{:S(2)}) async-start(bf16[256,8,128]{2,1,0:T(8,128)(2,1)} %bitcast.5), calls=%async_computation.1 | async-start | bytes 1048576 | tf_op jit(solution)/shard_map/all_to_all | solution.py:507
  39.1 13.3 %copy-start.1 = (f32[2,32,32,128]{3,2,1,0:T(8,128)S(1)}, f32[2,32,32,128]{3,2,1,0:T(8,128)}, u32[]{:S(2)}) copy-start(f32[2,32,32,128]{3,2,1,0:T(8,128)} %constant.164.clone.t_ref) | copy-start | bytes 3145732
  39.1 13.3 %copy-start.3 = (bf16[256,192]{1,0:T(8,128)(2,1)S(1)}, bf16[256,192]{1,0:T(8,128)(2,1)}, u32[]{:S(2)}) copy-start(bf16[256,192]{1,0:T(8,128)(2,1)} %constant.159.clone.v_ref) | copy-start | bytes 294916
  39.1 13.3 %copy-start.4 = (bf16[256,192]{1,0:T(8,128)(2,1)S(1)}, bf16[256,192]{1,0:T(8,128)(2,1)}, u32[]{:S(2)}) copy-start(bf16[256,192]{1,0:T(8,128)(2,1)} %constant.158.clone.w_ref) | copy-start | bytes 294916
  52.4 18.2 %copy-start.15 = (f32[32,32,128]{2,1,0:T(8,128)S(1)}, f32[32,32,128]{2,1,0:T(8,128)}, u32[]{:S(2)}) copy-start(f32[32,32,128]{2,1,0:T(8,128)} %copy-done.14) | copy-start | bytes 1572868
  54.8 15.8 %copy-start.9 = (f32[48,128]{1,0:T(8,128)S(1)}, f32[48,128]{1,0:T(8,128)}, u32[]{:S(2)}) copy-start(f32[48,128]{1,0:T(8,128)} %get-tuple-element.20.c_ref) | copy-start | bytes 73732
  54.8 15.8 %copy-start.12 = (bf16[768,256]{1,0:T(8,128)(2,1)S(1)}, bf16[768,256]{1,0:T(8,128)(2,1)}, u32[]{:S(2)}) copy-start(bf16[768,256]{1,0:T(8,128)(2,1)} %constant.160.clone.w_ref) | copy-start | bytes 1179652
  54.8 15.8 %copy-start.13 = (bf16[512,256]{1,0:T(8,128)(2,1)S(1)}, bf16[512,256]{1,0:T(8,128)(2,1)}, u32[]{:S(2)}) copy-start(bf16[512,256]{1,0:T(8,128)(2,1)} %constant.161.clone.v_ref) | copy-start | bytes 786436
  87.5 27.6 %copy-start.6 = (bf16[512,256]{1,0:T(8,128)(2,1)S(1)}, bf16[512,256]{1,0:T(8,128)(2,1)}, u32[]{:S(2)}) copy-start(bf16[512,256]{1,0:T(8,128)(2,1)} %constant.163.clone.w_ref) | copy-start | bytes 786436
  89.7 25.4 %copy-start.2 = (f32[8,16,8,256]{3,2,1,0:T(8,128)S(1)}, f32[8,16,8,256]{3,2,1,0:T(8,128)}, u32[]{:S(2)}) copy-start(f32[8,16,8,256]{3,2,1,0:T(8,128)} %copy.21) | copy-start | bytes 3145732

commit v5 on v4

--- a/solution.py
+++ b/solution.py
@@ -490,30 +490,9 @@
         name="prepare",
     )
 
-    sent = call(
-        first_kernel,
-        lined,
-        [(OUTER, each * GROUP, LANES), (1024, 2 * LANES)],
-        0,
-        widths,
-        pairs,
-        moments,
-        w_out.T,
-        turns_rows,
-        forward_whole,
-        flops=FLOPS["first"],
-        name="first",
-    )
-    cols = lax.all_to_all(sent, EVERY, 0, 0, tiled=True)
-
+    pairs, targets = lax.optimization_barrier((pairs, targets))
     lane = jnp.arange(LANES, dtype=jnp.int32)
     first = jnp.arange(FIRST, dtype=jnp.int32)
-    row = jnp.arange(ROWS, dtype=jnp.int32)[:, None] + ROWS * (lane // SECOND)[None, :]
-    kx = signed_kappa(first[:, None, None] + FIRST * row[None])
-    ky = signed_kappa(plane_index + FIRST * (lane % SECOND))
-    wavelength = 1.5 + wave_index.astype(jnp.float32) / (WAVES - 1)
-    kern_re, kern_im = transfer(wavelength, kx, ky[None, None, :], FOCAL)
-
     own_targets = lax.dynamic_index_in_dim(targets, wave_index, 0, keepdims=False)
     place_row = plane_index * SECOND + jnp.arange(ROWS, dtype=jnp.int32)
     hit_a = own_targets[:, 1][None, :] // SECOND == first[:, None]
@@ -535,6 +514,31 @@
         flops=FLOPS["spots"],
         name="spots",
     )
+
+    widths, spots = lax.optimization_barrier((widths, spots))
+
+    sent = call(
+        first_kernel,
+        lined,
+        [(OUTER, each * GROUP, LANES), (1024, 2 * LANES)],
+        0,
+        widths,
+        pairs,
+        moments,
+        w_out.T,
+        turns_rows,
+        forward_whole,
+        flops=FLOPS["first"],
+        name="first",
+    )
+    sent, wave_index, widths = lax.optimization_barrier((sent, wave_index, widths))
+    cols = lax.all_to_all(sent, EVERY, 0, 0, tiled=True)
+
+    row = jnp.arange(ROWS, dtype=jnp.int32)[:, None] + ROWS * (lane // SECOND)[None, :]
+    kx = signed_kappa(first[:, None, None] + FIRST * row[None])
+    ky = signed_kappa(plane_index + FIRST * (lane % SECOND))
+    wavelength = 1.5 + wave_index.astype(jnp.float32) / (WAVES - 1)
+    kern_re, kern_im = transfer(wavelength, kx, ky[None, None, :], FOCAL)
 
     slopes = slope_rows(widths, w_in, b_in, w_out).reshape(WAVES, 2 * WAVES * GROUP, cols_here)
     together = (cols, kern_re, kern_im, spots, consts, slopes)

time: 125 us -> 124 us (level)
    all_to_all x1, waiting for transfers between devices: 11.6 us -> 9.17 us  [local(): cols = lax.all_to_all(sent, EVERY, 0, 0, tiled=True)]
    all_to_all x1, waiting for transfers between devices: 0.01 us -> 2.45 us  [local(): lax.all_to_all(level_widths(levels, offsets), WAVE, 0, 0, tiled=True)]
  transfers between devices with their start and end apart: 2 -> 2, of which waited for: 1 -> 2; matrix products, arithmetic and copies ran while one was open for 9% -> 9% of each run, Pallas kernels for 2% -> 2%
where the time goes in v5:
time: 124 us
  blocking collectives  64.7 us (52%)
  starting transfers between devices  20.1 us (16%)
  Pallas kernels  14 us (11%)
  waiting for transfers between devices  11.6 us (9%)
  matrix products  6.44 us (5%)
  other arithmetic  4.34 us (4%)
  local copies, waits for them, and re-layouts  2.33 us (2%)
    all_to_all x2, blocking collectives, exchange(): return lax.all_to_all(x, PLANE, 0, 0, tiled=True)  30.9 us
    all_to_all x1, blocking collectives, local(): lines = lax.all_to_all(cols, EVERY, 0, 0, tiled=True)  25.4 us
    all_to_all x1, starting transfers between devices, local(): cols = lax.all_to_all(sent, EVERY, 0, 0, tiled=True)  14.1 us
    pallas_call x7, Pallas kernels, call(): pl.pallas_call(kernel, out_shape=out_shape, out_specs=(where,) * len(outs...  14 us
    all_to_all x1, waiting for transfers between devices, local(): cols = lax.all_to_all(sent, EVERY, 0, 0, tiled=True)  9.17 us
    all_to_all x1, blocking collectives, local(): return lax.all_to_all(gradient, WAVE, 0, 0, tiled=True)  8.45 us
    dot_general x1, matrix products, slope_rows(): jnp.einsum('mich,hj->mjic', slope.astype(jnp.bfloat16), w_out, preferred_...  6.44 us
    all_to_all x1, starting transfers between devices, local(): lax.all_to_all(level_widths(levels, offsets), WAVE, 0, 0, tiled=True)  5.95 us
  transfers between devices with their start and end apart: 2, of which 2 were waited for; matrix products, arithmetic and copies ran while one was open for 9% of the time, Pallas kernels for 2%

profile of v5, /device:TPU:1, one launch (start us, length us, event | category | flops | bytes accessed | tf_op | source)
XLA Modules:
  0.0 123.9 jit_solution(12976565649487656623)
XLA Ops:
  0.0 1.5 %add_bitcast_fusion = f32[8,8,256]{2,1,0:T(8,128)} fusion(f32[64,256]{1,0:T(8,128)} %param.18, s32[64,256]{1,0:T(8,128)} %param.17), kind=kLoop, calls=%fused_computation.19 | loop fusion | flops 65536 | bytes 196608 | tf_op jit(solution)/shard_map/all_to_all | solution.py:468
  1.5 5.9 %all-to-all-start = ((f32[8,8,256]{2,1,0:T(8,128)}), f32[8,8,256]{2,1,0:T(8,128)S(1)}, u32[]{:S(2)}, u32[]{:S(2)}) async-start(f32[8,8,256]{2,1,0:T(8,128)} %add_bitcast_fusion), calls=%async_computation | async-start | bytes 131072 | tf_op jit(solution)/shard_map/all_to_all | solution.py:468
  7.5 1.8 %prepare.1 = (f32[2,256,128]{2,1,0:T(8,128)}, f32[2,16,128]{2,1,0:T(8,128)}, f32[48,128]{1,0:T(8,128)}) custom-call(f32[1,256]{1,0:T(1,128)} %bitcast.49, f32[1,256]{1,0:T(1,128)} %bitcast.50, f32[1,16]{1,0:T(1,128)} %bitcast.51, bf16[16,256]{1,0:T(8,128)(2,1)} %bitcast.44, f32[2,128]{1,0:T(2,128)} %constant.166.clone.u_ref, f32[2,8,128]{2,1,0:T(8,128)} %constant.167.clone.dc_ref), custom_call_target="tpu_custom_call" | custom-call | flops 20000000000 | tf_op jit(solution)/shard_map/prepare/pallas_call | solution.py:400
  9.4 0.1 broadcast_compare_fusion.1
  9.5 0.1 broadcast_and_fusion.1
  9.6 0.2 add_convert_fusion.near_ref
  9.8 0.1 compare_and_fusion.1
  9.9 0.0 copy-start.5
  10.0 0.0 copy-start.8
  10.0 0.0 copy-start.11
  10.0 0.2 spots.1.s_ref
  10.2 2.4 %all-to-all-done.x_ref = f32[8,8,256]{2,1,0:T(8,128)S(1)} async-done(((f32[8,8,256]{2,1,0:T(8,128)}), f32[8,8,256]{2,1,0:T(8,128)S(1)}, u32[]{:S(2)}, u32[]{:S(2)}) %all-to-all-start) | async-done | bytes 65568 | tf_op jit(solution)/shard_map/all_to_all | solution.py:468
  12.7 0.0 copy-done.8
  12.7 0.0 copy-start.16
  12.7 0.0 copy-start.17
  12.7 4.7 %first.1 = bf16[2048,128]{1,0:T(8,128)(2,1)} custom-call(f32[8,8,256]{2,1,0:T(8,128)S(1)} %all-to-all-done.x_ref, f32[2,256,128]{2,1,0:T(8,128)S(1)} %copy-done.7, f32[2,16,128]{2,1,0:T(8,128)S(1)} %copy-done.10, bf16[16,256]{1,0:T(8,128)(2,1)S(1)} %bitcast.45, f32[48,2,128]{2,1,0:T(2,128)S(1)} %copy-done.8, bf16[768,256]{1,0:T(8,128)(2,1)S(1)} %copy-done.5), custom_call_target="tpu_custom_call" | custom-call | flops 100000000 | bytes 1318912 | tf_op jit(solution)/shard_map/first/pallas_call | solution.py:400
  17.4 14.1 %all-to-all-start.1 = ((bf16[256,8,128]{2,1,0:T(8,128)(2,1)}), bf16[256,8,128]{2,1,0:T(8,128)(2,1)S(1)}, u32[]{:S(2)}, u32[]{:S(2)}) async-start(bf16[256,8,128]{2,1,0:T(8,128)(2,1)} %bitcast.11), calls=%async_computation.1 | async-start | bytes 1048576 | tf_op jit(solution)/shard_map/all_to_all | solution.py:535
  31.6 6.4 %fusion.1 = f32[8,16,8,256]{3,1,2,0:T(8,128)S(1)} fusion(f32[256]{0:T(256)S(1)} %copy-done.17, f32[256]{0:T(256)S(1)} %copy-done.16, f32[8,8,256]{2,1,0:T(8,128)S(1)} %all-to-all-done.x_ref, bf16[256,16]{0,1:T(8,128)(2,1)S(1)} %copy-done.11), kind=kOutput, calls=%fused_computation.3 | convolution fusion | flops 180355072 | bytes 1124352 | tf_op jit(solution)/shard_map/mich,hj->mjic/dot_general | solution.py:419
  38.0 1.6 %copy.21 = f32[8,16,8,256]{3,2,1,0:T(8,128)} copy(f32[8,16,8,256]{3,1,2,0:T(8,128)S(1)} %fusion.1) | data formatting | bytes 2097152 | tf_op jit(solution)/shard_map/mich,hj->mjic/transpose | solution.py:419
  39.7 2.2 %sine_multiply_fusion = (f32[32,32,128]{2,1,0:T(8,128)S(1)}, f32[32,32,128]{2,1,0:T(8,128)S(1)}) fusion(f32[128]{0:T(128)S(1)} %fusion.13, s32[32,128]{1,0:T(8,128)S(1)} %add_multiply_fusion, f32[]{:T(128)S(6)} %mul.116), kind=kLoop, calls=%fused_computation.10 | loop fusion | flops 2228224 | bytes 1065476 | tf_op jit(solution)/shard_map/mul | solution.py:434
  41.9 9.2 %all-to-all-done.1 = bf16[256,8,128]{2,1,0:T(8,128)(2,1)S(1)} async-done(((bf16[256,8,128]{2,1,0:T(8,128)(2,1)}), bf16[256,8,128]{2,1,0:T(8,128)(2,1)S(1)}, u32[]{:S(2)}, u32[]{:S(2)}) %all-to-all-start.1) | async-done | bytes 524320 | tf_op jit(solution)/shard_map/all_to_all | solution.py:535
  51.1 2.6 %filter.1 = bf16[32,64,128]{2,1,0:T(8,128)(2,1)S(1)} custom-call(bf16[32,64,128]{2,1,0:T(8,128)(2,1)S(1)} %bitcast.40, f32[32,32,128]{2,1,0:T(8,128)S(1)} %get-tuple-element.32.kr_ref, f32[32,32,128]{2,1,0:T(8,128)S(1)} %get-tuple-element.33.ki_ref, f32[2,32,32,128]{3,2,1,0:T(8,128)S(1)} %copy-done.1, bf16[256,192]{1,0:T(8,128)(2,1)S(1)} %copy-done.3, ...), custom_call_target="tpu_custom_call" | custom-call | flops 100000000 | bytes 3342336 | tf_op jit(solution)/shard_map/filter/pallas_call | solution.py:400
  53.7 0.0 copy-start.12
  53.7 0.0 copy-start.13
  53.7 15.8 %all_to_all.54.x_ref = bf16[32,64,128]{2,1,0:T(8,128)(2,1)S(1)} all-to-all(bf16[32,64,128]{2,1,0:T(8,128)(2,1)S(1)} %filter.1), channel_id=1, replica_groups=mesh['xl'=2,'y'=4,'xh'=2,'z'=8,'c'=2] {'xh','c','xl','y'}, dimensions={0} | all-to-all | bytes 1048576 | tf_op jit(solution)/shard_map/all_to_all | solution.py:565
  69.6 1.8 %middle.1 = bf16[32,64,128]{2,1,0:T(8,128)(2,1)S(1)} custom-call(bf16[32,64,128]{2,1,0:T(8,128)(2,1)S(1)} %all_to_all.54.x_ref, f32[48,128]{1,0:T(8,128)S(1)} %copy-done.9, f32[32,32,128]{2,1,0:T(8,128)S(1)} %copy-done.15, f32[48,2,128]{2,1,0:T(2,128)S(1)} %copy-done.8, bf16[768,256]{1,0:T(8,128)(2,1)S(1)} %copy-done.12, bf16[512,256]{1,0:T(8,128)(2,1)S(1)} %copy-done.13), custom_call_target="tpu_custom_call" | custom-call | flops 6000000000 | bytes 2301952 | tf_op jit(solution)/shard_map/middle/pallas_call | solution.py:400
  71.4 15.1 %all_to_all.55.x_ref = bf16[32,64,128]{2,1,0:T(8,128)(2,1)S(1)} all-to-all(bf16[32,64,128]{2,1,0:T(8,128)(2,1)S(1)} %middle.1), channel_id=1, replica_groups=mesh['xl'=2,'y'=4,'xh'=2,'z'=8,'c'=2] {'xh','c','xl','y'}, dimensions={0} | all-to-all | bytes 1048576 | tf_op jit(solution)/shard_map/all_to_all | solution.py:565
  86.4 2.2 %filter_back.1 = bf16[32,64,128]{2,1,0:T(8,128)(2,1)S(1)} custom-call(bf16[32,64,128]{2,1,0:T(8,128)(2,1)S(1)} %all_to_all.55.x_ref, f32[32,32,128]{2,1,0:T(8,128)S(1)} %get-tuple-element.32.kr_ref, f32[32,32,128]{2,1,0:T(8,128)S(1)} %get-tuple-element.33.ki_ref, f32[2,32,32,128]{3,2,1,0:T(8,128)S(1)} %copy-done.1, bf16[256,192]{1,0:T(8,128)(2,1)S(1)} %copy-done.3, ...), custom_call_target="tpu_custom_call" | custom-call | flops 100000000 | bytes 3342336 | tf_op jit(solution)/shard_map/filter_back/pallas_call | solution.py:400
  88.6 25.4 %all_to_all.56 = bf16[256,8,128]{2,1,0:T(8,128)(2,1)S(1)} all-to-all(bf16[256,8,128]{2,1,0:T(8,128)(2,1)S(1)} %bitcast.41), channel_id=1, replica_groups=mesh['xl'=2,'y'=4,'xh'=2,'z'=8,'c'=2] {'xh','z','c','xl','y'}, dimensions={0} | all-to-all | bytes 1048576 | tf_op jit(solution)/shard_map/all_to_all | solution.py:583
  114.0 0.7 last.1
  114.8 8.4 %all_to_all.57 = f32[8,8,256]{2,1,0:T(8,128)S(1)} all-to-all(f32[8,8,256]{2,1,0:T(8,128)S(1)} %bitcast.43), channel_id=1, replica_groups=mesh['xl'=2,'y'=4,'xh'=2,'z'=8,'c'=2] {'xl','y'}, dimensions={0} | all-to-all | bytes 131072 | tf_op jit(solution)/shard_map/all_to_all | solution.py:596
  123.2 0.6 copy.23
  (39 shorter events, 0.1 us)
Async XLA Ops:
  0.0 9.3 %copy-start = (s32[8,64,2]{1,2,0:T(2,128)S(1)}, s32[8,64,2]{1,2,0:T(2,128)}, u32[]{:S(2)}) copy-start(s32[8,64,2]{1,2,0:T(2,128)} %param.19) | copy-start | bytes 12292
  1.5 11.1 %all-to-all-start = ((f32[8,8,256]{2,1,0:T(8,128)}), f32[8,8,256]{2,1,0:T(8,128)S(1)}, u32[]{:S(2)}, u32[]{:S(2)}) async-start(f32[8,8,256]{2,1,0:T(8,128)} %add_bitcast_fusion), calls=%async_computation | async-start | bytes 131072 | tf_op jit(solution)/shard_map/all_to_all | solution.py:468
  9.9 2.7 %copy-start.5 = (bf16[768,256]{1,0:T(8,128)(2,1)S(1)}, bf16[768,256]{1,0:T(8,128)(2,1)}, u32[]{:S(2)}) copy-start(bf16[768,256]{1,0:T(8,128)(2,1)} %constant.162.clone.w_ref) | copy-start | bytes 1179652
  9.9 2.7 %copy-start.7 = (f32[2,256,128]{2,1,0:T(8,128)S(1)}, f32[2,256,128]{2,1,0:T(8,128)}, u32[]{:S(2)}) copy-start(f32[2,256,128]{2,1,0:T(8,128)} %get-tuple-element.24.s_ref) | copy-start | bytes 786436
  10.0 2.7 %copy-start.8 = (f32[48,2,128]{2,1,0:T(2,128)S(1)}, f32[48,2,128]{2,1,0:T(2,128)}, u32[]{:S(2)}) copy-start(f32[48,2,128]{2,1,0:T(2,128)} %constant.165.clone.t_ref) | copy-start | bytes 147460
  10.0 2.7 %copy-start.10 = (f32[2,16,128]{2,1,0:T(8,128)S(1)}, f32[2,16,128]{2,1,0:T(8,128)}, u32[]{:S(2)}) copy-start(f32[2,16,128]{2,1,0:T(8,128)} %get-tuple-element.25.m_ref) | copy-start | bytes 49156
  10.0 2.7 %copy-start.11 = (bf16[256,16]{0,1:T(8,128)(2,1)S(1)}, bf16[256,16]{0,1:T(8,128)(2,1)}, u32[]{:S(2)}) copy-start(bf16[256,16]{0,1:T(8,128)(2,1)} %param.22) | copy-start | bytes 24580
  10.2 7.2 %copy-start.14 = (f32[32,32,128]{2,1,0:T(8,128)}, f32[32,32,128]{2,1,0:T(8,128)S(1)}, u32[]{:S(2)}) copy-start(f32[32,32,128]{2,1,0:T(8,128)S(1)} %spots.1.s_ref) | copy-start | bytes 1572868
  12.7 18.9 %copy-start.16 = (f32[256]{0:T(256)S(1)}, f32[256]{0:T(256)}, u32[]{:S(2)}) copy-start(f32[256]{0:T(256)} %param.20) | copy-start | bytes 3076
  12.7 18.9 %copy-start.17 = (f32[256]{0:T(256)S(1)}, f32[256]{0:T(256)}, u32[]{:S(2)}) copy-start(f32[256]{0:T(256)} %param.21) | copy-start | bytes 3076
  17.4 33.7 %all-to-all-start.1 = ((bf16[256,8,128]{2,1,0:T(8,128)(2,1)}), bf16[256,8,128]{2,1,0:T(8,128)(2,1)S(1)}, u32[]{:S(2)}, u32[]{:S(2)}) async-start(bf16[256,8,128]{2,1,0:T(8,128)(2,1)} %bitcast.11), calls=%async_computation.1 | async-start | bytes 1048576 | tf_op jit(solution)/shard_map/all_to_all | solution.py:535
  38.0 13.1 %copy-start.3 = (bf16[256,192]{1,0:T(8,128)(2,1)S(1)}, bf16[256,192]{1,0:T(8,128)(2,1)}, u32[]{:S(2)}) copy-start(bf16[256,192]{1,0:T(8,128)(2,1)} %constant.158.clone.w_ref) | copy-start | bytes 294916
  38.0 13.1 %copy-start.4 = (bf16[256,192]{1,0:T(8,128)(2,1)S(1)}, bf16[256,192]{1,0:T(8,128)(2,1)}, u32[]{:S(2)}) copy-start(bf16[256,192]{1,0:T(8,128)(2,1)} %constant.159.clone.v_ref) | copy-start | bytes 294916
  39.6 11.5 %copy-start.1 = (f32[2,32,32,128]{3,2,1,0:T(8,128)S(1)}, f32[2,32,32,128]{3,2,1,0:T(8,128)}, u32[]{:S(2)}) copy-start(f32[2,32,32,128]{3,2,1,0:T(8,128)} %constant.164.clone.t_ref) | copy-start | bytes 3145732
  51.1 18.4 %copy-start.15 = (f32[32,32,128]{2,1,0:T(8,128)S(1)}, f32[32,32,128]{2,1,0:T(8,128)}, u32[]{:S(2)}) copy-start(f32[32,32,128]{2,1,0:T(8,128)} %copy-done.14) | copy-start | bytes 1572868
  53.7 15.8 %copy-start.9 = (f32[48,128]{1,0:T(8,128)S(1)}, f32[48,128]{1,0:T(8,128)}, u32[]{:S(2)}) copy-start(f32[48,128]{1,0:T(8,128)} %get-tuple-element.34.c_ref) | copy-start | bytes 73732
  53.7 15.8 %copy-start.12 = (bf16[768,256]{1,0:T(8,128)(2,1)S(1)}, bf16[768,256]{1,0:T(8,128)(2,1)}, u32[]{:S(2)}) copy-start(bf16[768,256]{1,0:T(8,128)(2,1)} %constant.160.clone.w_ref) | copy-start | bytes 1179652
  53.7 15.8 %copy-start.13 = (bf16[512,256]{1,0:T(8,128)(2,1)S(1)}, bf16[512,256]{1,0:T(8,128)(2,1)}, u32[]{:S(2)}) copy-start(bf16[512,256]{1,0:T(8,128)(2,1)} %constant.161.clone.v_ref) | copy-start | bytes 786436
  86.4 27.6 %copy-start.6 = (bf16[512,256]{1,0:T(8,128)(2,1)S(1)}, bf16[512,256]{1,0:T(8,128)(2,1)}, u32[]{:S(2)}) copy-start(bf16[512,256]{1,0:T(8,128)(2,1)} %constant.163.clone.w_ref) | copy-start | bytes 786436
  88.6 25.4 %copy-start.2 = (f32[8,16,8,256]{3,2,1,0:T(8,128)S(1)}, f32[8,16,8,256]{3,2,1,0:T(8,128)}, u32[]{:S(2)}) copy-start(f32[8,16,8,256]{3,2,1,0:T(8,128)} %copy.21) | copy-start | bytes 3145732

commit v6 on v5

--- a/solution.py
+++ b/solution.py
@@ -59,7 +59,9 @@
     for cut in (slice(0, ROWS), slice(ROWS, SECOND)):
         halves.append((np.concatenate([cos[:, cut], -sin[:, cut]], 1), np.concatenate([sin[:, cut], cos[:, cut]], 1)))
     high, low = split_np(np.concatenate([halves[0][0], halves[1][0], halves[0][1], halves[1][1]], 0))
-    return np.concatenate([high, high, low], 1)
+    split = np.concatenate([high, high, low], 1)
+    high, low = split_np(np.concatenate([cos, sin], 0))
+    return np.concatenate([split, np.concatenate([high, high, low], 1)], 0)
 
 
 def whole_row_tables(direction):
@@ -312,6 +314,24 @@
     return [join_halves(both[:, i * LANES : (i + 1) * LANES]) for i in range(len(parts))]
 
 
+def wide_step(parts, table):
+    left = left_lanes()
+    data = []
+    for real, imag in parts:
+        data.append(jnp.concatenate([jnp.where(left, real, swap(imag)), jnp.where(left, swap(real), imag)], 0))
+    high, low = split_pair(jnp.concatenate(data, 1))
+    both = matmul(table, jnp.concatenate([high, low, high], 0))
+    results = []
+    for i in range(len(parts)):
+        lanes = slice(i * LANES, (i + 1) * LANES)
+        c_top, c_low = both[:ROWS, lanes], both[ROWS:SECOND, lanes]
+        s_top, s_low = both[SECOND : SECOND + ROWS, lanes], both[SECOND + ROWS :, lanes]
+        real = jnp.where(left, c_top, -s_low) + swap(jnp.where(left, c_low, -s_top))
+        imag = jnp.where(left, s_top, c_low) + swap(jnp.where(left, s_low, c_top))
+        results.append((real, imag))
+    return results
+
+
 def col_kernel(conjugate, x_ref, kr_ref, ki_ref, t_ref, w_ref, v_ref, out_ref, y_ref, *keep):
     for g in range(0, ROWS, 16):
         halves = load_groups(x_ref, g) if conjugate else load_lanes(x_ref, g)
@@ -322,12 +342,14 @@
                 y_ref[0, k, rows, :], y_ref[1, k, rows, :] = turn(
                     real[k], imag[k], t_ref[0, k, rows, :], t_ref[1, k, rows, :]
                 )
+    cut = slice(0, 2 * LANES) if conjugate else slice(2 * LANES, 3 * LANES)
+    step = col_step if conjugate else wide_step
     for k in range(0, FIRST, 2):
-        parts = col_step([(y_ref[0, k + i], y_ref[1, k + i]) for i in range(2)], w_ref[...])
+        parts = step([(y_ref[0, k + i], y_ref[1, k + i]) for i in range(2)], w_ref[cut, :])
         for i in range(2):
             turned = turn_back if conjugate else turn
             parts[i] = turned(parts[i][0], parts[i][1], kr_ref[k + i], ki_ref[k + i])
-        parts = col_step(parts, v_ref[...])
+        parts = step(parts, v_ref[cut, :])
         for i in range(2):
             y_ref[0, k + i], y_ref[1, k + i] = turn_back(
                 parts[i][0], parts[i][1], t_ref[0, k + i], t_ref[1, k + i]

time: 124 us -> 124 us (level)
  no operation moved by 1% of the time
where the time goes in v6:
time: 124 us
  blocking collectives  64.8 us (52%)
  starting transfers between devices  20.1 us (16%)
  Pallas kernels  13.8 us (11%)
  waiting for transfers between devices  11.6 us (9%)
  matrix products  6.44 us (5%)
  other arithmetic  4.34 us (4%)
  local copies, waits for them, and re-layouts  2.33 us (2%)
    all_to_all x2, blocking collectives, exchange(): return lax.all_to_all(x, PLANE, 0, 0, tiled=True)  31 us
    all_to_all x1, blocking collectives, local(): lines = lax.all_to_all(cols, EVERY, 0, 0, tiled=True)  25.4 us
    all_to_all x1, starting transfers between devices, local(): cols = lax.all_to_all(sent, EVERY, 0, 0, tiled=True)  14.1 us
    pallas_call x7, Pallas kernels, call(): pl.pallas_call(kernel, out_shape=out_shape, out_specs=(where,) * len(outs...  13.8 us
    all_to_all x1, waiting for transfers between devices, local(): cols = lax.all_to_all(sent, EVERY, 0, 0, tiled=True)  9.17 us
    all_to_all x1, blocking collectives, local(): return lax.all_to_all(gradient, WAVE, 0, 0, tiled=True)  8.45 us
    dot_general x1, matrix products, slope_rows(): jnp.einsum('mich,hj->mjic', slope.astype(jnp.bfloat16), w_out, preferred_...  6.44 us
    all_to_all x1, starting transfers between devices, local(): lax.all_to_all(level_widths(levels, offsets), WAVE, 0, 0, tiled=True)  5.95 us
  transfers between devices with their start and end apart: 2, of which 2 were waited for; matrix products, arithmetic and copies ran while one was open for 9% of the time, Pallas kernels for 2%

profile of v6, /device:TPU:1, one launch (start us, length us, event | category | flops | bytes accessed | tf_op | source)
XLA Modules:
  0.0 123.7 jit_solution(9279474023418906085)
XLA Ops:
  0.0 1.5 %add_bitcast_fusion = f32[8,8,256]{2,1,0:T(8,128)} fusion(f32[64,256]{1,0:T(8,128)} %param.18, s32[64,256]{1,0:T(8,128)} %param.17), kind=kLoop, calls=%fused_computation.19 | loop fusion | flops 65536 | bytes 196608 | tf_op jit(solution)/shard_map/all_to_all | solution.py:490
  1.5 5.9 %all-to-all-start = ((f32[8,8,256]{2,1,0:T(8,128)}), f32[8,8,256]{2,1,0:T(8,128)S(1)}, u32[]{:S(2)}, u32[]{:S(2)}) async-start(f32[8,8,256]{2,1,0:T(8,128)} %add_bitcast_fusion), calls=%async_computation | async-start | bytes 131072 | tf_op jit(solution)/shard_map/all_to_all | solution.py:490
  7.5 1.8 %prepare.1 = (f32[2,256,128]{2,1,0:T(8,128)}, f32[2,16,128]{2,1,0:T(8,128)}, f32[48,128]{1,0:T(8,128)}) custom-call(f32[1,256]{1,0:T(1,128)} %bitcast.49, f32[1,256]{1,0:T(1,128)} %bitcast.50, f32[1,16]{1,0:T(1,128)} %bitcast.51, bf16[16,256]{1,0:T(8,128)(2,1)} %bitcast.44, f32[2,128]{1,0:T(2,128)} %constant.166.clone.u_ref, f32[2,8,128]{2,1,0:T(8,128)} %constant.167.clone.dc_ref), custom_call_target="tpu_custom_call" | custom-call | flops 20000000000 | tf_op jit(solution)/shard_map/prepare/pallas_call | solution.py:422
  9.4 0.1 broadcast_compare_fusion.1
  9.5 0.1 broadcast_and_fusion.1
  9.6 0.2 add_convert_fusion.near_ref
  9.8 0.1 compare_and_fusion.1
  9.9 0.0 copy-start.5
  10.0 0.0 copy-start.8
  10.0 0.0 copy-start.11
  10.0 0.2 spots.1.s_ref
  10.2 2.4 %all-to-all-done.x_ref = f32[8,8,256]{2,1,0:T(8,128)S(1)} async-done(((f32[8,8,256]{2,1,0:T(8,128)}), f32[8,8,256]{2,1,0:T(8,128)S(1)}, u32[]{:S(2)}, u32[]{:S(2)}) %all-to-all-start) | async-done | bytes 65568 | tf_op jit(solution)/shard_map/all_to_all | solution.py:490
  12.7 0.0 copy-done.8
  12.7 0.0 copy-start.16
  12.7 0.0 copy-start.17
  12.7 4.7 %first.1 = bf16[2048,128]{1,0:T(8,128)(2,1)} custom-call(f32[8,8,256]{2,1,0:T(8,128)S(1)} %all-to-all-done.x_ref, f32[2,256,128]{2,1,0:T(8,128)S(1)} %copy-done.7, f32[2,16,128]{2,1,0:T(8,128)S(1)} %copy-done.10, bf16[16,256]{1,0:T(8,128)(2,1)S(1)} %bitcast.45, f32[48,2,128]{2,1,0:T(2,128)S(1)} %copy-done.8, bf16[768,256]{1,0:T(8,128)(2,1)S(1)} %copy-done.5), custom_call_target="tpu_custom_call" | custom-call | flops 100000000 | bytes 1318912 | tf_op jit(solution)/shard_map/first/pallas_call | solution.py:422
  17.4 14.1 %all-to-all-start.1 = ((bf16[256,8,128]{2,1,0:T(8,128)(2,1)}), bf16[256,8,128]{2,1,0:T(8,128)(2,1)S(1)}, u32[]{:S(2)}, u32[]{:S(2)}) async-start(bf16[256,8,128]{2,1,0:T(8,128)(2,1)} %bitcast.11), calls=%async_computation.1 | async-start | bytes 1048576 | tf_op jit(solution)/shard_map/all_to_all | solution.py:557
  31.6 6.4 %fusion.1 = f32[8,16,8,256]{3,1,2,0:T(8,128)S(1)} fusion(f32[256]{0:T(256)S(1)} %copy-done.17, f32[256]{0:T(256)S(1)} %copy-done.16, f32[8,8,256]{2,1,0:T(8,128)S(1)} %all-to-all-done.x_ref, bf16[256,16]{0,1:T(8,128)(2,1)S(1)} %copy-done.11), kind=kOutput, calls=%fused_computation.3 | convolution fusion | flops 180355072 | bytes 1124352 | tf_op jit(solution)/shard_map/mich,hj->mjic/dot_general | solution.py:441
  38.0 1.6 %copy.21 = f32[8,16,8,256]{3,2,1,0:T(8,128)} copy(f32[8,16,8,256]{3,1,2,0:T(8,128)S(1)} %fusion.1) | data formatting | bytes 2097152 | tf_op jit(solution)/shard_map/mich,hj->mjic/transpose | solution.py:441
  39.7 2.2 %sine_multiply_fusion = (f32[32,32,128]{2,1,0:T(8,128)S(1)}, f32[32,32,128]{2,1,0:T(8,128)S(1)}) fusion(f32[128]{0:T(128)S(1)} %fusion.13, s32[32,128]{1,0:T(8,128)S(1)} %add_multiply_fusion, f32[]{:T(128)S(6)} %mul.116), kind=kLoop, calls=%fused_computation.10 | loop fusion | flops 2228224 | bytes 1065476 | tf_op jit(solution)/shard_map/mul | solution.py:456
  41.9 9.2 %all-to-all-done.1 = bf16[256,8,128]{2,1,0:T(8,128)(2,1)S(1)} async-done(((bf16[256,8,128]{2,1,0:T(8,128)(2,1)}), bf16[256,8,128]{2,1,0:T(8,128)(2,1)S(1)}, u32[]{:S(2)}, u32[]{:S(2)}) %all-to-all-start.1) | async-done | bytes 524320 | tf_op jit(solution)/shard_map/all_to_all | solution.py:557
  51.1 2.3 %filter.1 = bf16[32,64,128]{2,1,0:T(8,128)(2,1)S(1)} custom-call(bf16[32,64,128]{2,1,0:T(8,128)(2,1)S(1)} %bitcast.40, f32[32,32,128]{2,1,0:T(8,128)S(1)} %get-tuple-element.32.kr_ref, f32[32,32,128]{2,1,0:T(8,128)S(1)} %get-tuple-element.33.ki_ref, f32[2,32,32,128]{3,2,1,0:T(8,128)S(1)} %copy-done.1, bf16[384,192]{1,0:T(8,128)(2,1)S(1)} %copy-done.3, ...), custom_call_target="tpu_custom_call" | custom-call | flops 100000000 | bytes 3440640 | tf_op jit(solution)/shard_map/filter/pallas_call | solution.py:422
  53.5 0.0 copy-start.12
  53.5 0.0 copy-start.13
  53.5 15.9 %all_to_all.54.x_ref = bf16[32,64,128]{2,1,0:T(8,128)(2,1)S(1)} all-to-all(bf16[32,64,128]{2,1,0:T(8,128)(2,1)S(1)} %filter.1), channel_id=1, replica_groups=mesh['xl'=2,'y'=4,'xh'=2,'z'=8,'c'=2] {'xh','c','xl','y'}, dimensions={0} | all-to-all | bytes 1048576 | tf_op jit(solution)/shard_map/all_to_all | solution.py:587
  69.4 1.8 %middle.1 = bf16[32,64,128]{2,1,0:T(8,128)(2,1)S(1)} custom-call(bf16[32,64,128]{2,1,0:T(8,128)(2,1)S(1)} %all_to_all.54.x_ref, f32[48,128]{1,0:T(8,128)S(1)} %copy-done.9, f32[32,32,128]{2,1,0:T(8,128)S(1)} %copy-done.15, f32[48,2,128]{2,1,0:T(2,128)S(1)} %copy-done.8, bf16[768,256]{1,0:T(8,128)(2,1)S(1)} %copy-done.12, bf16[512,256]{1,0:T(8,128)(2,1)S(1)} %copy-done.13), custom_call_target="tpu_custom_call" | custom-call | flops 6000000000 | bytes 2301952 | tf_op jit(solution)/shard_map/middle/pallas_call | solution.py:422
  71.2 15.1 %all_to_all.55.x_ref = bf16[32,64,128]{2,1,0:T(8,128)(2,1)S(1)} all-to-all(bf16[32,64,128]{2,1,0:T(8,128)(2,1)S(1)} %middle.1), channel_id=1, replica_groups=mesh['xl'=2,'y'=4,'xh'=2,'z'=8,'c'=2] {'xh','c','xl','y'}, dimensions={0} | all-to-all | bytes 1048576 | tf_op jit(solution)/shard_map/all_to_all | solution.py:587
  86.3 2.2 %filter_back.1 = bf16[32,64,128]{2,1,0:T(8,128)(2,1)S(1)} custom-call(bf16[32,64,128]{2,1,0:T(8,128)(2,1)S(1)} %all_to_all.55.x_ref, f32[32,32,128]{2,1,0:T(8,128)S(1)} %get-tuple-element.32.kr_ref, f32[32,32,128]{2,1,0:T(8,128)S(1)} %get-tuple-element.33.ki_ref, f32[2,32,32,128]{3,2,1,0:T(8,128)S(1)} %copy-done.1, bf16[384,192]{1,0:T(8,128)(2,1)S(1)} %copy-done.3, ...), custom_call_target="tpu_custom_call" | custom-call | flops 100000000 | bytes 3440640 | tf_op jit(solution)/shard_map/filter_back/pallas_call | solution.py:422
  88.5 25.4 %all_to_all.56 = bf16[256,8,128]{2,1,0:T(8,128)(2,1)S(1)} all-to-all(bf16[256,8,128]{2,1,0:T(8,128)(2,1)S(1)} %bitcast.41), channel_id=1, replica_groups=mesh['xl'=2,'y'=4,'xh'=2,'z'=8,'c'=2] {'xh','z','c','xl','y'}, dimensions={0} | all-to-all | bytes 1048576 | tf_op jit(solution)/shard_map/all_to_all | solution.py:605
  113.9 0.7 last.1
  114.6 8.4 %all_to_all.57 = f32[8,8,256]{2,1,0:T(8,128)S(1)} all-to-all(f32[8,8,256]{2,1,0:T(8,128)S(1)} %bitcast.43), channel_id=1, replica_groups=mesh['xl'=2,'y'=4,'xh'=2,'z'=8,'c'=2] {'xl','y'}, dimensions={0} | all-to-all | bytes 131072 | tf_op jit(solution)/shard_map/all_to_all | solution.py:618
  123.1 0.6 copy.23
  (39 shorter events, 0.1 us)
Async XLA Ops:
  0.0 9.3 %copy-start = (s32[8,64,2]{1,2,0:T(2,128)S(1)}, s32[8,64,2]{1,2,0:T(2,128)}, u32[]{:S(2)}) copy-start(s32[8,64,2]{1,2,0:T(2,128)} %param.19) | copy-start | bytes 12292
  1.5 11.1 %all-to-all-start = ((f32[8,8,256]{2,1,0:T(8,128)}), f32[8,8,256]{2,1,0:T(8,128)S(1)}, u32[]{:S(2)}, u32[]{:S(2)}) async-start(f32[8,8,256]{2,1,0:T(8,128)} %add_bitcast_fusion), calls=%async_computation | async-start | bytes 131072 | tf_op jit(solution)/shard_map/all_to_all | solution.py:490
  9.9 2.7 %copy-start.5 = (bf16[768,256]{1,0:T(8,128)(2,1)S(1)}, bf16[768,256]{1,0:T(8,128)(2,1)}, u32[]{:S(2)}) copy-start(bf16[768,256]{1,0:T(8,128)(2,1)} %constant.162.clone.w_ref) | copy-start | bytes 1179652
  9.9 2.7 %copy-start.7 = (f32[2,256,128]{2,1,0:T(8,128)S(1)}, f32[2,256,128]{2,1,0:T(8,128)}, u32[]{:S(2)}) copy-start(f32[2,256,128]{2,1,0:T(8,128)} %get-tuple-element.24.s_ref) | copy-start | bytes 786436
  10.0 2.7 %copy-start.8 = (f32[48,2,128]{2,1,0:T(2,128)S(1)}, f32[48,2,128]{2,1,0:T(2,128)}, u32[]{:S(2)}) copy-start(f32[48,2,128]{2,1,0:T(2,128)} %constant.165.clone.t_ref) | copy-start | bytes 147460
  10.0 2.7 %copy-start.10 = (f32[2,16,128]{2,1,0:T(8,128)S(1)}, f32[2,16,128]{2,1,0:T(8,128)}, u32[]{:S(2)}) copy-start(f32[2,16,128]{2,1,0:T(8,128)} %get-tuple-element.25.m_ref) | copy-start | bytes 49156
  10.0 2.7 %copy-start.11 = (bf16[256,16]{0,1:T(8,128)(2,1)S(1)}, bf16[256,16]{0,1:T(8,128)(2,1)}, u32[]{:S(2)}) copy-start(bf16[256,16]{0,1:T(8,128)(2,1)} %param.22) | copy-start | bytes 24580
  10.2 7.2 %copy-start.14 = (f32[32,32,128]{2,1,0:T(8,128)}, f32[32,32,128]{2,1,0:T(8,128)S(1)}, u32[]{:S(2)}) copy-start(f32[32,32,128]{2,1,0:T(8,128)S(1)} %spots.1.s_ref) | copy-start | bytes 1572868
  12.7 18.9 %copy-start.16 = (f32[256]{0:T(256)S(1)}, f32[256]{0:T(256)}, u32[]{:S(2)}) copy-start(f32[256]{0:T(256)} %param.20) | copy-start | bytes 3076
  12.7 18.9 %copy-start.17 = (f32[256]{0:T(256)S(1)}, f32[256]{0:T(256)}, u32[]{:S(2)}) copy-start(f32[256]{0:T(256)} %param.21) | copy-start | bytes 3076
  17.4 33.7 %all-to-all-start.1 = ((bf16[256,8,128]{2,1,0:T(8,128)(2,1)}), bf16[256,8,128]{2,1,0:T(8,128)(2,1)S(1)}, u32[]{:S(2)}, u32[]{:S(2)}) async-start(bf16[256,8,128]{2,1,0:T(8,128)(2,1)} %bitcast.11), calls=%async_computation.1 | async-start | bytes 1048576 | tf_op jit(solution)/shard_map/all_to_all | solution.py:557
  38.0 13.1 %copy-start.3 = (bf16[384,192]{1,0:T(8,128)(2,1)S(1)}, bf16[384,192]{1,0:T(8,128)(2,1)}, u32[]{:S(2)}) copy-start(bf16[384,192]{1,0:T(8,128)(2,1)} %constant.158.clone.w_ref) | copy-start | bytes 442372
  38.0 13.1 %copy-start.4 = (bf16[384,192]{1,0:T(8,128)(2,1)S(1)}, bf16[384,192]{1,0:T(8,128)(2,1)}, u32[]{:S(2)}) copy-start(bf16[384,192]{1,0:T(8,128)(2,1)} %constant.159.clone.v_ref) | copy-start | bytes 442372
  39.6 11.5 %copy-start.1 = (f32[2,32,32,128]{3,2,1,0:T(8,128)S(1)}, f32[2,32,32,128]{3,2,1,0:T(8,128)}, u32[]{:S(2)}) copy-start(f32[2,32,32,128]{3,2,1,0:T(8,128)} %constant.164.clone.t_ref) | copy-start | bytes 3145732
  51.1 18.3 %copy-start.15 = (f32[32,32,128]{2,1,0:T(8,128)S(1)}, f32[32,32,128]{2,1,0:T(8,128)}, u32[]{:S(2)}) copy-start(f32[32,32,128]{2,1,0:T(8,128)} %copy-done.14) | copy-start | bytes 1572868
  53.5 15.9 %copy-start.9 = (f32[48,128]{1,0:T(8,128)S(1)}, f32[48,128]{1,0:T(8,128)}, u32[]{:S(2)}) copy-start(f32[48,128]{1,0:T(8,128)} %get-tuple-element.34.c_ref) | copy-start | bytes 73732
  53.5 15.9 %copy-start.12 = (bf16[768,256]{1,0:T(8,128)(2,1)S(1)}, bf16[768,256]{1,0:T(8,128)(2,1)}, u32[]{:S(2)}) copy-start(bf16[768,256]{1,0:T(8,128)(2,1)} %constant.160.clone.w_ref) | copy-start | bytes 1179652
  53.5 15.9 %copy-start.13 = (bf16[512,256]{1,0:T(8,128)(2,1)S(1)}, bf16[512,256]{1,0:T(8,128)(2,1)}, u32[]{:S(2)}) copy-start(bf16[512,256]{1,0:T(8,128)(2,1)} %constant.161.clone.v_ref) | copy-start | bytes 786436
  86.3 27.6 %copy-start.6 = (bf16[512,256]{1,0:T(8,128)(2,1)S(1)}, bf16[512,256]{1,0:T(8,128)(2,1)}, u32[]{:S(2)}) copy-start(bf16[512,256]{1,0:T(8,128)(2,1)} %constant.163.clone.w_ref) | copy-start | bytes 786436
  88.5 25.4 %copy-start.2 = (f32[8,16,8,256]{3,2,1,0:T(8,128)S(1)}, f32[8,16,8,256]{3,2,1,0:T(8,128)}, u32[]{:S(2)}) copy-start(f32[8,16,8,256]{3,2,1,0:T(8,128)} %copy.21) | copy-start | bytes 3145732

commit v7 on v6

--- a/solution.py
+++ b/solution.py
@@ -516,16 +516,14 @@
     lane = jnp.arange(LANES, dtype=jnp.int32)
     first = jnp.arange(FIRST, dtype=jnp.int32)
     own_targets = lax.dynamic_index_in_dim(targets, wave_index, 0, keepdims=False)
-    place_row = plane_index * SECOND + jnp.arange(ROWS, dtype=jnp.int32)
-    hit_a = own_targets[:, 1][None, :] // SECOND == first[:, None]
-    near, far = [], []
-    for half in range(2):
-        hit_row = own_targets[:, 0][None, :] == (place_row + half * ROWS)[:, None]
-        near.append((hit_a[:, None, :] & hit_row[None, :, :]).reshape(FIRST * ROWS, -1))
-        hit_col = (own_targets[:, 1] % SECOND)[:, None] == (lane % SECOND)[None, :]
-        far.append(hit_col & (lane // SECOND == half)[None, :])
-    near = jnp.concatenate(near, 1).astype(jnp.bfloat16)
-    far = jnp.concatenate(far, 0).astype(jnp.bfloat16)
+    near_row = own_targets[:, 0] - plane_index * SECOND
+    held = (near_row >= 0) & (near_row < SECOND)
+    code = jnp.where(held, own_targets[:, 1] // SECOND * SECOND + near_row, -1)
+    place = (first[:, None] * SECOND + jnp.arange(ROWS, dtype=jnp.int32)[None, :]).reshape(-1)
+    half = lane // SECOND
+    near = (place[:, None] + ROWS * half[None, :] == jnp.tile(code, 2)[None, :]).astype(jnp.bfloat16)
+    spot_lane = jnp.tile(own_targets[:, 1] % SECOND, 2) + SECOND * half
+    far = (spot_lane[:, None] == lane[None, :]).astype(jnp.bfloat16)
     spots = call(
         spots_kernel,
         jax.ShapeDtypeStruct((FIRST, ROWS, LANES), jnp.float32),

time: 124 us -> 124 us (level)
  no operation moved by 1% of the time
where the time goes in v7:
time: 124 us
  blocking collectives  64.8 us (52%)
  starting transfers between devices  20.1 us (16%)
  Pallas kernels  13.8 us (11%)
  waiting for transfers between devices  11.6 us (9%)
  matrix products  6.44 us (5%)
  other arithmetic  4.19 us (3%)
  local copies, waits for them, and re-layouts  2.57 us (2%)
    all_to_all x2, blocking collectives, exchange(): return lax.all_to_all(x, PLANE, 0, 0, tiled=True)  31 us
    all_to_all x1, blocking collectives, local(): lines = lax.all_to_all(cols, EVERY, 0, 0, tiled=True)  25.4 us
    all_to_all x1, starting transfers between devices, local(): cols = lax.all_to_all(sent, EVERY, 0, 0, tiled=True)  14.1 us
    pallas_call x7, Pallas kernels, call(): pl.pallas_call(kernel, out_shape=out_shape, out_specs=(where,) * len(outs...  13.8 us
    all_to_all x1, waiting for transfers between devices, local(): cols = lax.all_to_all(sent, EVERY, 0, 0, tiled=True)  9.17 us
    all_to_all x1, blocking collectives, local(): return lax.all_to_all(gradient, WAVE, 0, 0, tiled=True)  8.45 us
    dot_general x1, matrix products, slope_rows(): jnp.einsum('mich,hj->mjic', slope.astype(jnp.bfloat16), w_out, preferred_...  6.44 us
    all_to_all x1, starting transfers between devices, local(): lax.all_to_all(level_widths(levels, offsets), WAVE, 0, 0, tiled=True)  5.95 us
  transfers between devices with their start and end apart: 2, of which 2 were waited for; matrix products, arithmetic and copies ran while one was open for 9% of the time, Pallas kernels for 2%

profile of v7, /device:TPU:1, one launch (start us, length us, event | category | flops | bytes accessed | tf_op | source)
XLA Modules:
  0.0 123.7 jit_solution(11441398676364981209)
XLA Ops:
  0.0 1.5 %add_bitcast_fusion = f32[8,8,256]{2,1,0:T(8,128)} fusion(f32[64,256]{1,0:T(8,128)} %param.18, s32[64,256]{1,0:T(8,128)} %param.17), kind=kLoop, calls=%fused_computation.19 | loop fusion | flops 65536 | bytes 196608 | tf_op jit(solution)/shard_map/all_to_all | solution.py:490
  1.5 5.9 %all-to-all-start = ((f32[8,8,256]{2,1,0:T(8,128)}), f32[8,8,256]{2,1,0:T(8,128)S(1)}, u32[]{:S(2)}, u32[]{:S(2)}) async-start(f32[8,8,256]{2,1,0:T(8,128)} %add_bitcast_fusion), calls=%async_computation | async-start | bytes 131072 | tf_op jit(solution)/shard_map/all_to_all | solution.py:490
  7.5 1.8 %prepare.1 = (f32[2,256,128]{2,1,0:T(8,128)}, f32[2,16,128]{2,1,0:T(8,128)}, f32[48,128]{1,0:T(8,128)}) custom-call(f32[1,256]{1,0:T(1,128)} %bitcast.55, f32[1,256]{1,0:T(1,128)} %bitcast.56, f32[1,16]{1,0:T(1,128)} %bitcast.57, bf16[16,256]{1,0:T(8,128)(2,1)} %bitcast.52, f32[2,128]{1,0:T(2,128)} %constant.152.clone.u_ref, f32[2,8,128]{2,1,0:T(8,128)} %constant.153.clone.dc_ref), custom_call_target="tpu_custom_call" | custom-call | flops 20000000000 | tf_op jit(solution)/shard_map/prepare/pallas_call | solution.py:422
  9.3 0.1 eq.27
  9.4 0.1 iota_add_fusion
  9.5 0.1 add.169
  9.6 0.1 tile.8
  9.7 0.1 fusion.9.far_ref
  9.8 0.2 fusion.8.near_ref
  10.0 0.0 copy-start.5
  10.0 0.0 copy-start.8
  10.0 0.0 copy-start.11
  10.0 0.2 spots.1.s_ref
  10.3 2.4 %all-to-all-done.x_ref = f32[8,8,256]{2,1,0:T(8,128)S(1)} async-done(((f32[8,8,256]{2,1,0:T(8,128)}), f32[8,8,256]{2,1,0:T(8,128)S(1)}, u32[]{:S(2)}, u32[]{:S(2)}) %all-to-all-start) | async-done | bytes 65568 | tf_op jit(solution)/shard_map/all_to_all | solution.py:490
  12.7 0.0 copy-start.17
  12.7 4.7 %first.1 = bf16[2048,128]{1,0:T(8,128)(2,1)} custom-call(f32[8,8,256]{2,1,0:T(8,128)S(1)} %all-to-all-done.x_ref, f32[2,256,128]{2,1,0:T(8,128)S(1)} %copy-done.7, f32[2,16,128]{2,1,0:T(8,128)S(1)} %copy-done.10, bf16[16,256]{1,0:T(8,128)(2,1)S(1)} %bitcast.53, f32[48,2,128]{2,1,0:T(2,128)S(1)} %copy-done.8, bf16[768,256]{1,0:T(8,128)(2,1)S(1)} %copy-done.5), custom_call_target="tpu_custom_call" | custom-call | flops 100000000 | bytes 1318912 | tf_op jit(solution)/shard_map/first/pallas_call | solution.py:422
  17.5 14.1 %all-to-all-start.1 = ((bf16[256,8,128]{2,1,0:T(8,128)(2,1)}), bf16[256,8,128]{2,1,0:T(8,128)(2,1)S(1)}, u32[]{:S(2)}, u32[]{:S(2)}) async-start(bf16[256,8,128]{2,1,0:T(8,128)(2,1)} %bitcast.8), calls=%async_computation.1 | async-start | bytes 1048576 | tf_op jit(solution)/shard_map/all_to_all | solution.py:555
  31.6 6.4 %fusion.1 = f32[8,16,8,256]{3,1,2,0:T(8,128)S(1)} fusion(f32[256]{0:T(256)S(1)} %copy-done.17, f32[256]{0:T(256)S(1)} %copy-done.16, f32[8,8,256]{2,1,0:T(8,128)S(1)} %all-to-all-done.x_ref, bf16[256,16]{0,1:T(8,128)(2,1)S(1)} %copy-done.11), kind=kOutput, calls=%fused_computation.3 | convolution fusion | flops 180355072 | bytes 1124352 | tf_op jit(solution)/shard_map/mich,hj->mjic/dot_general | solution.py:441
  38.0 1.6 %copy.21 = f32[8,16,8,256]{3,2,1,0:T(8,128)} copy(f32[8,16,8,256]{3,1,2,0:T(8,128)S(1)} %fusion.1) | data formatting | bytes 2097152 | tf_op jit(solution)/shard_map/mich,hj->mjic/transpose | solution.py:441
  39.7 2.2 %sine_multiply_fusion = (f32[32,32,128]{2,1,0:T(8,128)S(1)}, f32[32,32,128]{2,1,0:T(8,128)S(1)}) fusion(f32[128]{0:T(128)S(1)} %fusion.15, s32[32,128]{1,0:T(8,128)S(1)} %add_multiply_fusion, f32[]{:T(128)S(6)} %mul.147), kind=kLoop, calls=%fused_computation.10 | loop fusion | flops 2228224 | bytes 1065476 | tf_op jit(solution)/shard_map/mul | solution.py:456
  42.0 9.2 %all-to-all-done.1 = bf16[256,8,128]{2,1,0:T(8,128)(2,1)S(1)} async-done(((bf16[256,8,128]{2,1,0:T(8,128)(2,1)}), bf16[256,8,128]{2,1,0:T(8,128)(2,1)S(1)}, u32[]{:S(2)}, u32[]{:S(2)}) %all-to-all-start.1) | async-done | bytes 524320 | tf_op jit(solution)/shard_map/all_to_all | solution.py:555
  51.1 2.3 %filter.1 = bf16[32,64,128]{2,1,0:T(8,128)(2,1)S(1)} custom-call(bf16[32,64,128]{2,1,0:T(8,128)(2,1)S(1)} %bitcast.48, f32[32,32,128]{2,1,0:T(8,128)S(1)} %get-tuple-element.32.kr_ref, f32[32,32,128]{2,1,0:T(8,128)S(1)} %get-tuple-element.33.ki_ref, f32[2,32,32,128]{3,2,1,0:T(8,128)S(1)} %copy-done.1, bf16[384,192]{1,0:T(8,128)(2,1)S(1)} %copy-done.3, ...), custom_call_target="tpu_custom_call" | custom-call | flops 100000000 | bytes 3440640 | tf_op jit(solution)/shard_map/filter/pallas_call | solution.py:422
  53.5 0.0 copy-start.12
  53.5 0.0 copy-start.13
  53.5 15.9 %all_to_all.54.x_ref = bf16[32,64,128]{2,1,0:T(8,128)(2,1)S(1)} all-to-all(bf16[32,64,128]{2,1,0:T(8,128)(2,1)S(1)} %filter.1), channel_id=1, replica_groups=mesh['xl'=2,'y'=4,'xh'=2,'z'=8,'c'=2] {'xh','c','xl','y'}, dimensions={0} | all-to-all | bytes 1048576 | tf_op jit(solution)/shard_map/all_to_all | solution.py:585
  69.4 1.8 %middle.1 = bf16[32,64,128]{2,1,0:T(8,128)(2,1)S(1)} custom-call(bf16[32,64,128]{2,1,0:T(8,128)(2,1)S(1)} %all_to_all.54.x_ref, f32[48,128]{1,0:T(8,128)S(1)} %copy-done.9, f32[32,32,128]{2,1,0:T(8,128)S(1)} %copy-done.15, f32[48,2,128]{2,1,0:T(2,128)S(1)} %copy-done.8, bf16[768,256]{1,0:T(8,128)(2,1)S(1)} %copy-done.12, bf16[512,256]{1,0:T(8,128)(2,1)S(1)} %copy-done.13), custom_call_target="tpu_custom_call" | custom-call | flops 6000000000 | bytes 2301952 | tf_op jit(solution)/shard_map/middle/pallas_call | solution.py:422
  71.2 15.1 %all_to_all.55.x_ref = bf16[32,64,128]{2,1,0:T(8,128)(2,1)S(1)} all-to-all(bf16[32,64,128]{2,1,0:T(8,128)(2,1)S(1)} %middle.1), channel_id=1, replica_groups=mesh['xl'=2,'y'=4,'xh'=2,'z'=8,'c'=2] {'xh','c','xl','y'}, dimensions={0} | all-to-all | bytes 1048576 | tf_op jit(solution)/shard_map/all_to_all | solution.py:585
  86.3 2.2 %filter_back.1 = bf16[32,64,128]{2,1,0:T(8,128)(2,1)S(1)} custom-call(bf16[32,64,128]{2,1,0:T(8,128)(2,1)S(1)} %all_to_all.55.x_ref, f32[32,32,128]{2,1,0:T(8,128)S(1)} %get-tuple-element.32.kr_ref, f32[32,32,128]{2,1,0:T(8,128)S(1)} %get-tuple-element.33.ki_ref, f32[2,32,32,128]{3,2,1,0:T(8,128)S(1)} %copy-done.1, bf16[384,192]{1,0:T(8,128)(2,1)S(1)} %copy-done.3, ...), custom_call_target="tpu_custom_call" | custom-call | flops 100000000 | bytes 3440640 | tf_op jit(solution)/shard_map/filter_back/pallas_call | solution.py:422
  88.5 25.4 %all_to_all.56 = bf16[256,8,128]{2,1,0:T(8,128)(2,1)S(1)} all-to-all(bf16[256,8,128]{2,1,0:T(8,128)(2,1)S(1)} %bitcast.49), channel_id=1, replica_groups=mesh['xl'=2,'y'=4,'xh'=2,'z'=8,'c'=2] {'xh','z','c','xl','y'}, dimensions={0} | all-to-all | bytes 1048576 | tf_op jit(solution)/shard_map/all_to_all | solution.py:603
  113.9 0.7 last.1
  114.7 8.4 %all_to_all.57 = f32[8,8,256]{2,1,0:T(8,128)S(1)} all-to-all(f32[8,8,256]{2,1,0:T(8,128)S(1)} %bitcast.51), channel_id=1, replica_groups=mesh['xl'=2,'y'=4,'xh'=2,'z'=8,'c'=2] {'xl','y'}, dimensions={0} | all-to-all | bytes 131072 | tf_op jit(solution)/shard_map/all_to_all | solution.py:616
  123.1 0.6 copy.23
  (39 shorter events, 0.1 us)
Async XLA Ops:
  0.0 9.3 %copy-start = (s32[8,64,2]{1,2,0:T(2,128)S(1)}, s32[8,64,2]{1,2,0:T(2,128)}, u32[]{:S(2)}) copy-start(s32[8,64,2]{1,2,0:T(2,128)} %param.19) | copy-start | bytes 12292
  1.5 11.1 %all-to-all-start = ((f32[8,8,256]{2,1,0:T(8,128)}), f32[8,8,256]{2,1,0:T(8,128)S(1)}, u32[]{:S(2)}, u32[]{:S(2)}) async-start(f32[8,8,256]{2,1,0:T(8,128)} %add_bitcast_fusion), calls=%async_computation | async-start | bytes 131072 | tf_op jit(solution)/shard_map/all_to_all | solution.py:490
  10.0 2.7 %copy-start.5 = (bf16[768,256]{1,0:T(8,128)(2,1)S(1)}, bf16[768,256]{1,0:T(8,128)(2,1)}, u32[]{:S(2)}) copy-start(bf16[768,256]{1,0:T(8,128)(2,1)} %constant.148.clone.w_ref) | copy-start | bytes 1179652
  10.0 2.7 %copy-start.7 = (f32[2,256,128]{2,1,0:T(8,128)S(1)}, f32[2,256,128]{2,1,0:T(8,128)}, u32[]{:S(2)}) copy-start(f32[2,256,128]{2,1,0:T(8,128)} %get-tuple-element.24.s_ref) | copy-start | bytes 786436
  10.0 2.7 %copy-start.8 = (f32[48,2,128]{2,1,0:T(2,128)S(1)}, f32[48,2,128]{2,1,0:T(2,128)}, u32[]{:S(2)}) copy-start(f32[48,2,128]{2,1,0:T(2,128)} %constant.151.clone.t_ref) | copy-start | bytes 147460
  10.0 2.7 %copy-start.10 = (f32[2,16,128]{2,1,0:T(8,128)S(1)}, f32[2,16,128]{2,1,0:T(8,128)}, u32[]{:S(2)}) copy-start(f32[2,16,128]{2,1,0:T(8,128)} %get-tuple-element.25.m_ref) | copy-start | bytes 49156
  10.0 2.7 %copy-start.11 = (bf16[256,16]{0,1:T(8,128)(2,1)S(1)}, bf16[256,16]{0,1:T(8,128)(2,1)}, u32[]{:S(2)}) copy-start(bf16[256,16]{0,1:T(8,128)(2,1)} %param.22) | copy-start | bytes 24580
  10.3 7.2 %copy-start.14 = (f32[32,32,128]{2,1,0:T(8,128)}, f32[32,32,128]{2,1,0:T(8,128)S(1)}, u32[]{:S(2)}) copy-start(f32[32,32,128]{2,1,0:T(8,128)S(1)} %spots.1.s_ref) | copy-start | bytes 1572868
  12.7 18.9 %copy-start.16 = (f32[256]{0:T(256)S(1)}, f32[256]{0:T(256)}, u32[]{:S(2)}) copy-start(f32[256]{0:T(256)} %param.20) | copy-start | bytes 3076
  12.7 18.9 %copy-start.17 = (f32[256]{0:T(256)S(1)}, f32[256]{0:T(256)}, u32[]{:S(2)}) copy-start(f32[256]{0:T(256)} %param.21) | copy-start | bytes 3076
  17.5 33.7 %all-to-all-start.1 = ((bf16[256,8,128]{2,1,0:T(8,128)(2,1)}), bf16[256,8,128]{2,1,0:T(8,128)(2,1)S(1)}, u32[]{:S(2)}, u32[]{:S(2)}) async-start(bf16[256,8,128]{2,1,0:T(8,128)(2,1)} %bitcast.8), calls=%async_computation.1 | async-start | bytes 1048576 | tf_op jit(solution)/shard_map/all_to_all | solution.py:555
  38.0 13.1 %copy-start.3 = (bf16[384,192]{1,0:T(8,128)(2,1)S(1)}, bf16[384,192]{1,0:T(8,128)(2,1)}, u32[]{:S(2)}) copy-start(bf16[384,192]{1,0:T(8,128)(2,1)} %constant.144.clone.w_ref) | copy-start | bytes 442372
  38.0 13.1 %copy-start.4 = (bf16[384,192]{1,0:T(8,128)(2,1)S(1)}, bf16[384,192]{1,0:T(8,128)(2,1)}, u32[]{:S(2)}) copy-start(bf16[384,192]{1,0:T(8,128)(2,1)} %constant.145.clone.v_ref) | copy-start | bytes 442372
  39.6 11.5 %copy-start.1 = (f32[2,32,32,128]{3,2,1,0:T(8,128)S(1)}, f32[2,32,32,128]{3,2,1,0:T(8,128)}, u32[]{:S(2)}) copy-start(f32[2,32,32,128]{3,2,1,0:T(8,128)} %constant.150.clone.t_ref) | copy-start | bytes 3145732
  51.1 18.3 %copy-start.15 = (f32[32,32,128]{2,1,0:T(8,128)S(1)}, f32[32,32,128]{2,1,0:T(8,128)}, u32[]{:S(2)}) copy-start(f32[32,32,128]{2,1,0:T(8,128)} %copy-done.14) | copy-start | bytes 1572868
  53.5 15.9 %copy-start.9 = (f32[48,128]{1,0:T(8,128)S(1)}, f32[48,128]{1,0:T(8,128)}, u32[]{:S(2)}) copy-start(f32[48,128]{1,0:T(8,128)} %get-tuple-element.34.c_ref) | copy-start | bytes 73732
  53.5 15.9 %copy-start.12 = (bf16[768,256]{1,0:T(8,128)(2,1)S(1)}, bf16[768,256]{1,0:T(8,128)(2,1)}, u32[]{:S(2)}) copy-start(bf16[768,256]{1,0:T(8,128)(2,1)} %constant.146.clone.w_ref) | copy-start | bytes 1179652
  53.5 15.9 %copy-start.13 = (bf16[512,256]{1,0:T(8,128)(2,1)S(1)}, bf16[512,256]{1,0:T(8,128)(2,1)}, u32[]{:S(2)}) copy-start(bf16[512,256]{1,0:T(8,128)(2,1)} %constant.147.clone.v_ref) | copy-start | bytes 786436
  86.3 27.6 %copy-start.6 = (bf16[512,256]{1,0:T(8,128)(2,1)S(1)}, bf16[512,256]{1,0:T(8,128)(2,1)}, u32[]{:S(2)}) copy-start(bf16[512,256]{1,0:T(8,128)(2,1)} %constant.149.clone.w_ref) | copy-start | bytes 786436
  88.5 25.4 %copy-start.2 = (f32[8,16,8,256]{3,2,1,0:T(8,128)S(1)}, f32[8,16,8,256]{3,2,1,0:T(8,128)}, u32[]{:S(2)}) copy-start(f32[8,16,8,256]{3,2,1,0:T(8,128)} %copy.21) | copy-start | bytes 3145732
